TPU v7x, 32 devices: a whole 2x2x4 slice. The times are simulated.
32 devices in a mesh: section: 2 (over core), tp: 16 (over z, y, x).
Axes of the slice: x: 2, y: 2, z: 4, core: 2. Of those that a mesh axis runs over, the one named last changes fastest.
Arguments:
- start_tokens: bfloat16 [2, 32, 8192], P(None, None, 'tp'), may hold values from -6 to 6
- target_weight: bfloat16 [2, 8192, 8192], P('section', None, 'tp'), may hold values from -0.0625 to 0.0625
- online_weight: bfloat16 [2, 8192, 8192], P('section', 'tp'), may hold values from -0.0625 to 0.0625
- head_weight: bfloat16 [8192, 256], P('tp'), may hold values from -0.0625 to 0.0625
- reward: float32 [2, 32], P(None, 'section'), may hold values from -6 to 6
- action_bin: int32 [2, 32], P(None, 'section'), may hold values from 0 to 255
Outputs:
- target_value: float32 [2, 32], P(None, 'section')
- q_taken: float32 [2, 32], P(None, 'section')
All inputs are finite; a program needn't handle non-finite values.
Results may differ from a plain program's by a relative error of at most 0.018.
Values may be sent and summed in bfloat16 or wider, within the bound.
No kernel may reach another device: no remote copies, remote signals or barrier semaphores. Data moves between devices by JAX's collectives and lax.ppermute only.
A program may use at most 128 MiB of HBM per device.

v0:
```python
import functools

import jax
import jax.numpy as jnp
from jax import lax
from jax.experimental import pallas as pl
from jax.experimental.pallas import tpu as pltpu
from jax.sharding import PartitionSpec as P


def digits_of(size, most):
    radices = []
    left = size
    while left > 1:
        radix = next((r for r in range(min(most, left), 1, -1) if left % r == 0), None)
        if radix is None:
            radix = next(r for r in range(2, left + 1) if left % r == 0)
        radices.insert(0, radix)
        left //= radix
    strides = []
    stride = size
    for radix in radices:
        stride //= radix
        strides.append(stride)
    return list(zip(radices, strides))


def peer(digit, step, radix):
    if radix & (radix - 1) == 0:
        return digit ^ step
    return (digit + step) % radix


def exchange(value, axes, tp, routes, radix, stride, step):
    pairs = []
    for start, end in routes:
        for t in range(tp):
            digit = t // stride % radix
            other = t + (peer(digit, step, radix) - digit) * stride
            pairs.append((start * tp + t, end * tp + other))
    return lax.ppermute(value, axes, pairs)


def block_of(steps, digits, names):
    index = 0
    for step, (radix, stride), name in zip(steps, digits, names):
        index = index + peer(lax.axis_index(name), step, radix) * stride
    return index


def gather_steps(radix, last):
    return [*range(radix)] if last else [*range(radix - 1, -1, -1)]


def scatter_steps(radix, last):
    half = radix // 2 if last else 0
    return [*range(radix - 1, half - 1, -1), *range(half)]


def relative(digits, steps_of):
    found = [()]
    for number, (radix, _) in enumerate(digits):
        found = [one + (step,) for step in steps_of(radix, number == len(digits) - 1) for one in found]
    return found


def spread_kernel(x, weight, *outs, first, layer, digits, names):
    share, _, width = outs[0].shape

    @pl.when(lax.axis_index("section") == layer)
    def _():
        for j, steps in enumerate(relative(digits, scatter_steps)[first : first + share * len(outs)]):
            start = pl.multiple_of(block_of(steps, digits, names) * width, width)
            part = jnp.dot(x[...], weight[0, :, pl.ds(start, width)], preferred_element_type=jnp.float32)
            outs[j // share][j % share] = part.astype(outs[0].dtype)


def first_spread_kernel(x, weight, *rest, outputs, layer, digits, names):
    outs, (here, held, total, x_arrived, arrived) = rest[:outputs], rest[outputs:]
    share, _, width = outs[0].shape
    chunks, pieces = arrived.shape
    depth = weight.shape[1] // chunks
    rows = depth // pieces

    @pl.when(lax.axis_index("section") == layer)
    def _():
        x_copy = pltpu.make_async_copy(x, here, x_arrived)
        x_copy.start()
        copies = []
        for chunk in range(chunks):
            for piece in range(pieces):
                these = pl.ds(chunk * depth + piece * rows, rows)
                copies.append(
                    pltpu.make_async_copy(weight.at[0, these, :], held.at[these, :], arrived.at[chunk, piece])
                )
                copies[-1].start()
        x_copy.wait()
        for chunk in range(chunks):
            for piece in range(pieces):
                copies[chunk * pieces + piece].wait()
            those = slice(chunk * depth, (chunk + 1) * depth)
            for j, steps in enumerate(relative(digits, scatter_steps)):
                start = pl.multiple_of(block_of(steps, digits, names) * width, width)
                part = jnp.dot(here[:, those], held[those, pl.ds(start, width)], preferred_element_type=jnp.float32)
                if chunk > 0:
                    part = part + total[j]
                if chunk < chunks - 1:
                    total[j] = part
                else:
                    outs[j // share][j % share] = part.astype(outs[0].dtype)


def spread(x, weight, first, groups, layer, digits, names):
    rows, depth = x.shape
    count = len(relative(digits, scatter_steps))
    share = count // digits[-1][0]
    width = weight.shape[2] // count
    vmem = pl.BlockSpec(memory_space=pltpu.VMEM)
    outs = [jax.ShapeDtypeStruct((share, rows, width), jnp.bfloat16)] * groups
    if layer > 0:
        return pl.pallas_call(
            functools.partial(spread_kernel, first=first * share, layer=layer, digits=digits, names=names),
            out_shape=outs,
            in_specs=[vmem, vmem],
            out_specs=[vmem] * groups,
            compiler_params=pltpu.CompilerParams(vmem_limit_bytes=8 * 2**20),
            name="spread",
        )(x, pltpu.with_memory_space_constraint(weight, pltpu.VMEM))
    chunks = 2 if depth % 256 == 0 else 1
    return pl.pallas_call(
        functools.partial(first_spread_kernel, outputs=groups, layer=layer, digits=digits, names=names),
        out_shape=outs,
        in_specs=[pl.BlockSpec(memory_space=pltpu.HBM)] * 2,
        out_specs=[vmem] * groups,
        scratch_shapes=[
            pltpu.VMEM(x.shape, x.dtype),
            pltpu.VMEM(weight.shape[1:], weight.dtype),
            pltpu.VMEM((count, rows, width), jnp.float32),
            pltpu.SemaphoreType.DMA,
            pltpu.SemaphoreType.DMA((chunks, 4)),
        ],
        compiler_params=pltpu.CompilerParams(vmem_limit_bytes=20 * 2**20),
        name="first_spread",
    )(
        pltpu.with_memory_space_constraint(x, pltpu.HBM),
        pltpu.with_memory_space_constraint(weight, pltpu.HBM),
    )


def meet_kernel(weight, *rest, first, blocks, layer, digits, names):
    inputs, before, (total, square) = rest[:blocks], rest[blocks:-2], rest[-2:]
    share, _, depth = inputs[0].shape
    inside = lax.axis_index("section") == layer

    @pl.when(inside)
    def _():
        sum_of = before[0][...] if before else jnp.zeros(total.shape, jnp.float32)
        squares = before[1][...] if before else jnp.zeros(square.shape, jnp.float32)
        for j, steps in enumerate(relative(digits, gather_steps)[first : first + share * blocks]):
            x = inputs[j // share][j % share]
            wide = x.astype(jnp.float32)
            squares = squares + jnp.sum(wide * wide, axis=1, keepdims=True)
            start = pl.multiple_of(block_of(steps, digits, names) * depth, depth)
            sum_of = sum_of + jnp.dot(x, weight[0, pl.ds(start, depth), :], preferred_element_type=jnp.float32)
        total[...] = sum_of
        square[...] = squares

    @pl.when(jnp.logical_not(inside))
    def _():
        total[...] = jnp.zeros_like(total)
        square[...] = jnp.full_like(square, -1.0)


def meet(weight, groups, first, before, layer, digits, names):
    rows = groups[0].shape[1]
    vmem = pl.BlockSpec(memory_space=pltpu.VMEM)
    return pl.pallas_call(
        functools.partial(
            meet_kernel, first=first, blocks=len(groups), layer=layer, digits=digits, names=names
        ),
        out_shape=[
            jax.ShapeDtypeStruct((rows, weight.shape[2]), jnp.float32),
            jax.ShapeDtypeStruct((rows, 1), jnp.float32),
        ],
        in_specs=[vmem] * (1 + len(groups) + len(before)),
        out_specs=[vmem, vmem],
        compiler_params=pltpu.CompilerParams(vmem_limit_bytes=8 * 2**20),
        name="meet",
    )(pltpu.with_memory_space_constraint(weight, pltpu.VMEM), *groups, *before)


def tell_kernel(hidden, head, *outs, micro):
    values = jnp.dot(hidden[...], head[...], preferred_element_type=jnp.float32)
    tokens = values.shape[0] // micro
    share = tokens // len(outs)
    for section, out in enumerate(outs):
        starts = [m * tokens + section * share for m in range(micro)]
        out[...] = jnp.concatenate([values[start : start + share] for start in starts], axis=0)


def tell(hidden, head, micro, sections):
    shape = (hidden.shape[0] // sections, head.shape[1])
    vmem = pl.BlockSpec(memory_space=pltpu.VMEM)
    return pl.pallas_call(
        functools.partial(tell_kernel, micro=micro),
        out_shape=[jax.ShapeDtypeStruct(shape, jnp.float32)] * sections,
        in_specs=[vmem, vmem],
        out_specs=[vmem] * sections,
        compiler_params=pltpu.CompilerParams(vmem_limit_bytes=8 * 2**20),
        name="tell",
    )(hidden, head)


def paired_sum(terms):
    while len(terms) > 1:
        terms = [a + b for a, b in zip(terms[::2], terms[1::2])] + terms[len(terms) // 2 * 2 :]
    return terms[0]


def per_device(start_tokens, target_weight, online_weight, head_weight, reward, action_bin, sections, digits, names):
    micro, tokens, width = start_tokens.shape
    tp = 1
    for radix, _ in digits:
        tp *= radix
    everyone = ("section",) + names
    rows = micro * tokens
    features = width * tp
    rounds = len(digits)
    send = functools.partial(exchange, axes=everyone, tp=tp)
    own = start_tokens.reshape(rows, width)
    inner = digits[-1][0]
    half = inner // 2
    for layer in range(sections):
        place = dict(layer=layer, digits=digits, names=names)
        helper = layer - 1 if layer > 0 else min(1, sections - 1)
        both = [(layer, helper), (helper, layer)] if helper != layer else [(layer, layer)]
        if layer > 0:
            own = own + send(own, routes=both, radix=1, stride=1, step=0)

        if layer == 0:
            parts = list(spread(own, online_weight, 0, inner, **place))
        else:
            parts = list(spread(own, online_weight, 0, half, **place)) if half else []
            parts += spread(own, online_weight, half, inner - half, **place)
        stack = own[None]
        for number, (radix, stride) in enumerate(digits):
            final = number == rounds - 1
            routes = both
            if final:
                routes = [(helper, layer)]
                at = layer if number % 2 == 0 else helper
                sent = []
                for step, one in zip(scatter_steps(radix, True), parts):
                    if step > 0 or at != layer:
                        one = send(one, routes=[(layer, at)], radix=radix, stride=stride, step=step)
                    sent.append(one)
                if layer == 0 and rounds > 1:
                    stack, sent[:1] = lax.optimization_barrier((stack, sent[:1]))
            gathered = [
                stack if step == 0 else send(stack, routes=routes, radix=radix, stride=stride, step=step)
                for step in gather_steps(radix, final)
            ]
            if not final:
                gathered, parts[half:] = lax.optimization_barrier((gathered, parts[half:]))
                stack = jnp.concatenate(gathered, axis=0)
        wide = functools.reduce(jnp.add, [one.astype(jnp.float32) for one in sent])
        for number in range(rounds - 2, -1, -1):
            radix, stride = digits[number]
            to = layer if at != layer or number % 2 == 0 else helper
            part = wide.shape[0] // radix
            sent = []
            for i, step in enumerate(scatter_steps(radix, False)):
                one = wide[i * part : (i + 1) * part].astype(jnp.bfloat16)
                if step > 0 or to != at:
                    one = send(one, routes=[(at, to)], radix=radix, stride=stride, step=step)
                sent.append(one)
            at = to
            wide = functools.reduce(jnp.add, [one.astype(jnp.float32) for one in sent])

        before = []
        for begin in range(0, len(gathered), max(1, half)):
            groups = gathered[begin : begin + max(1, half)]
            before = meet(target_weight, groups, begin * groups[0].shape[0], before, **place)
        total, square = before
        update = lax.rsqrt(square / features + 1e-06) * (0.25 * wide[0] + 0.75 * total)
        own = jnp.where(square >= 0.0, own.astype(jnp.float32) + update, 0.0).astype(jnp.bfloat16)

    share_rows = reward.shape[1]
    end = sections - 1
    values = tell(own, head_weight, micro, sections)
    mine = values[end]
    for other in range(end):
        mine = mine + send(values[other], routes=[(end, other), (other, end)], radix=1, stride=1, step=0)
    everywhere = [(section, section) for section in range(sections)]
    for radix, stride in digits[::-1]:
        told = mine.astype(jnp.bfloat16)
        far = [send(told, routes=everywhere, radix=radix, stride=stride, step=step) for step in range(radix - 1, 0, -1)]
        mine = paired_sum([term.astype(jnp.float32) for term in [*far, told]])
    mine = mine.reshape(micro, share_rows, head_weight.shape[1])
    best = jnp.max(mine, axis=2)
    bin_ids = lax.broadcasted_iota(jnp.int32, mine.shape, 2)
    taken = jnp.sum(jnp.where(bin_ids == action_bin[:, :, None], mine, 0.0), axis=2)
    return (reward + 0.98 * best, taken)


def solution(mesh):
    sections, tp = mesh.shape["section"], mesh.shape["tp"]
    digits = digits_of(tp, 4)
    names = tuple(f"tp{number}" for number in range(len(digits)))
    cut = jax.sharding.Mesh(
        mesh.devices.reshape([sections] + [radix for radix, _ in digits]), ("section",) + names
    )
    in_specs = (
        P(None, None, names),
        P("section", None, names),
        P("section", names, None),
        P(names, None),
        P(None, "section"),
        P(None, "section"),
    )
    out_specs = (P(None, "section"), P(None, "section"))
    body = functools.partial(per_device, sections=sections, digits=digits, names=names)
    return jax.shard_map(body, mesh=cut, in_specs=in_specs, out_specs=out_specs, check_vma=False)
```

profile of v0, /device:TPU:0, one launch (start us, length us, event | category | flops | bytes accessed | tf_op | source)
XLA Modules:
  0.0 78.0 jit_solution(15755304333523400783)
XLA Ops:
  0.6 4.6 %collective-permute-start = (bf16[1,64,512]{2,1,0:T(8,128)(2,1)}, bf16[1,64,512]{2,1,0:T(8,128)(2,1)S(1)}, u32[]{:S(2)}, u32[]{:S(2)}) collective-permute-start(bf16[1,64,512]{2,1,0:T(8,128)(2,1)} %bitcast.30), channel_id=1, source_target_pairs={{0,28},{1,29},{2,30},{3,31},{4,24},{5,25},{6,26},{7,27},{8,20},{9,... | collective-permute-start | bytes 196616 | tf_op jit(solution)/shard_map/ppermute | solution.py:41
  6.1 4.7 %first_spread.1 = (bf16[4,64,512]{2,1,0:T(8,128)(2,1)S(1)}, bf16[4,64,512]{2,1,0:T(8,128)(2,1)S(1)}, bf16[4,64,512]{2,1,0:T(8,128)(2,1)S(1)}, bf16[4,64,512]{2,1,0:T(8,128)(2,1)S(1)}) custom-call(bf16[64,512]{1,0:T(8,128)(2,1)} %bitcast.33, bf16[1,512,8192]{2,1,0:T(8,128)(2,1)} %weight.13), custom_call_target="tpu_custom_call" | custom-call | tf_op jit(solution)/shard_map/first_spread/pallas_call | solution.py:130
  10.8 1.3 %collective-permute-start.3 = (bf16[4,64,512]{2,1,0:T(8,128)(2,1)S(1)}, bf16[4,64,512]{2,1,0:T(8,128)(2,1)S(1)}, u32[]{:S(2)}, u32[]{:S(2)}) collective-permute-start(bf16[4,64,512]{2,1,0:T(8,128)(2,1)S(1)} %get-tuple-element.40), channel_id=1, source_target_pairs={{0,19},{1,18},{2,17},{3,16},{4,23},{5,22},{6,21},{7,20},{8,27},{9,... | collective-permute-start | bytes 786440 | tf_op jit(solution)/shard_map/ppermute | solution.py:41
  12.1 1.3 %collective-permute-start.7 = (bf16[4,64,512]{2,1,0:T(8,128)(2,1)S(1)}, bf16[4,64,512]{2,1,0:T(8,128)(2,1)S(1)}, u32[]{:S(2)}, u32[]{:S(2)}) collective-permute-start(bf16[4,64,512]{2,1,0:T(8,128)(2,1)S(1)} %get-tuple-element.46), channel_id=1, source_target_pairs={{0,18},{1,19},{2,16},{3,17},{4,22},{5,23},{6,20},{7,21},{8,26},{9,... | collective-permute-start | bytes 786440 | tf_op jit(solution)/shard_map/ppermute | solution.py:41
  13.5 1.3 %collective-permute-start.8 = (bf16[4,64,512]{2,1,0:T(8,128)(2,1)S(1)}, bf16[4,64,512]{2,1,0:T(8,128)(2,1)S(1)}, u32[]{:S(2)}, u32[]{:S(2)}) collective-permute-start(bf16[4,64,512]{2,1,0:T(8,128)(2,1)S(1)} %get-tuple-element.47), channel_id=1, source_target_pairs={{0,16},{1,17},{2,18},{3,19},{4,20},{5,21},{6,22},{7,23},{8,24},{9,... | collective-permute-start | bytes 786440 | tf_op jit(solution)/shard_map/ppermute | solution.py:41
  14.8 1.5 %collective-permute-start.9 = (bf16[4,64,512]{2,1,0:T(8,128)(2,1)S(1)}, bf16[4,64,512]{2,1,0:T(8,128)(2,1)S(1)}, u32[]{:S(2)}, u32[]{:S(2)}) collective-permute-start(bf16[4,64,512]{2,1,0:T(8,128)(2,1)S(1)} %get-tuple-element.48), channel_id=1, source_target_pairs={{0,17},{1,16},{2,19},{3,18},{4,21},{5,20},{6,23},{7,22},{8,25},{9,... | collective-permute-start | bytes 786440 | tf_op jit(solution)/shard_map/ppermute | solution.py:41
  16.4 1.3 %collective-permute-start.6 = (bf16[4,64,512]{2,1,0:T(8,128)(2,1)S(1)}, bf16[4,64,512]{2,1,0:T(8,128)(2,1)S(1)}, u32[]{:S(2)}, u32[]{:S(2)}) collective-permute-start(bf16[4,64,512]{2,1,0:T(8,128)(2,1)S(1)} %pad_maximum_fusion.rest_0_), channel_id=1, source_target_pairs={{16,1},{17,0},{18,3},{19,2},{20,5},{21,4},{22,7},{23,6},{24,9},{25... | collective-permute-start | bytes 786440 | tf_op jit(solution)/shard_map/ppermute | solution.py:41
  17.7 1.3 %collective-permute-start.4 = (bf16[4,64,512]{2,1,0:T(8,128)(2,1)S(1)}, bf16[4,64,512]{2,1,0:T(8,128)(2,1)S(1)}, u32[]{:S(2)}, u32[]{:S(2)}) collective-permute-start(bf16[4,64,512]{2,1,0:T(8,128)(2,1)S(1)} %pad_maximum_fusion.rest_0_), channel_id=1, source_target_pairs={{16,2},{17,3},{18,0},{19,1},{20,6},{21,7},{22,4},{23,5},{24,10},{2... | collective-permute-start | bytes 786440 | tf_op jit(solution)/shard_map/ppermute | solution.py:41
  24.7 1.5 %collective-permute-start.12 = (bf16[1,64,512]{2,1,0:T(8,128)(2,1)S(1)}, bf16[1,64,512]{2,1,0:T(8,128)(2,1)S(1)}, u32[]{:S(2)}, u32[]{:S(2)}) collective-permute-start(bf16[1,64,512]{2,1,0:T(8,128)(2,1)S(1)} %get-tuple-element.74), channel_id=1, source_target_pairs={{16,4},{17,5},{18,6},{19,7},{20,0},{21,1},{22,2},{23,3},{24,12},{2... | collective-permute-start | bytes 196616 | tf_op jit(solution)/shard_map/ppermute | solution.py:41
  27.2 1.8 %collective-permute-done.4.rest_0_ = bf16[4,64,512]{2,1,0:T(8,128)(2,1)S(1)} collective-permute-done((bf16[4,64,512]{2,1,0:T(8,128)(2,1)S(1)}, bf16[4,64,512]{2,1,0:T(8,128)(2,1)S(1)}, u32[]{:S(2)}, u32[]{:S(2)}) %collective-permute-start.4) | collective-permute-done | bytes 262176 | tf_op jit(solution)/shard_map/ppermute | solution.py:41
  33.5 3.0 %collective-permute-start.15 = (bf16[1,64,512]{2,1,0:T(8,128)(2,1)S(1)}, bf16[1,64,512]{2,1,0:T(8,128)(2,1)S(1)}, u32[]{:S(2)}, u32[]{:S(2)}) collective-permute-start(bf16[1,64,512]{2,1,0:T(8,128)(2,1)S(1)} %bitcast.26), channel_id=1, source_target_pairs={{16,12},{17,13},{18,14},{19,15},{20,8},{21,9},{22,10},{23,11},{24,... | collective-permute-start | bytes 196616 | tf_op jit(solution)/shard_map/ppermute | solution.py:41
  37.5 1.3 %collective-permute-start.21 = (bf16[4,64,512]{2,1,0:T(8,128)(2,1)S(1)}, bf16[4,64,512]{2,1,0:T(8,128)(2,1)S(1)}, u32[]{:S(2)}, u32[]{:S(2)}) collective-permute-start(bf16[4,64,512]{2,1,0:T(8,128)(2,1)S(1)} %get-tuple-element.59), channel_id=1, source_target_pairs={{16,3},{17,2},{18,1},{19,0},{20,7},{21,6},{22,5},{23,4},{24,11},{2... | collective-permute-start | bytes 786440 | tf_op jit(solution)/shard_map/ppermute | solution.py:41
  38.8 1.3 %collective-permute-start.22 = (bf16[4,64,512]{2,1,0:T(8,128)(2,1)S(1)}, bf16[4,64,512]{2,1,0:T(8,128)(2,1)S(1)}, u32[]{:S(2)}, u32[]{:S(2)}) collective-permute-start(bf16[4,64,512]{2,1,0:T(8,128)(2,1)S(1)} %get-tuple-element.60), channel_id=1, source_target_pairs={{16,2},{17,3},{18,0},{19,1},{20,6},{21,7},{22,4},{23,5},{24,10},{2... | collective-permute-start | bytes 786440 | tf_op jit(solution)/shard_map/ppermute | solution.py:41
  40.1 2.7 %collective-permute-done.16 = bf16[1,64,512]{2,1,0:T(8,128)(2,1)S(1)} collective-permute-done((bf16[1,64,512]{2,1,0:T(8,128)(2,1)S(1)}, bf16[1,64,512]{2,1,0:T(8,128)(2,1)S(1)}, u32[]{:S(2)}, u32[]{:S(2)}) %collective-permute-start.16) | collective-permute-done | bytes 65568 | tf_op jit(solution)/shard_map/ppermute | solution.py:41
  45.4 4.3 %collective-permute-start.20 = (bf16[4,64,512]{2,1,0:T(8,128)(2,1)S(1)}, bf16[4,64,512]{2,1,0:T(8,128)(2,1)S(1)}, u32[]{:S(2)}, u32[]{:S(2)}) collective-permute-start(bf16[4,64,512]{2,1,0:T(8,128)(2,1)S(1)} %constant_dynamic-update-slice_fusion.rest_0_), channel_id=1, source_target_pairs={{0,17},{1,16},{2,19},{3,18},{4,21},{5,20},{6,23},{7,22},{8,25},{9,... | collective-permute-start | bytes 786440 | tf_op jit(solution)/shard_map/ppermute | solution.py:41
  49.7 1.3 %collective-permute-start.18 = (bf16[4,64,512]{2,1,0:T(8,128)(2,1)S(1)}, bf16[4,64,512]{2,1,0:T(8,128)(2,1)S(1)}, u32[]{:S(2)}, u32[]{:S(2)}) collective-permute-start(bf16[4,64,512]{2,1,0:T(8,128)(2,1)S(1)} %constant_dynamic-update-slice_fusion.rest_0_), channel_id=1, source_target_pairs={{0,18},{1,19},{2,16},{3,17},{4,22},{5,23},{6,20},{7,21},{8,26},{9,... | collective-permute-start | bytes 786440 | tf_op jit(solution)/shard_map/ppermute | solution.py:41
  51.1 1.5 %collective-permute-start.19 = (bf16[4,64,512]{2,1,0:T(8,128)(2,1)S(1)}, bf16[4,64,512]{2,1,0:T(8,128)(2,1)S(1)}, u32[]{:S(2)}, u32[]{:S(2)}) collective-permute-start(bf16[4,64,512]{2,1,0:T(8,128)(2,1)S(1)} %constant_dynamic-update-slice_fusion.rest_0_), channel_id=1, source_target_pairs={{0,19},{1,18},{2,17},{3,16},{4,23},{5,22},{6,21},{7,20},{8,27},{9,... | collective-permute-start | bytes 786440 | tf_op jit(solution)/shard_map/ppermute | solution.py:41
  52.8 1.9 %collective-permute-start.25 = (bf16[1,64,512]{2,1,0:T(8,128)(2,1)S(1)}, bf16[1,64,512]{2,1,0:T(8,128)(2,1)S(1)}, u32[]{:S(2)}, u32[]{:S(2)}) collective-permute-start(bf16[1,64,512]{2,1,0:T(8,128)(2,1)S(1)} %get-tuple-element.68), channel_id=1, source_target_pairs={{0,28},{1,29},{2,30},{3,31},{4,24},{5,25},{6,26},{7,27},{8,20},{9,... | collective-permute-start | bytes 196616 | tf_op jit(solution)/shard_map/ppermute | solution.py:41
  54.7 1.3 %collective-permute-start.26 = (bf16[1,64,512]{2,1,0:T(8,128)(2,1)S(1)}, bf16[1,64,512]{2,1,0:T(8,128)(2,1)S(1)}, u32[]{:S(2)}, u32[]{:S(2)}) collective-permute-start(bf16[1,64,512]{2,1,0:T(8,128)(2,1)S(1)} %get-tuple-element.71), channel_id=1, source_target_pairs={{0,24},{1,25},{2,26},{3,27},{4,28},{5,29},{6,30},{7,31},{8,16},{9,... | collective-permute-start | bytes 196616 | tf_op jit(solution)/shard_map/ppermute | solution.py:41
  56.0 1.4 %collective-permute-start.27 = (bf16[1,64,512]{2,1,0:T(8,128)(2,1)S(1)}, bf16[1,64,512]{2,1,0:T(8,128)(2,1)S(1)}, u32[]{:S(2)}, u32[]{:S(2)}) collective-permute-start(bf16[1,64,512]{2,1,0:T(8,128)(2,1)S(1)} %get-tuple-element.70), channel_id=1, source_target_pairs={{0,20},{1,21},{2,22},{3,23},{4,16},{5,17},{6,18},{7,19},{8,28},{9,... | collective-permute-start | bytes 196616 | tf_op jit(solution)/shard_map/ppermute | solution.py:41
  57.7 3.0 %collective-permute-start.28 = (bf16[1,64,512]{2,1,0:T(8,128)(2,1)S(1)}, bf16[1,64,512]{2,1,0:T(8,128)(2,1)S(1)}, u32[]{:S(2)}, u32[]{:S(2)}) collective-permute-start(bf16[1,64,512]{2,1,0:T(8,128)(2,1)S(1)} %get-tuple-element.69), channel_id=1, source_target_pairs={{0,16},{1,17},{2,18},{3,19},{4,20},{5,21},{6,22},{7,23},{8,24},{9,... | collective-permute-start | bytes 196616 | tf_op jit(solution)/shard_map/ppermute | solution.py:41
  63.2 1.4 %collective-permute-start.30 = (bf16[32,256]{1,0:T(8,128)(2,1)S(1)}, bf16[32,256]{1,0:T(8,128)(2,1)S(1)}, u32[]{:S(2)}, u32[]{:S(2)}) collective-permute-start(bf16[32,256]{1,0:T(8,128)(2,1)S(1)} %add_convert_fusion.3), channel_id=1, source_target_pairs={{0,3},{1,2},{2,1},{3,0},{4,7},{5,6},{6,5},{7,4},{8,11},{9,10},{10,... | collective-permute-start | bytes 49160 | tf_op jit(solution)/shard_map/ppermute | solution.py:41
  69.6 2.3 %collective-permute-start.33 = (bf16[32,256]{1,0:T(8,128)(2,1)S(1)}, bf16[32,256]{1,0:T(8,128)(2,1)S(1)}, u32[]{:S(2)}, u32[]{:S(2)}) collective-permute-start(bf16[32,256]{1,0:T(8,128)(2,1)S(1)} %add_convert_fusion.2), channel_id=1, source_target_pairs={{0,12},{1,13},{2,14},{3,15},{4,8},{5,9},{6,10},{7,11},{8,4},{9,5},... | collective-permute-start | bytes 49160 | tf_op jit(solution)/shard_map/ppermute | solution.py:41
  72.0 2.0 %collective-permute-start.35 = (bf16[32,256]{1,0:T(8,128)(2,1)S(1)}, bf16[32,256]{1,0:T(8,128)(2,1)S(1)}, u32[]{:S(2)}, u32[]{:S(2)}) collective-permute-start(bf16[32,256]{1,0:T(8,128)(2,1)S(1)} %add_convert_fusion.2), channel_id=1, source_target_pairs={{0,4},{1,5},{2,6},{3,7},{4,0},{5,1},{6,2},{7,3},{8,12},{9,13},{10,... | collective-permute-start | bytes 49160 | tf_op jit(solution)/shard_map/ppermute | solution.py:41
  (95 shorter events, 27.5 us)
Async XLA Ops:
  0.6 12.8 %collective-permute-start = (bf16[1,64,512]{2,1,0:T(8,128)(2,1)}, bf16[1,64,512]{2,1,0:T(8,128)(2,1)S(1)}, u32[]{:S(2)}, u32[]{:S(2)}) collective-permute-start(bf16[1,64,512]{2,1,0:T(8,128)(2,1)} %bitcast.30), channel_id=1, source_target_pairs={{0,28},{1,29},{2,30},{3,31},{4,24},{5,25},{6,26},{7,27},{8,20},{9,... | collective-permute-start | bytes 196616 | tf_op jit(solution)/shard_map/ppermute | solution.py:41
  5.2 8.3 %collective-permute-start.1 = (bf16[1,64,512]{2,1,0:T(8,128)(2,1)}, bf16[1,64,512]{2,1,0:T(8,128)(2,1)S(1)}, u32[]{:S(2)}, u32[]{:S(2)}) collective-permute-start(bf16[1,64,512]{2,1,0:T(8,128)(2,1)} %bitcast.31), channel_id=1, source_target_pairs={{0,24},{1,25},{2,26},{3,27},{4,28},{5,29},{6,30},{7,31},{8,16},{9,... | collective-permute-start | bytes 196616 | tf_op jit(solution)/shard_map/ppermute | solution.py:41
  5.2 8.3 %collective-permute-start.2 = (bf16[1,64,512]{2,1,0:T(8,128)(2,1)}, bf16[1,64,512]{2,1,0:T(8,128)(2,1)S(1)}, u32[]{:S(2)}, u32[]{:S(2)}) collective-permute-start(bf16[1,64,512]{2,1,0:T(8,128)(2,1)} %bitcast.32), channel_id=1, source_target_pairs={{0,20},{1,21},{2,22},{3,23},{4,16},{5,17},{6,18},{7,19},{8,28},{9,... | collective-permute-start | bytes 196616 | tf_op jit(solution)/shard_map/ppermute | solution.py:41
  12.1 7.6 %collective-permute-start.7 = (bf16[4,64,512]{2,1,0:T(8,128)(2,1)S(1)}, bf16[4,64,512]{2,1,0:T(8,128)(2,1)S(1)}, u32[]{:S(2)}, u32[]{:S(2)}) collective-permute-start(bf16[4,64,512]{2,1,0:T(8,128)(2,1)S(1)} %get-tuple-element.46), channel_id=1, source_target_pairs={{0,18},{1,19},{2,16},{3,17},{4,22},{5,23},{6,20},{7,21},{8,26},{9,... | collective-permute-start | bytes 786440 | tf_op jit(solution)/shard_map/ppermute | solution.py:41
  13.5 7.5 %collective-permute-start.8 = (bf16[4,64,512]{2,1,0:T(8,128)(2,1)S(1)}, bf16[4,64,512]{2,1,0:T(8,128)(2,1)S(1)}, u32[]{:S(2)}, u32[]{:S(2)}) collective-permute-start(bf16[4,64,512]{2,1,0:T(8,128)(2,1)S(1)} %get-tuple-element.47), channel_id=1, source_target_pairs={{0,16},{1,17},{2,18},{3,19},{4,20},{5,21},{6,22},{7,23},{8,24},{9,... | collective-permute-start | bytes 786440 | tf_op jit(solution)/shard_map/ppermute | solution.py:41
  14.8 6.2 %collective-permute-start.9 = (bf16[4,64,512]{2,1,0:T(8,128)(2,1)S(1)}, bf16[4,64,512]{2,1,0:T(8,128)(2,1)S(1)}, u32[]{:S(2)}, u32[]{:S(2)}) collective-permute-start(bf16[4,64,512]{2,1,0:T(8,128)(2,1)S(1)} %get-tuple-element.48), channel_id=1, source_target_pairs={{0,17},{1,16},{2,19},{3,18},{4,21},{5,20},{6,23},{7,22},{8,25},{9,... | collective-permute-start | bytes 786440 | tf_op jit(solution)/shard_map/ppermute | solution.py:41
  16.4 8.4 %collective-permute-start.6 = (bf16[4,64,512]{2,1,0:T(8,128)(2,1)S(1)}, bf16[4,64,512]{2,1,0:T(8,128)(2,1)S(1)}, u32[]{:S(2)}, u32[]{:S(2)}) collective-permute-start(bf16[4,64,512]{2,1,0:T(8,128)(2,1)S(1)} %pad_maximum_fusion.rest_0_), channel_id=1, source_target_pairs={{16,1},{17,0},{18,3},{19,2},{20,5},{21,4},{22,7},{23,6},{24,9},{25... | collective-permute-start | bytes 786440 | tf_op jit(solution)/shard_map/ppermute | solution.py:41
  17.7 11.3 %collective-permute-start.4 = (bf16[4,64,512]{2,1,0:T(8,128)(2,1)S(1)}, bf16[4,64,512]{2,1,0:T(8,128)(2,1)S(1)}, u32[]{:S(2)}, u32[]{:S(2)}) collective-permute-start(bf16[4,64,512]{2,1,0:T(8,128)(2,1)S(1)} %pad_maximum_fusion.rest_0_), channel_id=1, source_target_pairs={{16,2},{17,3},{18,0},{19,1},{20,6},{21,7},{22,4},{23,5},{24,10},{2... | collective-permute-start | bytes 786440 | tf_op jit(solution)/shard_map/ppermute | solution.py:41
  19.7 10.5 %collective-permute-start.5 = (bf16[4,64,512]{2,1,0:T(8,128)(2,1)S(1)}, bf16[4,64,512]{2,1,0:T(8,128)(2,1)S(1)}, u32[]{:S(2)}, u32[]{:S(2)}) collective-permute-start(bf16[4,64,512]{2,1,0:T(8,128)(2,1)S(1)} %pad_maximum_fusion.rest_0_), channel_id=1, source_target_pairs={{16,3},{17,2},{18,1},{19,0},{20,7},{21,6},{22,5},{23,4},{24,11},{2... | collective-permute-start | bytes 786440 | tf_op jit(solution)/shard_map/ppermute | solution.py:41
  21.2 10.2 %collective-permute-start.10 = (bf16[1,64,512]{2,1,0:T(8,128)(2,1)S(1)}, bf16[1,64,512]{2,1,0:T(8,128)(2,1)S(1)}, u32[]{:S(2)}, u32[]{:S(2)}) collective-permute-start(bf16[1,64,512]{2,1,0:T(8,128)(2,1)S(1)} %get-tuple-element.72), channel_id=1, source_target_pairs={{16,12},{17,13},{18,14},{19,15},{20,8},{21,9},{22,10},{23,11},{24,... | collective-permute-start | bytes 196616 | tf_op jit(solution)/shard_map/ppermute | solution.py:41
  22.5 8.9 %collective-permute-start.11 = (bf16[1,64,512]{2,1,0:T(8,128)(2,1)S(1)}, bf16[1,64,512]{2,1,0:T(8,128)(2,1)S(1)}, u32[]{:S(2)}, u32[]{:S(2)}) collective-permute-start(bf16[1,64,512]{2,1,0:T(8,128)(2,1)S(1)} %get-tuple-element.75), channel_id=1, source_target_pairs={{16,8},{17,9},{18,10},{19,11},{20,12},{21,13},{22,14},{23,15},{24,... | collective-permute-start | bytes 196616 | tf_op jit(solution)/shard_map/ppermute | solution.py:41
  24.7 6.7 %collective-permute-start.12 = (bf16[1,64,512]{2,1,0:T(8,128)(2,1)S(1)}, bf16[1,64,512]{2,1,0:T(8,128)(2,1)S(1)}, u32[]{:S(2)}, u32[]{:S(2)}) collective-permute-start(bf16[1,64,512]{2,1,0:T(8,128)(2,1)S(1)} %get-tuple-element.74), channel_id=1, source_target_pairs={{16,4},{17,5},{18,6},{19,7},{20,0},{21,1},{22,2},{23,3},{24,12},{2... | collective-permute-start | bytes 196616 | tf_op jit(solution)/shard_map/ppermute | solution.py:41
  33.5 6.5 %collective-permute-start.15 = (bf16[1,64,512]{2,1,0:T(8,128)(2,1)S(1)}, bf16[1,64,512]{2,1,0:T(8,128)(2,1)S(1)}, u32[]{:S(2)}, u32[]{:S(2)}) collective-permute-start(bf16[1,64,512]{2,1,0:T(8,128)(2,1)S(1)} %bitcast.26), channel_id=1, source_target_pairs={{16,12},{17,13},{18,14},{19,15},{20,8},{21,9},{22,10},{23,11},{24,... | collective-permute-start | bytes 196616 | tf_op jit(solution)/shard_map/ppermute | solution.py:41
  36.6 6.2 %collective-permute-start.16 = (bf16[1,64,512]{2,1,0:T(8,128)(2,1)S(1)}, bf16[1,64,512]{2,1,0:T(8,128)(2,1)S(1)}, u32[]{:S(2)}, u32[]{:S(2)}) collective-permute-start(bf16[1,64,512]{2,1,0:T(8,128)(2,1)S(1)} %bitcast.27), channel_id=1, source_target_pairs={{16,8},{17,9},{18,10},{19,11},{20,12},{21,13},{22,14},{23,15},{24,... | collective-permute-start | bytes 196616 | tf_op jit(solution)/shard_map/ppermute | solution.py:41
  36.6 6.2 %collective-permute-start.17 = (bf16[1,64,512]{2,1,0:T(8,128)(2,1)S(1)}, bf16[1,64,512]{2,1,0:T(8,128)(2,1)S(1)}, u32[]{:S(2)}, u32[]{:S(2)}) collective-permute-start(bf16[1,64,512]{2,1,0:T(8,128)(2,1)S(1)} %bitcast.28), channel_id=1, source_target_pairs={{16,4},{17,5},{18,6},{19,7},{20,0},{21,1},{22,2},{23,3},{24,12},{2... | collective-permute-start | bytes 196616 | tf_op jit(solution)/shard_map/ppermute | solution.py:41
  37.5 12.2 %collective-permute-start.21 = (bf16[4,64,512]{2,1,0:T(8,128)(2,1)S(1)}, bf16[4,64,512]{2,1,0:T(8,128)(2,1)S(1)}, u32[]{:S(2)}, u32[]{:S(2)}) collective-permute-start(bf16[4,64,512]{2,1,0:T(8,128)(2,1)S(1)} %get-tuple-element.59), channel_id=1, source_target_pairs={{16,3},{17,2},{18,1},{19,0},{20,7},{21,6},{22,5},{23,4},{24,11},{2... | collective-permute-start | bytes 786440 | tf_op jit(solution)/shard_map/ppermute | solution.py:41
  38.8 12.3 %collective-permute-start.22 = (bf16[4,64,512]{2,1,0:T(8,128)(2,1)S(1)}, bf16[4,64,512]{2,1,0:T(8,128)(2,1)S(1)}, u32[]{:S(2)}, u32[]{:S(2)}) collective-permute-start(bf16[4,64,512]{2,1,0:T(8,128)(2,1)S(1)} %get-tuple-element.60), channel_id=1, source_target_pairs={{16,2},{17,3},{18,0},{19,1},{20,6},{21,7},{22,4},{23,5},{24,10},{2... | collective-permute-start | bytes 786440 | tf_op jit(solution)/shard_map/ppermute | solution.py:41
  42.8 9.8 %collective-permute-start.23 = (bf16[4,64,512]{2,1,0:T(8,128)(2,1)S(1)}, bf16[4,64,512]{2,1,0:T(8,128)(2,1)S(1)}, u32[]{:S(2)}, u32[]{:S(2)}) collective-permute-start(bf16[4,64,512]{2,1,0:T(8,128)(2,1)S(1)} %get-tuple-element.61), channel_id=1, source_target_pairs={{16,0},{17,1},{18,2},{19,3},{20,4},{21,5},{22,6},{23,7},{24,8},{25... | collective-permute-start | bytes 786440 | tf_op jit(solution)/shard_map/ppermute | solution.py:41
  44.1 8.6 %collective-permute-start.24 = (bf16[4,64,512]{2,1,0:T(8,128)(2,1)S(1)}, bf16[4,64,512]{2,1,0:T(8,128)(2,1)S(1)}, u32[]{:S(2)}, u32[]{:S(2)}) collective-permute-start(bf16[4,64,512]{2,1,0:T(8,128)(2,1)S(1)} %get-tuple-element.62), channel_id=1, source_target_pairs={{16,1},{17,0},{18,3},{19,2},{20,5},{21,4},{22,7},{23,6},{24,9},{25... | collective-permute-start | bytes 786440 | tf_op jit(solution)/shard_map/ppermute | solution.py:41
  45.4 10.6 %collective-permute-start.20 = (bf16[4,64,512]{2,1,0:T(8,128)(2,1)S(1)}, bf16[4,64,512]{2,1,0:T(8,128)(2,1)S(1)}, u32[]{:S(2)}, u32[]{:S(2)}) collective-permute-start(bf16[4,64,512]{2,1,0:T(8,128)(2,1)S(1)} %constant_dynamic-update-slice_fusion.rest_0_), channel_id=1, source_target_pairs={{0,17},{1,16},{2,19},{3,18},{4,21},{5,20},{6,23},{7,22},{8,25},{9,... | collective-permute-start | bytes 786440 | tf_op jit(solution)/shard_map/ppermute | solution.py:41
  49.7 8.0 %collective-permute-start.18 = (bf16[4,64,512]{2,1,0:T(8,128)(2,1)S(1)}, bf16[4,64,512]{2,1,0:T(8,128)(2,1)S(1)}, u32[]{:S(2)}, u32[]{:S(2)}) collective-permute-start(bf16[4,64,512]{2,1,0:T(8,128)(2,1)S(1)} %constant_dynamic-update-slice_fusion.rest_0_), channel_id=1, source_target_pairs={{0,18},{1,19},{2,16},{3,17},{4,22},{5,23},{6,20},{7,21},{8,26},{9,... | collective-permute-start | bytes 786440 | tf_op jit(solution)/shard_map/ppermute | solution.py:41
  51.1 9.7 %collective-permute-start.19 = (bf16[4,64,512]{2,1,0:T(8,128)(2,1)S(1)}, bf16[4,64,512]{2,1,0:T(8,128)(2,1)S(1)}, u32[]{:S(2)}, u32[]{:S(2)}) collective-permute-start(bf16[4,64,512]{2,1,0:T(8,128)(2,1)S(1)} %constant_dynamic-update-slice_fusion.rest_0_), channel_id=1, source_target_pairs={{0,19},{1,18},{2,17},{3,16},{4,23},{5,22},{6,21},{7,20},{8,27},{9,... | collective-permute-start | bytes 786440 | tf_op jit(solution)/shard_map/ppermute | solution.py:41
  52.8 8.2 %collective-permute-start.25 = (bf16[1,64,512]{2,1,0:T(8,128)(2,1)S(1)}, bf16[1,64,512]{2,1,0:T(8,128)(2,1)S(1)}, u32[]{:S(2)}, u32[]{:S(2)}) collective-permute-start(bf16[1,64,512]{2,1,0:T(8,128)(2,1)S(1)} %get-tuple-element.68), channel_id=1, source_target_pairs={{0,28},{1,29},{2,30},{3,31},{4,24},{5,25},{6,26},{7,27},{8,20},{9,... | collective-permute-start | bytes 196616 | tf_op jit(solution)/shard_map/ppermute | solution.py:41
  54.7 6.3 %collective-permute-start.26 = (bf16[1,64,512]{2,1,0:T(8,128)(2,1)S(1)}, bf16[1,64,512]{2,1,0:T(8,128)(2,1)S(1)}, u32[]{:S(2)}, u32[]{:S(2)}) collective-permute-start(bf16[1,64,512]{2,1,0:T(8,128)(2,1)S(1)} %get-tuple-element.71), channel_id=1, source_target_pairs={{0,24},{1,25},{2,26},{3,27},{4,28},{5,29},{6,30},{7,31},{8,16},{9,... | collective-permute-start | bytes 196616 | tf_op jit(solution)/shard_map/ppermute | solution.py:41
  (19 other events, 153.5 us)
where the time goes:
time: 78.5 us; the launch traced here: 78 us
  starting transfers between devices  52.5 us (67%)
  waiting for transfers between devices  15 us (19%)
  Pallas kernels  6.69 us (9%)
  other arithmetic  1.72 us (2%)
  between operations  1.2 us (2%)
  local copies, waits for them, and re-layouts  0.91 us (1%)
    ppermute x36, starting transfers between devices, exchange(): return lax.ppermute(value, axes, pairs)  52.5 us
    ppermute x36, waiting for transfers between devices, exchange(): return lax.ppermute(value, axes, pairs)  15 us
    pallas_call x1, Pallas kernels, spread(): pl.pallas_call(functools.partial(first_spread_kernel, outputs=groups, lay...  4.68 us
    pallas_call x4, Pallas kernels, meet(): pl.pallas_call(functools.partial(meet_kernel, first=first, blocks=len(gro...  1.83 us
  transfers between devices with their start and end apart: 36, of which 14 were waited for; matrix products, arithmetic and copies ran while one was open for 1% of the time, Pallas kernels for 8%

commit v1 on v0

--- a/solution.py
+++ b/solution.py
@@ -53,8 +53,7 @@
 
 
 def scatter_steps(radix, last):
-    half = radix // 2 if last else 0
-    return [*range(radix - 1, half - 1, -1), *range(half)]
+    return [*range(radix - 1, -1, -1)]
 
 
 def relative(digits, steps_of):
@@ -211,6 +210,28 @@
     )(hidden, head)
 
 
+def finish_kernel(*refs, terms):
+    values = paired_sum([ref[...].astype(jnp.float32) for ref in refs[:terms]])
+    reward, action, best, taken = refs[terms:]
+    values = values.reshape(*reward.shape, values.shape[1])
+    bins = lax.broadcasted_iota(jnp.int32, values.shape, 2)
+    picked = jnp.where(bins == action[...][:, :, None], values, 0.0)
+    best[...] = reward[...] + 0.98 * jnp.max(values, axis=2)
+    taken[...] = jnp.sum(picked, axis=2)
+
+
+def finish(terms, reward, action):
+    vmem = pl.BlockSpec(memory_space=pltpu.VMEM)
+    return pl.pallas_call(
+        functools.partial(finish_kernel, terms=len(terms)),
+        out_shape=[jax.ShapeDtypeStruct(reward.shape, jnp.float32)] * 2,
+        in_specs=[vmem] * (len(terms) + 2),
+        out_specs=[vmem] * 2,
+        compiler_params=pltpu.CompilerParams(vmem_limit_bytes=8 * 2**20),
+        name="finish",
+    )(*terms, reward, action)
+
+
 def paired_sum(terms):
     while len(terms) > 1:
         terms = [a + b for a, b in zip(terms[::2], terms[1::2])] + terms[len(terms) // 2 * 2 :]
@@ -261,7 +282,7 @@
                 for step in gather_steps(radix, final)
             ]
             if not final:
-                gathered, parts[half:] = lax.optimization_barrier((gathered, parts[half:]))
+                gathered, parts[-1:] = lax.optimization_barrier((gathered, parts[-1:]))
                 stack = jnp.concatenate(gathered, axis=0)
         wide = functools.reduce(jnp.add, [one.astype(jnp.float32) for one in sent])
         for number in range(rounds - 2, -1, -1):
@@ -285,22 +306,18 @@
         update = lax.rsqrt(square / features + 1e-06) * (0.25 * wide[0] + 0.75 * total)
         own = jnp.where(square >= 0.0, own.astype(jnp.float32) + update, 0.0).astype(jnp.bfloat16)
 
-    share_rows = reward.shape[1]
     end = sections - 1
     values = tell(own, head_weight, micro, sections)
     mine = values[end]
     for other in range(end):
         mine = mine + send(values[other], routes=[(end, other), (other, end)], radix=1, stride=1, step=0)
     everywhere = [(section, section) for section in range(sections)]
+    terms = [mine]
     for radix, stride in digits[::-1]:
-        told = mine.astype(jnp.bfloat16)
-        far = [send(told, routes=everywhere, radix=radix, stride=stride, step=step) for step in range(radix - 1, 0, -1)]
-        mine = paired_sum([term.astype(jnp.float32) for term in [*far, told]])
-    mine = mine.reshape(micro, share_rows, head_weight.shape[1])
-    best = jnp.max(mine, axis=2)
-    bin_ids = lax.broadcasted_iota(jnp.int32, mine.shape, 2)
-    taken = jnp.sum(jnp.where(bin_ids == action_bin[:, :, None], mine, 0.0), axis=2)
-    return (reward + 0.98 * best, taken)
+        told = paired_sum([term.astype(jnp.float32) for term in terms]).astype(jnp.bfloat16)
+        terms = [send(told, routes=everywhere, radix=radix, stride=stride, step=step) for step in range(radix - 1, 0, -1)]
+        terms.append(told)
+    return tuple(finish(terms, reward, action_bin))
 
 
 def solution(mesh):

time: 78.5 us -> 76.1 us (0.969)
  waiting for transfers between devices: 15 us -> 13.8 us
  local copies, waits for them, and re-layouts: 0.91 us -> 0.11 us
    ppermute x36, waiting for transfers between devices: 15 us -> 13.8 us  [exchange(): return lax.ppermute(value, axes, pairs)]
  transfers between devices with their start and end apart: 36 -> 36, of which waited for: 14 -> 13; matrix products, arithmetic and copies ran while one was open for 1% -> 1% of each run, Pallas kernels for 8% -> 9%
where the time goes in v1:
time: 76.1 us; the launch traced here: 75.6 us
  starting transfers between devices  52.1 us (68%)
  waiting for transfers between devices  13.8 us (18%)
  Pallas kernels  7.41 us (10%)
  between operations  1.19 us (2%)
  other arithmetic  0.98 us (1%)
    ppermute x36, starting transfers between devices, exchange(): return lax.ppermute(value, axes, pairs)  52.1 us
    ppermute x36, waiting for transfers between devices, exchange(): return lax.ppermute(value, axes, pairs)  13.8 us
    pallas_call x1, Pallas kernels, spread(): pl.pallas_call(functools.partial(first_spread_kernel, outputs=groups, lay...  4.68 us
    pallas_call x4, Pallas kernels, meet(): pl.pallas_call(functools.partial(meet_kernel, first=first, blocks=len(gro...  1.84 us
  transfers between devices with their start and end apart: 36, of which 13 were waited for; matrix products, arithmetic and copies ran while one was open for 1% of the time, Pallas kernels for 9%

profile of v1, /device:TPU:0, one launch (start us, length us, event | category | flops | bytes accessed | tf_op | source)
XLA Modules:
  0.0 75.6 jit_solution(17259235768519611697)
XLA Ops:
  0.6 4.6 %collective-permute-start = (bf16[1,64,512]{2,1,0:T(8,128)(2,1)}, bf16[1,64,512]{2,1,0:T(8,128)(2,1)S(1)}, u32[]{:S(2)}, u32[]{:S(2)}) collective-permute-start(bf16[1,64,512]{2,1,0:T(8,128)(2,1)} %bitcast.30), channel_id=1, source_target_pairs={{0,28},{1,29},{2,30},{3,31},{4,24},{5,25},{6,26},{7,27},{8,20},{9,... | collective-permute-start | bytes 196616 | tf_op jit(solution)/shard_map/ppermute | solution.py:41
  6.1 4.7 %first_spread.1 = (bf16[4,64,512]{2,1,0:T(8,128)(2,1)S(1)}, bf16[4,64,512]{2,1,0:T(8,128)(2,1)S(1)}, bf16[4,64,512]{2,1,0:T(8,128)(2,1)S(1)}, bf16[4,64,512]{2,1,0:T(8,128)(2,1)S(1)}) custom-call(bf16[64,512]{1,0:T(8,128)(2,1)} %bitcast.33, bf16[1,512,8192]{2,1,0:T(8,128)(2,1)} %weight.13), custom_call_target="tpu_custom_call" | custom-call | tf_op jit(solution)/shard_map/first_spread/pallas_call | solution.py:129
  10.8 1.3 %collective-permute-start.3 = (bf16[4,64,512]{2,1,0:T(8,128)(2,1)S(1)}, bf16[4,64,512]{2,1,0:T(8,128)(2,1)S(1)}, u32[]{:S(2)}, u32[]{:S(2)}) collective-permute-start(bf16[4,64,512]{2,1,0:T(8,128)(2,1)S(1)} %get-tuple-element.37), channel_id=1, source_target_pairs={{0,19},{1,18},{2,17},{3,16},{4,23},{5,22},{6,21},{7,20},{8,27},{9,... | collective-permute-start | bytes 786440 | tf_op jit(solution)/shard_map/ppermute | solution.py:41
  12.1 1.3 %collective-permute-start.7 = (bf16[4,64,512]{2,1,0:T(8,128)(2,1)S(1)}, bf16[4,64,512]{2,1,0:T(8,128)(2,1)S(1)}, u32[]{:S(2)}, u32[]{:S(2)}) collective-permute-start(bf16[4,64,512]{2,1,0:T(8,128)(2,1)S(1)} %get-tuple-element.43), channel_id=1, source_target_pairs={{0,18},{1,19},{2,16},{3,17},{4,22},{5,23},{6,20},{7,21},{8,26},{9,... | collective-permute-start | bytes 786440 | tf_op jit(solution)/shard_map/ppermute | solution.py:41
  13.5 1.3 %collective-permute-start.8 = (bf16[4,64,512]{2,1,0:T(8,128)(2,1)S(1)}, bf16[4,64,512]{2,1,0:T(8,128)(2,1)S(1)}, u32[]{:S(2)}, u32[]{:S(2)}) collective-permute-start(bf16[4,64,512]{2,1,0:T(8,128)(2,1)S(1)} %get-tuple-element.44), channel_id=1, source_target_pairs={{0,17},{1,16},{2,19},{3,18},{4,21},{5,20},{6,23},{7,22},{8,25},{9,... | collective-permute-start | bytes 786440 | tf_op jit(solution)/shard_map/ppermute | solution.py:41
  14.8 1.3 %collective-permute-start.9 = (bf16[4,64,512]{2,1,0:T(8,128)(2,1)S(1)}, bf16[4,64,512]{2,1,0:T(8,128)(2,1)S(1)}, u32[]{:S(2)}, u32[]{:S(2)}) collective-permute-start(bf16[4,64,512]{2,1,0:T(8,128)(2,1)S(1)} %get-tuple-element.45), channel_id=1, source_target_pairs={{0,16},{1,17},{2,18},{3,19},{4,20},{5,21},{6,22},{7,23},{8,24},{9,... | collective-permute-start | bytes 786440 | tf_op jit(solution)/shard_map/ppermute | solution.py:41
  16.2 1.3 %collective-permute-start.6 = (bf16[4,64,512]{2,1,0:T(8,128)(2,1)S(1)}, bf16[4,64,512]{2,1,0:T(8,128)(2,1)S(1)}, u32[]{:S(2)}, u32[]{:S(2)}) collective-permute-start(bf16[4,64,512]{2,1,0:T(8,128)(2,1)S(1)} %pad_maximum_fusion.rest_0_), channel_id=1, source_target_pairs={{16,1},{17,0},{18,3},{19,2},{20,5},{21,4},{22,7},{23,6},{24,9},{25... | collective-permute-start | bytes 786440 | tf_op jit(solution)/shard_map/ppermute | solution.py:41
  17.5 1.3 %collective-permute-start.4 = (bf16[4,64,512]{2,1,0:T(8,128)(2,1)S(1)}, bf16[4,64,512]{2,1,0:T(8,128)(2,1)S(1)}, u32[]{:S(2)}, u32[]{:S(2)}) collective-permute-start(bf16[4,64,512]{2,1,0:T(8,128)(2,1)S(1)} %pad_maximum_fusion.rest_0_), channel_id=1, source_target_pairs={{16,2},{17,3},{18,0},{19,1},{20,6},{21,7},{22,4},{23,5},{24,10},{2... | collective-permute-start | bytes 786440 | tf_op jit(solution)/shard_map/ppermute | solution.py:41
  21.2 1.3 %collective-permute-start.10 = (bf16[1,64,512]{2,1,0:T(8,128)(2,1)S(1)}, bf16[1,64,512]{2,1,0:T(8,128)(2,1)S(1)}, u32[]{:S(2)}, u32[]{:S(2)}) collective-permute-start(bf16[1,64,512]{2,1,0:T(8,128)(2,1)S(1)} %get-tuple-element.66), channel_id=1, source_target_pairs={{16,12},{17,13},{18,14},{19,15},{20,8},{21,9},{22,10},{23,11},{24,... | collective-permute-start | bytes 196616 | tf_op jit(solution)/shard_map/ppermute | solution.py:41
  24.3 1.5 %collective-permute-start.12 = (bf16[1,64,512]{2,1,0:T(8,128)(2,1)S(1)}, bf16[1,64,512]{2,1,0:T(8,128)(2,1)S(1)}, u32[]{:S(2)}, u32[]{:S(2)}) collective-permute-start(bf16[1,64,512]{2,1,0:T(8,128)(2,1)S(1)} %get-tuple-element.68), channel_id=1, source_target_pairs={{16,4},{17,5},{18,6},{19,7},{20,0},{21,1},{22,2},{23,3},{24,12},{2... | collective-permute-start | bytes 196616 | tf_op jit(solution)/shard_map/ppermute | solution.py:41
  26.7 2.2 %collective-permute-done.4.rest_0_ = bf16[4,64,512]{2,1,0:T(8,128)(2,1)S(1)} collective-permute-done((bf16[4,64,512]{2,1,0:T(8,128)(2,1)S(1)}, bf16[4,64,512]{2,1,0:T(8,128)(2,1)S(1)}, u32[]{:S(2)}, u32[]{:S(2)}) %collective-permute-start.4) | collective-permute-done | bytes 262176 | tf_op jit(solution)/shard_map/ppermute | solution.py:41
  33.5 3.0 %collective-permute-start.15 = (bf16[1,64,512]{2,1,0:T(8,128)(2,1)S(1)}, bf16[1,64,512]{2,1,0:T(8,128)(2,1)S(1)}, u32[]{:S(2)}, u32[]{:S(2)}) collective-permute-start(bf16[1,64,512]{2,1,0:T(8,128)(2,1)S(1)} %bitcast.26), channel_id=1, source_target_pairs={{16,12},{17,13},{18,14},{19,15},{20,8},{21,9},{22,10},{23,11},{24,... | collective-permute-start | bytes 196616 | tf_op jit(solution)/shard_map/ppermute | solution.py:41
  41.4 1.4 %collective-permute-done.16 = bf16[1,64,512]{2,1,0:T(8,128)(2,1)S(1)} collective-permute-done((bf16[1,64,512]{2,1,0:T(8,128)(2,1)S(1)}, bf16[1,64,512]{2,1,0:T(8,128)(2,1)S(1)}, u32[]{:S(2)}, u32[]{:S(2)}) %collective-permute-start.16) | collective-permute-done | bytes 65568 | tf_op jit(solution)/shard_map/ppermute | solution.py:41
  44.1 3.2 %collective-permute-start.20 = (bf16[4,64,512]{2,1,0:T(8,128)(2,1)S(1)}, bf16[4,64,512]{2,1,0:T(8,128)(2,1)S(1)}, u32[]{:S(2)}, u32[]{:S(2)}) collective-permute-start(bf16[4,64,512]{2,1,0:T(8,128)(2,1)S(1)} %constant_dynamic-update-slice_fusion.rest_0_), channel_id=1, source_target_pairs={{0,17},{1,16},{2,19},{3,18},{4,21},{5,20},{6,23},{7,22},{8,25},{9,... | collective-permute-start | bytes 786440 | tf_op jit(solution)/shard_map/ppermute | solution.py:41
  47.4 1.5 %collective-permute-start.18 = (bf16[4,64,512]{2,1,0:T(8,128)(2,1)S(1)}, bf16[4,64,512]{2,1,0:T(8,128)(2,1)S(1)}, u32[]{:S(2)}, u32[]{:S(2)}) collective-permute-start(bf16[4,64,512]{2,1,0:T(8,128)(2,1)S(1)} %constant_dynamic-update-slice_fusion.rest_0_), channel_id=1, source_target_pairs={{0,18},{1,19},{2,16},{3,17},{4,22},{5,23},{6,20},{7,21},{8,26},{9,... | collective-permute-start | bytes 786440 | tf_op jit(solution)/shard_map/ppermute | solution.py:41
  48.9 1.9 %collective-permute-start.19 = (bf16[4,64,512]{2,1,0:T(8,128)(2,1)S(1)}, bf16[4,64,512]{2,1,0:T(8,128)(2,1)S(1)}, u32[]{:S(2)}, u32[]{:S(2)}) collective-permute-start(bf16[4,64,512]{2,1,0:T(8,128)(2,1)S(1)} %constant_dynamic-update-slice_fusion.rest_0_), channel_id=1, source_target_pairs={{0,19},{1,18},{2,17},{3,16},{4,23},{5,22},{6,21},{7,20},{8,27},{9,... | collective-permute-start | bytes 786440 | tf_op jit(solution)/shard_map/ppermute | solution.py:41
  51.1 2.8 %collective-permute-start.25 = (bf16[1,64,512]{2,1,0:T(8,128)(2,1)S(1)}, bf16[1,64,512]{2,1,0:T(8,128)(2,1)S(1)}, u32[]{:S(2)}, u32[]{:S(2)}) collective-permute-start(bf16[1,64,512]{2,1,0:T(8,128)(2,1)S(1)} %get-tuple-element.62), channel_id=1, source_target_pairs={{0,28},{1,29},{2,30},{3,31},{4,24},{5,25},{6,26},{7,27},{8,20},{9,... | collective-permute-start | bytes 196616 | tf_op jit(solution)/shard_map/ppermute | solution.py:41
  53.8 1.3 %collective-permute-start.26 = (bf16[1,64,512]{2,1,0:T(8,128)(2,1)S(1)}, bf16[1,64,512]{2,1,0:T(8,128)(2,1)S(1)}, u32[]{:S(2)}, u32[]{:S(2)}) collective-permute-start(bf16[1,64,512]{2,1,0:T(8,128)(2,1)S(1)} %get-tuple-element.65), channel_id=1, source_target_pairs={{0,24},{1,25},{2,26},{3,27},{4,28},{5,29},{6,30},{7,31},{8,16},{9,... | collective-permute-start | bytes 196616 | tf_op jit(solution)/shard_map/ppermute | solution.py:41
  55.2 1.4 %collective-permute-start.27 = (bf16[1,64,512]{2,1,0:T(8,128)(2,1)S(1)}, bf16[1,64,512]{2,1,0:T(8,128)(2,1)S(1)}, u32[]{:S(2)}, u32[]{:S(2)}) collective-permute-start(bf16[1,64,512]{2,1,0:T(8,128)(2,1)S(1)} %get-tuple-element.64), channel_id=1, source_target_pairs={{0,20},{1,21},{2,22},{3,23},{4,16},{5,17},{6,18},{7,19},{8,28},{9,... | collective-permute-start | bytes 196616 | tf_op jit(solution)/shard_map/ppermute | solution.py:41
  56.7 2.3 %collective-permute-start.28 = (bf16[1,64,512]{2,1,0:T(8,128)(2,1)S(1)}, bf16[1,64,512]{2,1,0:T(8,128)(2,1)S(1)}, u32[]{:S(2)}, u32[]{:S(2)}) collective-permute-start(bf16[1,64,512]{2,1,0:T(8,128)(2,1)S(1)} %get-tuple-element.63), channel_id=1, source_target_pairs={{0,16},{1,17},{2,18},{3,19},{4,20},{5,21},{6,22},{7,23},{8,24},{9,... | collective-permute-start | bytes 196616 | tf_op jit(solution)/shard_map/ppermute | solution.py:41
  61.4 1.5 %collective-permute-start.30 = (bf16[32,256]{1,0:T(8,128)(2,1)S(1)}, bf16[32,256]{1,0:T(8,128)(2,1)S(1)}, u32[]{:S(2)}, u32[]{:S(2)}) collective-permute-start(bf16[32,256]{1,0:T(8,128)(2,1)S(1)} %add_convert_fusion.3), channel_id=1, source_target_pairs={{0,3},{1,2},{2,1},{3,0},{4,7},{5,6},{6,5},{7,4},{8,11},{9,10},{10,... | collective-permute-start | bytes 49160 | tf_op jit(solution)/shard_map/ppermute | solution.py:41
  67.5 2.7 %collective-permute-start.33 = (bf16[32,256]{1,0:T(8,128)(2,1)S(1)}, bf16[32,256]{1,0:T(8,128)(2,1)S(1)}, u32[]{:S(2)}, u32[]{:S(2)}) collective-permute-start(bf16[32,256]{1,0:T(8,128)(2,1)S(1)} %add_convert_fusion.2.refs_3_), channel_id=1, source_target_pairs={{0,12},{1,13},{2,14},{3,15},{4,8},{5,9},{6,10},{7,11},{8,4},{9,5},... | collective-permute-start | bytes 49160 | tf_op jit(solution)/shard_map/ppermute | solution.py:41
  70.2 1.7 %collective-permute-start.35 = (bf16[32,256]{1,0:T(8,128)(2,1)S(1)}, bf16[32,256]{1,0:T(8,128)(2,1)S(1)}, u32[]{:S(2)}, u32[]{:S(2)}) collective-permute-start(bf16[32,256]{1,0:T(8,128)(2,1)S(1)} %add_convert_fusion.2.refs_3_), channel_id=1, source_target_pairs={{0,4},{1,5},{2,6},{3,7},{4,0},{5,1},{6,2},{7,3},{8,12},{9,13},{10,... | collective-permute-start | bytes 49160 | tf_op jit(solution)/shard_map/ppermute | solution.py:41
  73.1 1.8 %collective-permute-done.34.refs_1_ = bf16[32,256]{1,0:T(8,128)(2,1)S(1)} collective-permute-done((bf16[32,256]{1,0:T(8,128)(2,1)S(1)}, bf16[32,256]{1,0:T(8,128)(2,1)S(1)}, u32[]{:S(2)}, u32[]{:S(2)}) %collective-permute-start.34) | collective-permute-done | bytes 16416 | tf_op jit(solution)/shard_map/ppermute | solution.py:41
  (90 shorter events, 25.7 us)
Async XLA Ops:
  0.6 12.8 %collective-permute-start = (bf16[1,64,512]{2,1,0:T(8,128)(2,1)}, bf16[1,64,512]{2,1,0:T(8,128)(2,1)S(1)}, u32[]{:S(2)}, u32[]{:S(2)}) collective-permute-start(bf16[1,64,512]{2,1,0:T(8,128)(2,1)} %bitcast.30), channel_id=1, source_target_pairs={{0,28},{1,29},{2,30},{3,31},{4,24},{5,25},{6,26},{7,27},{8,20},{9,... | collective-permute-start | bytes 196616 | tf_op jit(solution)/shard_map/ppermute | solution.py:41
  5.2 9.6 %collective-permute-start.1 = (bf16[1,64,512]{2,1,0:T(8,128)(2,1)}, bf16[1,64,512]{2,1,0:T(8,128)(2,1)S(1)}, u32[]{:S(2)}, u32[]{:S(2)}) collective-permute-start(bf16[1,64,512]{2,1,0:T(8,128)(2,1)} %bitcast.31), channel_id=1, source_target_pairs={{0,24},{1,25},{2,26},{3,27},{4,28},{5,29},{6,30},{7,31},{8,16},{9,... | collective-permute-start | bytes 196616 | tf_op jit(solution)/shard_map/ppermute | solution.py:41
  5.2 9.6 %collective-permute-start.2 = (bf16[1,64,512]{2,1,0:T(8,128)(2,1)}, bf16[1,64,512]{2,1,0:T(8,128)(2,1)S(1)}, u32[]{:S(2)}, u32[]{:S(2)}) collective-permute-start(bf16[1,64,512]{2,1,0:T(8,128)(2,1)} %bitcast.32), channel_id=1, source_target_pairs={{0,20},{1,21},{2,22},{3,23},{4,16},{5,17},{6,18},{7,19},{8,28},{9,... | collective-permute-start | bytes 196616 | tf_op jit(solution)/shard_map/ppermute | solution.py:41
  12.1 7.6 %collective-permute-start.7 = (bf16[4,64,512]{2,1,0:T(8,128)(2,1)S(1)}, bf16[4,64,512]{2,1,0:T(8,128)(2,1)S(1)}, u32[]{:S(2)}, u32[]{:S(2)}) collective-permute-start(bf16[4,64,512]{2,1,0:T(8,128)(2,1)S(1)} %get-tuple-element.43), channel_id=1, source_target_pairs={{0,18},{1,19},{2,16},{3,17},{4,22},{5,23},{6,20},{7,21},{8,26},{9,... | collective-permute-start | bytes 786440 | tf_op jit(solution)/shard_map/ppermute | solution.py:41
  13.5 7.6 %collective-permute-start.8 = (bf16[4,64,512]{2,1,0:T(8,128)(2,1)S(1)}, bf16[4,64,512]{2,1,0:T(8,128)(2,1)S(1)}, u32[]{:S(2)}, u32[]{:S(2)}) collective-permute-start(bf16[4,64,512]{2,1,0:T(8,128)(2,1)S(1)} %get-tuple-element.44), channel_id=1, source_target_pairs={{0,17},{1,16},{2,19},{3,18},{4,21},{5,20},{6,23},{7,22},{8,25},{9,... | collective-permute-start | bytes 786440 | tf_op jit(solution)/shard_map/ppermute | solution.py:41
  14.8 6.2 %collective-permute-start.9 = (bf16[4,64,512]{2,1,0:T(8,128)(2,1)S(1)}, bf16[4,64,512]{2,1,0:T(8,128)(2,1)S(1)}, u32[]{:S(2)}, u32[]{:S(2)}) collective-permute-start(bf16[4,64,512]{2,1,0:T(8,128)(2,1)S(1)} %get-tuple-element.45), channel_id=1, source_target_pairs={{0,16},{1,17},{2,18},{3,19},{4,20},{5,21},{6,22},{7,23},{8,24},{9,... | collective-permute-start | bytes 786440 | tf_op jit(solution)/shard_map/ppermute | solution.py:41
  16.2 8.1 %collective-permute-start.6 = (bf16[4,64,512]{2,1,0:T(8,128)(2,1)S(1)}, bf16[4,64,512]{2,1,0:T(8,128)(2,1)S(1)}, u32[]{:S(2)}, u32[]{:S(2)}) collective-permute-start(bf16[4,64,512]{2,1,0:T(8,128)(2,1)S(1)} %pad_maximum_fusion.rest_0_), channel_id=1, source_target_pairs={{16,1},{17,0},{18,3},{19,2},{20,5},{21,4},{22,7},{23,6},{24,9},{25... | collective-permute-start | bytes 786440 | tf_op jit(solution)/shard_map/ppermute | solution.py:41
  17.5 11.5 %collective-permute-start.4 = (bf16[4,64,512]{2,1,0:T(8,128)(2,1)S(1)}, bf16[4,64,512]{2,1,0:T(8,128)(2,1)S(1)}, u32[]{:S(2)}, u32[]{:S(2)}) collective-permute-start(bf16[4,64,512]{2,1,0:T(8,128)(2,1)S(1)} %pad_maximum_fusion.rest_0_), channel_id=1, source_target_pairs={{16,2},{17,3},{18,0},{19,1},{20,6},{21,7},{22,4},{23,5},{24,10},{2... | collective-permute-start | bytes 786440 | tf_op jit(solution)/shard_map/ppermute | solution.py:41
  19.7 10.5 %collective-permute-start.5 = (bf16[4,64,512]{2,1,0:T(8,128)(2,1)S(1)}, bf16[4,64,512]{2,1,0:T(8,128)(2,1)S(1)}, u32[]{:S(2)}, u32[]{:S(2)}) collective-permute-start(bf16[4,64,512]{2,1,0:T(8,128)(2,1)S(1)} %pad_maximum_fusion.rest_0_), channel_id=1, source_target_pairs={{16,3},{17,2},{18,1},{19,0},{20,7},{21,6},{22,5},{23,4},{24,11},{2... | collective-permute-start | bytes 786440 | tf_op jit(solution)/shard_map/ppermute | solution.py:41
  21.2 10.2 %collective-permute-start.10 = (bf16[1,64,512]{2,1,0:T(8,128)(2,1)S(1)}, bf16[1,64,512]{2,1,0:T(8,128)(2,1)S(1)}, u32[]{:S(2)}, u32[]{:S(2)}) collective-permute-start(bf16[1,64,512]{2,1,0:T(8,128)(2,1)S(1)} %get-tuple-element.66), channel_id=1, source_target_pairs={{16,12},{17,13},{18,14},{19,15},{20,8},{21,9},{22,10},{23,11},{24,... | collective-permute-start | bytes 196616 | tf_op jit(solution)/shard_map/ppermute | solution.py:41
  22.5 8.9 %collective-permute-start.11 = (bf16[1,64,512]{2,1,0:T(8,128)(2,1)S(1)}, bf16[1,64,512]{2,1,0:T(8,128)(2,1)S(1)}, u32[]{:S(2)}, u32[]{:S(2)}) collective-permute-start(bf16[1,64,512]{2,1,0:T(8,128)(2,1)S(1)} %get-tuple-element.69), channel_id=1, source_target_pairs={{16,8},{17,9},{18,10},{19,11},{20,12},{21,13},{22,14},{23,15},{24,... | collective-permute-start | bytes 196616 | tf_op jit(solution)/shard_map/ppermute | solution.py:41
  24.3 7.2 %collective-permute-start.12 = (bf16[1,64,512]{2,1,0:T(8,128)(2,1)S(1)}, bf16[1,64,512]{2,1,0:T(8,128)(2,1)S(1)}, u32[]{:S(2)}, u32[]{:S(2)}) collective-permute-start(bf16[1,64,512]{2,1,0:T(8,128)(2,1)S(1)} %get-tuple-element.68), channel_id=1, source_target_pairs={{16,4},{17,5},{18,6},{19,7},{20,0},{21,1},{22,2},{23,3},{24,12},{2... | collective-permute-start | bytes 196616 | tf_op jit(solution)/shard_map/ppermute | solution.py:41
  33.5 6.5 %collective-permute-start.15 = (bf16[1,64,512]{2,1,0:T(8,128)(2,1)S(1)}, bf16[1,64,512]{2,1,0:T(8,128)(2,1)S(1)}, u32[]{:S(2)}, u32[]{:S(2)}) collective-permute-start(bf16[1,64,512]{2,1,0:T(8,128)(2,1)S(1)} %bitcast.26), channel_id=1, source_target_pairs={{16,12},{17,13},{18,14},{19,15},{20,8},{21,9},{22,10},{23,11},{24,... | collective-permute-start | bytes 196616 | tf_op jit(solution)/shard_map/ppermute | solution.py:41
  36.6 6.2 %collective-permute-start.16 = (bf16[1,64,512]{2,1,0:T(8,128)(2,1)S(1)}, bf16[1,64,512]{2,1,0:T(8,128)(2,1)S(1)}, u32[]{:S(2)}, u32[]{:S(2)}) collective-permute-start(bf16[1,64,512]{2,1,0:T(8,128)(2,1)S(1)} %bitcast.27), channel_id=1, source_target_pairs={{16,8},{17,9},{18,10},{19,11},{20,12},{21,13},{22,14},{23,15},{24,... | collective-permute-start | bytes 196616 | tf_op jit(solution)/shard_map/ppermute | solution.py:41
  36.6 6.2 %collective-permute-start.17 = (bf16[1,64,512]{2,1,0:T(8,128)(2,1)S(1)}, bf16[1,64,512]{2,1,0:T(8,128)(2,1)S(1)}, u32[]{:S(2)}, u32[]{:S(2)}) collective-permute-start(bf16[1,64,512]{2,1,0:T(8,128)(2,1)S(1)} %bitcast.28), channel_id=1, source_target_pairs={{16,4},{17,5},{18,6},{19,7},{20,0},{21,1},{22,2},{23,3},{24,12},{2... | collective-permute-start | bytes 196616 | tf_op jit(solution)/shard_map/ppermute | solution.py:41
  37.5 9.9 %collective-permute-start.21 = (bf16[4,64,512]{2,1,0:T(8,128)(2,1)S(1)}, bf16[4,64,512]{2,1,0:T(8,128)(2,1)S(1)}, u32[]{:S(2)}, u32[]{:S(2)}) collective-permute-start(bf16[4,64,512]{2,1,0:T(8,128)(2,1)S(1)} %get-tuple-element.55), channel_id=1, source_target_pairs={{16,3},{17,2},{18,1},{19,0},{20,7},{21,6},{22,5},{23,4},{24,11},{2... | collective-permute-start | bytes 786440 | tf_op jit(solution)/shard_map/ppermute | solution.py:41
  38.8 10.1 %collective-permute-start.22 = (bf16[4,64,512]{2,1,0:T(8,128)(2,1)S(1)}, bf16[4,64,512]{2,1,0:T(8,128)(2,1)S(1)}, u32[]{:S(2)}, u32[]{:S(2)}) collective-permute-start(bf16[4,64,512]{2,1,0:T(8,128)(2,1)S(1)} %get-tuple-element.56), channel_id=1, source_target_pairs={{16,2},{17,3},{18,0},{19,1},{20,6},{21,7},{22,4},{23,5},{24,10},{2... | collective-permute-start | bytes 786440 | tf_op jit(solution)/shard_map/ppermute | solution.py:41
  40.1 10.8 %collective-permute-start.23 = (bf16[4,64,512]{2,1,0:T(8,128)(2,1)S(1)}, bf16[4,64,512]{2,1,0:T(8,128)(2,1)S(1)}, u32[]{:S(2)}, u32[]{:S(2)}) collective-permute-start(bf16[4,64,512]{2,1,0:T(8,128)(2,1)S(1)} %get-tuple-element.57), channel_id=1, source_target_pairs={{16,1},{17,0},{18,3},{19,2},{20,5},{21,4},{22,7},{23,6},{24,9},{25... | collective-permute-start | bytes 786440 | tf_op jit(solution)/shard_map/ppermute | solution.py:41
  42.8 8.1 %collective-permute-start.24 = (bf16[4,64,512]{2,1,0:T(8,128)(2,1)S(1)}, bf16[4,64,512]{2,1,0:T(8,128)(2,1)S(1)}, u32[]{:S(2)}, u32[]{:S(2)}) collective-permute-start(bf16[4,64,512]{2,1,0:T(8,128)(2,1)S(1)} %get-tuple-element.58), channel_id=1, source_target_pairs={{16,0},{17,1},{18,2},{19,3},{20,4},{21,5},{22,6},{23,7},{24,8},{25... | collective-permute-start | bytes 786440 | tf_op jit(solution)/shard_map/ppermute | solution.py:41
  44.1 11.0 %collective-permute-start.20 = (bf16[4,64,512]{2,1,0:T(8,128)(2,1)S(1)}, bf16[4,64,512]{2,1,0:T(8,128)(2,1)S(1)}, u32[]{:S(2)}, u32[]{:S(2)}) collective-permute-start(bf16[4,64,512]{2,1,0:T(8,128)(2,1)S(1)} %constant_dynamic-update-slice_fusion.rest_0_), channel_id=1, source_target_pairs={{0,17},{1,16},{2,19},{3,18},{4,21},{5,20},{6,23},{7,22},{8,25},{9,... | collective-permute-start | bytes 786440 | tf_op jit(solution)/shard_map/ppermute | solution.py:41
  47.4 9.3 %collective-permute-start.18 = (bf16[4,64,512]{2,1,0:T(8,128)(2,1)S(1)}, bf16[4,64,512]{2,1,0:T(8,128)(2,1)S(1)}, u32[]{:S(2)}, u32[]{:S(2)}) collective-permute-start(bf16[4,64,512]{2,1,0:T(8,128)(2,1)S(1)} %constant_dynamic-update-slice_fusion.rest_0_), channel_id=1, source_target_pairs={{0,18},{1,19},{2,16},{3,17},{4,22},{5,23},{6,20},{7,21},{8,26},{9,... | collective-permute-start | bytes 786440 | tf_op jit(solution)/shard_map/ppermute | solution.py:41
  48.9 10.0 %collective-permute-start.19 = (bf16[4,64,512]{2,1,0:T(8,128)(2,1)S(1)}, bf16[4,64,512]{2,1,0:T(8,128)(2,1)S(1)}, u32[]{:S(2)}, u32[]{:S(2)}) collective-permute-start(bf16[4,64,512]{2,1,0:T(8,128)(2,1)S(1)} %constant_dynamic-update-slice_fusion.rest_0_), channel_id=1, source_target_pairs={{0,19},{1,18},{2,17},{3,16},{4,23},{5,22},{6,21},{7,20},{8,27},{9,... | collective-permute-start | bytes 786440 | tf_op jit(solution)/shard_map/ppermute | solution.py:41
  51.1 8.2 %collective-permute-start.25 = (bf16[1,64,512]{2,1,0:T(8,128)(2,1)S(1)}, bf16[1,64,512]{2,1,0:T(8,128)(2,1)S(1)}, u32[]{:S(2)}, u32[]{:S(2)}) collective-permute-start(bf16[1,64,512]{2,1,0:T(8,128)(2,1)S(1)} %get-tuple-element.62), channel_id=1, source_target_pairs={{0,28},{1,29},{2,30},{3,31},{4,24},{5,25},{6,26},{7,27},{8,20},{9,... | collective-permute-start | bytes 196616 | tf_op jit(solution)/shard_map/ppermute | solution.py:41
  67.5 5.6 %collective-permute-start.33 = (bf16[32,256]{1,0:T(8,128)(2,1)S(1)}, bf16[32,256]{1,0:T(8,128)(2,1)S(1)}, u32[]{:S(2)}, u32[]{:S(2)}) collective-permute-start(bf16[32,256]{1,0:T(8,128)(2,1)S(1)} %add_convert_fusion.2.refs_3_), channel_id=1, source_target_pairs={{0,12},{1,13},{2,14},{3,15},{4,8},{5,9},{6,10},{7,11},{8,4},{9,5},... | collective-permute-start | bytes 49160 | tf_op jit(solution)/shard_map/ppermute | solution.py:41
  (19 other events, 150.5 us)

commit v2 on v1

--- a/solution.py
+++ b/solution.py
@@ -266,17 +266,17 @@
         stack = own[None]
         for number, (radix, stride) in enumerate(digits):
             final = number == rounds - 1
-            routes = both
             if final:
-                routes = [(helper, layer)]
                 at = layer if number % 2 == 0 else helper
                 sent = []
                 for step, one in zip(scatter_steps(radix, True), parts):
                     if step > 0 or at != layer:
-                        one = send(one, routes=[(layer, at)], radix=radix, stride=stride, step=step)
+                        routes = both if step == 0 else [(layer, at)]
+                        one = send(one, routes=routes, radix=radix, stride=stride, step=step)
                     sent.append(one)
                 if layer == 0 and rounds > 1:
                     stack, sent[:1] = lax.optimization_barrier((stack, sent[:1]))
+            routes = [(helper, layer)] if final else both
             gathered = [
                 stack if step == 0 else send(stack, routes=routes, radix=radix, stride=stride, step=step)
                 for step in gather_steps(radix, final)
@@ -293,7 +293,8 @@
             for i, step in enumerate(scatter_steps(radix, False)):
                 one = wide[i * part : (i + 1) * part].astype(jnp.bfloat16)
                 if step > 0 or to != at:
-                    one = send(one, routes=[(at, to)], radix=radix, stride=stride, step=step)
+                    routes = both if step == 0 else [(at, to)]
+                    one = send(one, routes=routes, radix=radix, stride=stride, step=step)
                 sent.append(one)
             at = to
             wide = functools.reduce(jnp.add, [one.astype(jnp.float32) for one in sent])

time: 76.1 us -> 72.9 us (0.958)
  starting transfers between devices: 52.1 us -> 46.6 us
  waiting for transfers between devices: 13.8 us -> 16.3 us
    ppermute x36, starting transfers between devices: 52.1 us -> 46.6 us  [exchange(): return lax.ppermute(value, axes, pairs)]
    ppermute x36, waiting for transfers between devices: 13.8 us -> 16.3 us  [exchange(): return lax.ppermute(value, axes, pairs)]
  transfers between devices with their start and end apart: 36 -> 36, of which waited for: 13 -> 16; matrix products, arithmetic and copies ran while one was open for 1% -> 1% of each run, Pallas kernels for 9% -> 9%
where the time goes in v2:
time: 72.9 us; the launch traced here: 72.5 us
  starting transfers between devices  46.6 us (64%)
  waiting for transfers between devices  16.3 us (22%)
  Pallas kernels  7.39 us (10%)
  between operations  1.13 us (2%)
  other arithmetic  0.98 us (1%)
    ppermute x36, starting transfers between devices, exchange(): return lax.ppermute(value, axes, pairs)  46.6 us
    ppermute x36, waiting for transfers between devices, exchange(): return lax.ppermute(value, axes, pairs)  16.3 us
    pallas_call x1, Pallas kernels, spread(): pl.pallas_call(functools.partial(first_spread_kernel, outputs=groups, lay...  4.68 us
    pallas_call x4, Pallas kernels, meet(): pl.pallas_call(functools.partial(meet_kernel, first=first, blocks=len(gro...  1.82 us
  transfers between devices with their start and end apart: 36, of which 16 were waited for; matrix products, arithmetic and copies ran while one was open for 1% of the time, Pallas kernels for 9%

profile of v2, /device:TPU:0, one launch (start us, length us, event | category | flops | bytes accessed | tf_op | source)
XLA Modules:
  0.0 72.5 jit_solution(17721162169136430472)
XLA Ops:
  0.6 4.6 %collective-permute-start = (bf16[1,64,512]{2,1,0:T(8,128)(2,1)}, bf16[1,64,512]{2,1,0:T(8,128)(2,1)S(1)}, u32[]{:S(2)}, u32[]{:S(2)}) collective-permute-start(bf16[1,64,512]{2,1,0:T(8,128)(2,1)} %bitcast.30), channel_id=1, source_target_pairs={{0,28},{1,29},{2,30},{3,31},{4,24},{5,25},{6,26},{7,27},{8,20},{9,... | collective-permute-start | bytes 196616 | tf_op jit(solution)/shard_map/ppermute | solution.py:41
  6.1 4.7 %first_spread.1 = (bf16[4,64,512]{2,1,0:T(8,128)(2,1)S(1)}, bf16[4,64,512]{2,1,0:T(8,128)(2,1)S(1)}, bf16[4,64,512]{2,1,0:T(8,128)(2,1)S(1)}, bf16[4,64,512]{2,1,0:T(8,128)(2,1)S(1)}) custom-call(bf16[64,512]{1,0:T(8,128)(2,1)} %bitcast.33, bf16[1,512,8192]{2,1,0:T(8,128)(2,1)} %weight.13), custom_call_target="tpu_custom_call" | custom-call | tf_op jit(solution)/shard_map/first_spread/pallas_call | solution.py:129
  10.8 1.3 %collective-permute-start.3 = (bf16[4,64,512]{2,1,0:T(8,128)(2,1)S(1)}, bf16[4,64,512]{2,1,0:T(8,128)(2,1)S(1)}, u32[]{:S(2)}, u32[]{:S(2)}) collective-permute-start(bf16[4,64,512]{2,1,0:T(8,128)(2,1)S(1)} %get-tuple-element.37), channel_id=1, source_target_pairs={{0,19},{1,18},{2,17},{3,16},{4,23},{5,22},{6,21},{7,20},{8,27},{9,... | collective-permute-start | bytes 786440 | tf_op jit(solution)/shard_map/ppermute | solution.py:41
  12.1 1.3 %collective-permute-start.7 = (bf16[4,64,512]{2,1,0:T(8,128)(2,1)S(1)}, bf16[4,64,512]{2,1,0:T(8,128)(2,1)S(1)}, u32[]{:S(2)}, u32[]{:S(2)}) collective-permute-start(bf16[4,64,512]{2,1,0:T(8,128)(2,1)S(1)} %get-tuple-element.43), channel_id=1, source_target_pairs={{0,18},{1,19},{2,16},{3,17},{4,22},{5,23},{6,20},{7,21},{8,26},{9,... | collective-permute-start | bytes 786440 | tf_op jit(solution)/shard_map/ppermute | solution.py:41
  13.5 1.3 %collective-permute-start.8 = (bf16[4,64,512]{2,1,0:T(8,128)(2,1)S(1)}, bf16[4,64,512]{2,1,0:T(8,128)(2,1)S(1)}, u32[]{:S(2)}, u32[]{:S(2)}) collective-permute-start(bf16[4,64,512]{2,1,0:T(8,128)(2,1)S(1)} %get-tuple-element.44), channel_id=1, source_target_pairs={{0,17},{1,16},{2,19},{3,18},{4,21},{5,20},{6,23},{7,22},{8,25},{9,... | collective-permute-start | bytes 786440 | tf_op jit(solution)/shard_map/ppermute | solution.py:41
  17.3 1.3 %collective-permute-start.4 = (bf16[4,64,512]{2,1,0:T(8,128)(2,1)S(1)}, bf16[4,64,512]{2,1,0:T(8,128)(2,1)S(1)}, u32[]{:S(2)}, u32[]{:S(2)}) collective-permute-start(bf16[4,64,512]{2,1,0:T(8,128)(2,1)S(1)} %pad_maximum_fusion.rest_0_), channel_id=1, source_target_pairs={{16,2},{17,3},{18,0},{19,1},{20,6},{21,7},{22,4},{23,5},{24,10},{2... | collective-permute-start | bytes 786440 | tf_op jit(solution)/shard_map/ppermute | solution.py:41
  21.2 1.3 %collective-permute-start.10 = (bf16[1,64,512]{2,1,0:T(8,128)(2,1)S(1)}, bf16[1,64,512]{2,1,0:T(8,128)(2,1)S(1)}, u32[]{:S(2)}, u32[]{:S(2)}) collective-permute-start(bf16[1,64,512]{2,1,0:T(8,128)(2,1)S(1)} %get-tuple-element.66), channel_id=1, source_target_pairs={{16,12},{17,13},{18,14},{19,15},{20,8},{21,9},{22,10},{23,11},{24,... | collective-permute-start | bytes 196616 | tf_op jit(solution)/shard_map/ppermute | solution.py:41
  22.5 1.3 %collective-permute-start.11 = (bf16[1,64,512]{2,1,0:T(8,128)(2,1)S(1)}, bf16[1,64,512]{2,1,0:T(8,128)(2,1)S(1)}, u32[]{:S(2)}, u32[]{:S(2)}) collective-permute-start(bf16[1,64,512]{2,1,0:T(8,128)(2,1)S(1)} %get-tuple-element.69), channel_id=1, source_target_pairs={{16,8},{17,9},{18,10},{19,11},{20,12},{21,13},{22,14},{23,15},{24,... | collective-permute-start | bytes 196616 | tf_op jit(solution)/shard_map/ppermute | solution.py:41
  24.3 1.5 %collective-permute-start.12 = (bf16[1,64,512]{2,1,0:T(8,128)(2,1)S(1)}, bf16[1,64,512]{2,1,0:T(8,128)(2,1)S(1)}, u32[]{:S(2)}, u32[]{:S(2)}) collective-permute-start(bf16[1,64,512]{2,1,0:T(8,128)(2,1)S(1)} %get-tuple-element.68), channel_id=1, source_target_pairs={{16,4},{17,5},{18,6},{19,7},{20,0},{21,1},{22,2},{23,3},{24,12},{2... | collective-permute-start | bytes 196616 | tf_op jit(solution)/shard_map/ppermute | solution.py:41
  26.7 2.1 %collective-permute-done.4.rest_0_ = bf16[4,64,512]{2,1,0:T(8,128)(2,1)S(1)} collective-permute-done((bf16[4,64,512]{2,1,0:T(8,128)(2,1)S(1)}, bf16[4,64,512]{2,1,0:T(8,128)(2,1)S(1)}, u32[]{:S(2)}, u32[]{:S(2)}) %collective-permute-start.4) | collective-permute-done | bytes 262176 | tf_op jit(solution)/shard_map/ppermute | solution.py:41
  32.8 1.7 %collective-permute-start.15 = (bf16[1,64,512]{2,1,0:T(8,128)(2,1)S(1)}, bf16[1,64,512]{2,1,0:T(8,128)(2,1)S(1)}, u32[]{:S(2)}, u32[]{:S(2)}) collective-permute-start(bf16[1,64,512]{2,1,0:T(8,128)(2,1)S(1)} %bitcast.26), channel_id=1, source_target_pairs={{16,12},{17,13},{18,14},{19,15},{20,8},{21,9},{22,10},{23,11},{24,... | collective-permute-start | bytes 196616 | tf_op jit(solution)/shard_map/ppermute | solution.py:41
  36.8 1.3 %collective-permute-start.21 = (bf16[4,64,512]{2,1,0:T(8,128)(2,1)S(1)}, bf16[4,64,512]{2,1,0:T(8,128)(2,1)S(1)}, u32[]{:S(2)}, u32[]{:S(2)}) collective-permute-start(bf16[4,64,512]{2,1,0:T(8,128)(2,1)S(1)} %get-tuple-element.55), channel_id=1, source_target_pairs={{16,3},{17,2},{18,1},{19,0},{20,7},{21,6},{22,5},{23,4},{24,11},{2... | collective-permute-start | bytes 786440 | tf_op jit(solution)/shard_map/ppermute | solution.py:41
  38.1 1.3 %collective-permute-start.22 = (bf16[4,64,512]{2,1,0:T(8,128)(2,1)S(1)}, bf16[4,64,512]{2,1,0:T(8,128)(2,1)S(1)}, u32[]{:S(2)}, u32[]{:S(2)}) collective-permute-start(bf16[4,64,512]{2,1,0:T(8,128)(2,1)S(1)} %get-tuple-element.56), channel_id=1, source_target_pairs={{16,2},{17,3},{18,0},{19,1},{20,6},{21,7},{22,4},{23,5},{24,10},{2... | collective-permute-start | bytes 786440 | tf_op jit(solution)/shard_map/ppermute | solution.py:41
  40.7 1.4 %collective-permute-done.16 = bf16[1,64,512]{2,1,0:T(8,128)(2,1)S(1)} collective-permute-done((bf16[1,64,512]{2,1,0:T(8,128)(2,1)S(1)}, bf16[1,64,512]{2,1,0:T(8,128)(2,1)S(1)}, u32[]{:S(2)}, u32[]{:S(2)}) %collective-permute-start.16) | collective-permute-done | bytes 65568 | tf_op jit(solution)/shard_map/ppermute | solution.py:41
  43.1 3.0 %collective-permute-start.20 = (bf16[4,64,512]{2,1,0:T(8,128)(2,1)S(1)}, bf16[4,64,512]{2,1,0:T(8,128)(2,1)S(1)}, u32[]{:S(2)}, u32[]{:S(2)}) collective-permute-start(bf16[4,64,512]{2,1,0:T(8,128)(2,1)S(1)} %constant_dynamic-update-slice_fusion.rest_0_), channel_id=1, source_target_pairs={{0,17},{1,16},{2,19},{3,18},{4,21},{5,20},{6,23},{7,22},{8,25},{9,... | collective-permute-start | bytes 786440 | tf_op jit(solution)/shard_map/ppermute | solution.py:41
  46.2 1.3 %collective-permute-start.18 = (bf16[4,64,512]{2,1,0:T(8,128)(2,1)S(1)}, bf16[4,64,512]{2,1,0:T(8,128)(2,1)S(1)}, u32[]{:S(2)}, u32[]{:S(2)}) collective-permute-start(bf16[4,64,512]{2,1,0:T(8,128)(2,1)S(1)} %constant_dynamic-update-slice_fusion.rest_0_), channel_id=1, source_target_pairs={{0,18},{1,19},{2,16},{3,17},{4,22},{5,23},{6,20},{7,21},{8,26},{9,... | collective-permute-start | bytes 786440 | tf_op jit(solution)/shard_map/ppermute | solution.py:41
  48.2 2.0 %collective-permute-start.19 = (bf16[4,64,512]{2,1,0:T(8,128)(2,1)S(1)}, bf16[4,64,512]{2,1,0:T(8,128)(2,1)S(1)}, u32[]{:S(2)}, u32[]{:S(2)}) collective-permute-start(bf16[4,64,512]{2,1,0:T(8,128)(2,1)S(1)} %constant_dynamic-update-slice_fusion.rest_0_), channel_id=1, source_target_pairs={{0,19},{1,18},{2,17},{3,16},{4,23},{5,22},{6,21},{7,20},{8,27},{9,... | collective-permute-start | bytes 786440 | tf_op jit(solution)/shard_map/ppermute | solution.py:41
  50.4 1.7 %collective-permute-start.25 = (bf16[1,64,512]{2,1,0:T(8,128)(2,1)S(1)}, bf16[1,64,512]{2,1,0:T(8,128)(2,1)S(1)}, u32[]{:S(2)}, u32[]{:S(2)}) collective-permute-start(bf16[1,64,512]{2,1,0:T(8,128)(2,1)S(1)} %get-tuple-element.62), channel_id=1, source_target_pairs={{0,28},{1,29},{2,30},{3,31},{4,24},{5,25},{6,26},{7,27},{8,20},{9,... | collective-permute-start | bytes 196616 | tf_op jit(solution)/shard_map/ppermute | solution.py:41
  52.1 1.3 %collective-permute-start.26 = (bf16[1,64,512]{2,1,0:T(8,128)(2,1)S(1)}, bf16[1,64,512]{2,1,0:T(8,128)(2,1)S(1)}, u32[]{:S(2)}, u32[]{:S(2)}) collective-permute-start(bf16[1,64,512]{2,1,0:T(8,128)(2,1)S(1)} %get-tuple-element.65), channel_id=1, source_target_pairs={{0,24},{1,25},{2,26},{3,27},{4,28},{5,29},{6,30},{7,31},{8,16},{9,... | collective-permute-start | bytes 196616 | tf_op jit(solution)/shard_map/ppermute | solution.py:41
  53.5 1.4 %collective-permute-start.27 = (bf16[1,64,512]{2,1,0:T(8,128)(2,1)S(1)}, bf16[1,64,512]{2,1,0:T(8,128)(2,1)S(1)}, u32[]{:S(2)}, u32[]{:S(2)}) collective-permute-start(bf16[1,64,512]{2,1,0:T(8,128)(2,1)S(1)} %get-tuple-element.64), channel_id=1, source_target_pairs={{0,20},{1,21},{2,22},{3,23},{4,16},{5,17},{6,18},{7,19},{8,28},{9,... | collective-permute-start | bytes 196616 | tf_op jit(solution)/shard_map/ppermute | solution.py:41
  55.3 1.5 %collective-permute-done.27 = bf16[1,64,512]{2,1,0:T(8,128)(2,1)S(1)} collective-permute-done((bf16[1,64,512]{2,1,0:T(8,128)(2,1)S(1)}, bf16[1,64,512]{2,1,0:T(8,128)(2,1)S(1)}, u32[]{:S(2)}, u32[]{:S(2)}) %collective-permute-start.27) | collective-permute-done | bytes 65568 | tf_op jit(solution)/shard_map/ppermute | solution.py:41
  58.8 1.4 %collective-permute-start.30 = (bf16[32,256]{1,0:T(8,128)(2,1)S(1)}, bf16[32,256]{1,0:T(8,128)(2,1)S(1)}, u32[]{:S(2)}, u32[]{:S(2)}) collective-permute-start(bf16[32,256]{1,0:T(8,128)(2,1)S(1)} %add_convert_fusion.3), channel_id=1, source_target_pairs={{0,3},{1,2},{2,1},{3,0},{4,7},{5,6},{6,5},{7,4},{8,11},{9,10},{10,... | collective-permute-start | bytes 49160 | tf_op jit(solution)/shard_map/ppermute | solution.py:41
  65.0 1.9 %collective-permute-start.33 = (bf16[32,256]{1,0:T(8,128)(2,1)S(1)}, bf16[32,256]{1,0:T(8,128)(2,1)S(1)}, u32[]{:S(2)}, u32[]{:S(2)}) collective-permute-start(bf16[32,256]{1,0:T(8,128)(2,1)S(1)} %add_convert_fusion.2.refs_3_), channel_id=1, source_target_pairs={{0,12},{1,13},{2,14},{3,15},{4,8},{5,9},{6,10},{7,11},{8,4},{9,5},... | collective-permute-start | bytes 49160 | tf_op jit(solution)/shard_map/ppermute | solution.py:41
  68.0 1.5 %collective-permute-start.35 = (bf16[32,256]{1,0:T(8,128)(2,1)S(1)}, bf16[32,256]{1,0:T(8,128)(2,1)S(1)}, u32[]{:S(2)}, u32[]{:S(2)}) collective-permute-start(bf16[32,256]{1,0:T(8,128)(2,1)S(1)} %add_convert_fusion.2.refs_3_), channel_id=1, source_target_pairs={{0,4},{1,5},{2,6},{3,7},{4,0},{5,1},{6,2},{7,3},{8,12},{9,13},{10,... | collective-permute-start | bytes 49160 | tf_op jit(solution)/shard_map/ppermute | solution.py:41
  (90 shorter events, 27.9 us)
Async XLA Ops:
  0.6 12.8 %collective-permute-start = (bf16[1,64,512]{2,1,0:T(8,128)(2,1)}, bf16[1,64,512]{2,1,0:T(8,128)(2,1)S(1)}, u32[]{:S(2)}, u32[]{:S(2)}) collective-permute-start(bf16[1,64,512]{2,1,0:T(8,128)(2,1)} %bitcast.30), channel_id=1, source_target_pairs={{0,28},{1,29},{2,30},{3,31},{4,24},{5,25},{6,26},{7,27},{8,20},{9,... | collective-permute-start | bytes 196616 | tf_op jit(solution)/shard_map/ppermute | solution.py:41
  5.2 9.6 %collective-permute-start.1 = (bf16[1,64,512]{2,1,0:T(8,128)(2,1)}, bf16[1,64,512]{2,1,0:T(8,128)(2,1)S(1)}, u32[]{:S(2)}, u32[]{:S(2)}) collective-permute-start(bf16[1,64,512]{2,1,0:T(8,128)(2,1)} %bitcast.31), channel_id=1, source_target_pairs={{0,24},{1,25},{2,26},{3,27},{4,28},{5,29},{6,30},{7,31},{8,16},{9,... | collective-permute-start | bytes 196616 | tf_op jit(solution)/shard_map/ppermute | solution.py:41
  5.2 9.6 %collective-permute-start.2 = (bf16[1,64,512]{2,1,0:T(8,128)(2,1)}, bf16[1,64,512]{2,1,0:T(8,128)(2,1)S(1)}, u32[]{:S(2)}, u32[]{:S(2)}) collective-permute-start(bf16[1,64,512]{2,1,0:T(8,128)(2,1)} %bitcast.32), channel_id=1, source_target_pairs={{0,20},{1,21},{2,22},{3,23},{4,16},{5,17},{6,18},{7,19},{8,28},{9,... | collective-permute-start | bytes 196616 | tf_op jit(solution)/shard_map/ppermute | solution.py:41
  10.8 5.2 %collective-permute-start.3 = (bf16[4,64,512]{2,1,0:T(8,128)(2,1)S(1)}, bf16[4,64,512]{2,1,0:T(8,128)(2,1)S(1)}, u32[]{:S(2)}, u32[]{:S(2)}) collective-permute-start(bf16[4,64,512]{2,1,0:T(8,128)(2,1)S(1)} %get-tuple-element.37), channel_id=1, source_target_pairs={{0,19},{1,18},{2,17},{3,16},{4,23},{5,22},{6,21},{7,20},{8,27},{9,... | collective-permute-start | bytes 786440 | tf_op jit(solution)/shard_map/ppermute | solution.py:41
  12.1 7.6 %collective-permute-start.7 = (bf16[4,64,512]{2,1,0:T(8,128)(2,1)S(1)}, bf16[4,64,512]{2,1,0:T(8,128)(2,1)S(1)}, u32[]{:S(2)}, u32[]{:S(2)}) collective-permute-start(bf16[4,64,512]{2,1,0:T(8,128)(2,1)S(1)} %get-tuple-element.43), channel_id=1, source_target_pairs={{0,18},{1,19},{2,16},{3,17},{4,22},{5,23},{6,20},{7,21},{8,26},{9,... | collective-permute-start | bytes 786440 | tf_op jit(solution)/shard_map/ppermute | solution.py:41
  13.5 7.6 %collective-permute-start.8 = (bf16[4,64,512]{2,1,0:T(8,128)(2,1)S(1)}, bf16[4,64,512]{2,1,0:T(8,128)(2,1)S(1)}, u32[]{:S(2)}, u32[]{:S(2)}) collective-permute-start(bf16[4,64,512]{2,1,0:T(8,128)(2,1)S(1)} %get-tuple-element.44), channel_id=1, source_target_pairs={{0,17},{1,16},{2,19},{3,18},{4,21},{5,20},{6,23},{7,22},{8,25},{9,... | collective-permute-start | bytes 786440 | tf_op jit(solution)/shard_map/ppermute | solution.py:41
  14.8 6.2 %collective-permute-start.9 = (bf16[4,64,512]{2,1,0:T(8,128)(2,1)S(1)}, bf16[4,64,512]{2,1,0:T(8,128)(2,1)S(1)}, u32[]{:S(2)}, u32[]{:S(2)}) collective-permute-start(bf16[4,64,512]{2,1,0:T(8,128)(2,1)S(1)} %get-tuple-element.45), channel_id=1, source_target_pairs={{0,16},{1,17},{2,18},{3,19},{4,20},{5,21},{6,22},{7,23},{8,24},{9,... | collective-permute-start | bytes 786440 | tf_op jit(solution)/shard_map/ppermute | solution.py:41
  16.0 8.3 %collective-permute-start.6 = (bf16[4,64,512]{2,1,0:T(8,128)(2,1)S(1)}, bf16[4,64,512]{2,1,0:T(8,128)(2,1)S(1)}, u32[]{:S(2)}, u32[]{:S(2)}) collective-permute-start(bf16[4,64,512]{2,1,0:T(8,128)(2,1)S(1)} %pad_maximum_fusion.rest_0_), channel_id=1, source_target_pairs={{16,1},{17,0},{18,3},{19,2},{20,5},{21,4},{22,7},{23,6},{24,9},{25... | collective-permute-start | bytes 786440 | tf_op jit(solution)/shard_map/ppermute | solution.py:41
  17.3 11.5 %collective-permute-start.4 = (bf16[4,64,512]{2,1,0:T(8,128)(2,1)S(1)}, bf16[4,64,512]{2,1,0:T(8,128)(2,1)S(1)}, u32[]{:S(2)}, u32[]{:S(2)}) collective-permute-start(bf16[4,64,512]{2,1,0:T(8,128)(2,1)S(1)} %pad_maximum_fusion.rest_0_), channel_id=1, source_target_pairs={{16,2},{17,3},{18,0},{19,1},{20,6},{21,7},{22,4},{23,5},{24,10},{2... | collective-permute-start | bytes 786440 | tf_op jit(solution)/shard_map/ppermute | solution.py:41
  19.7 9.7 %collective-permute-start.5 = (bf16[4,64,512]{2,1,0:T(8,128)(2,1)S(1)}, bf16[4,64,512]{2,1,0:T(8,128)(2,1)S(1)}, u32[]{:S(2)}, u32[]{:S(2)}) collective-permute-start(bf16[4,64,512]{2,1,0:T(8,128)(2,1)S(1)} %pad_maximum_fusion.rest_0_), channel_id=1, source_target_pairs={{16,3},{17,2},{18,1},{19,0},{20,7},{21,6},{22,5},{23,4},{24,11},{2... | collective-permute-start | bytes 786440 | tf_op jit(solution)/shard_map/ppermute | solution.py:41
  21.2 9.4 %collective-permute-start.10 = (bf16[1,64,512]{2,1,0:T(8,128)(2,1)S(1)}, bf16[1,64,512]{2,1,0:T(8,128)(2,1)S(1)}, u32[]{:S(2)}, u32[]{:S(2)}) collective-permute-start(bf16[1,64,512]{2,1,0:T(8,128)(2,1)S(1)} %get-tuple-element.66), channel_id=1, source_target_pairs={{16,12},{17,13},{18,14},{19,15},{20,8},{21,9},{22,10},{23,11},{24,... | collective-permute-start | bytes 196616 | tf_op jit(solution)/shard_map/ppermute | solution.py:41
  22.5 8.1 %collective-permute-start.11 = (bf16[1,64,512]{2,1,0:T(8,128)(2,1)S(1)}, bf16[1,64,512]{2,1,0:T(8,128)(2,1)S(1)}, u32[]{:S(2)}, u32[]{:S(2)}) collective-permute-start(bf16[1,64,512]{2,1,0:T(8,128)(2,1)S(1)} %get-tuple-element.69), channel_id=1, source_target_pairs={{16,8},{17,9},{18,10},{19,11},{20,12},{21,13},{22,14},{23,15},{24,... | collective-permute-start | bytes 196616 | tf_op jit(solution)/shard_map/ppermute | solution.py:41
  24.3 7.1 %collective-permute-start.12 = (bf16[1,64,512]{2,1,0:T(8,128)(2,1)S(1)}, bf16[1,64,512]{2,1,0:T(8,128)(2,1)S(1)}, u32[]{:S(2)}, u32[]{:S(2)}) collective-permute-start(bf16[1,64,512]{2,1,0:T(8,128)(2,1)S(1)} %get-tuple-element.68), channel_id=1, source_target_pairs={{16,4},{17,5},{18,6},{19,7},{20,0},{21,1},{22,2},{23,3},{24,12},{2... | collective-permute-start | bytes 196616 | tf_op jit(solution)/shard_map/ppermute | solution.py:41
  32.8 6.5 %collective-permute-start.15 = (bf16[1,64,512]{2,1,0:T(8,128)(2,1)S(1)}, bf16[1,64,512]{2,1,0:T(8,128)(2,1)S(1)}, u32[]{:S(2)}, u32[]{:S(2)}) collective-permute-start(bf16[1,64,512]{2,1,0:T(8,128)(2,1)S(1)} %bitcast.26), channel_id=1, source_target_pairs={{16,12},{17,13},{18,14},{19,15},{20,8},{21,9},{22,10},{23,11},{24,... | collective-permute-start | bytes 196616 | tf_op jit(solution)/shard_map/ppermute | solution.py:41
  34.6 7.5 %collective-permute-start.16 = (bf16[1,64,512]{2,1,0:T(8,128)(2,1)S(1)}, bf16[1,64,512]{2,1,0:T(8,128)(2,1)S(1)}, u32[]{:S(2)}, u32[]{:S(2)}) collective-permute-start(bf16[1,64,512]{2,1,0:T(8,128)(2,1)S(1)} %bitcast.27), channel_id=1, source_target_pairs={{16,8},{17,9},{18,10},{19,11},{20,12},{21,13},{22,14},{23,15},{24,... | collective-permute-start | bytes 196616 | tf_op jit(solution)/shard_map/ppermute | solution.py:41
  35.6 6.5 %collective-permute-start.17 = (bf16[1,64,512]{2,1,0:T(8,128)(2,1)S(1)}, bf16[1,64,512]{2,1,0:T(8,128)(2,1)S(1)}, u32[]{:S(2)}, u32[]{:S(2)}) collective-permute-start(bf16[1,64,512]{2,1,0:T(8,128)(2,1)S(1)} %bitcast.28), channel_id=1, source_target_pairs={{16,4},{17,5},{18,6},{19,7},{20,0},{21,1},{22,2},{23,3},{24,12},{2... | collective-permute-start | bytes 196616 | tf_op jit(solution)/shard_map/ppermute | solution.py:41
  36.8 9.4 %collective-permute-start.21 = (bf16[4,64,512]{2,1,0:T(8,128)(2,1)S(1)}, bf16[4,64,512]{2,1,0:T(8,128)(2,1)S(1)}, u32[]{:S(2)}, u32[]{:S(2)}) collective-permute-start(bf16[4,64,512]{2,1,0:T(8,128)(2,1)S(1)} %get-tuple-element.55), channel_id=1, source_target_pairs={{16,3},{17,2},{18,1},{19,0},{20,7},{21,6},{22,5},{23,4},{24,11},{2... | collective-permute-start | bytes 786440 | tf_op jit(solution)/shard_map/ppermute | solution.py:41
  38.1 10.1 %collective-permute-start.22 = (bf16[4,64,512]{2,1,0:T(8,128)(2,1)S(1)}, bf16[4,64,512]{2,1,0:T(8,128)(2,1)S(1)}, u32[]{:S(2)}, u32[]{:S(2)}) collective-permute-start(bf16[4,64,512]{2,1,0:T(8,128)(2,1)S(1)} %get-tuple-element.56), channel_id=1, source_target_pairs={{16,2},{17,3},{18,0},{19,1},{20,6},{21,7},{22,4},{23,5},{24,10},{2... | collective-permute-start | bytes 786440 | tf_op jit(solution)/shard_map/ppermute | solution.py:41
  39.4 10.8 %collective-permute-start.23 = (bf16[4,64,512]{2,1,0:T(8,128)(2,1)S(1)}, bf16[4,64,512]{2,1,0:T(8,128)(2,1)S(1)}, u32[]{:S(2)}, u32[]{:S(2)}) collective-permute-start(bf16[4,64,512]{2,1,0:T(8,128)(2,1)S(1)} %get-tuple-element.57), channel_id=1, source_target_pairs={{16,1},{17,0},{18,3},{19,2},{20,5},{21,4},{22,7},{23,6},{24,9},{25... | collective-permute-start | bytes 786440 | tf_op jit(solution)/shard_map/ppermute | solution.py:41
  42.1 8.2 %collective-permute-start.24 = (bf16[4,64,512]{2,1,0:T(8,128)(2,1)S(1)}, bf16[4,64,512]{2,1,0:T(8,128)(2,1)S(1)}, u32[]{:S(2)}, u32[]{:S(2)}) collective-permute-start(bf16[4,64,512]{2,1,0:T(8,128)(2,1)S(1)} %get-tuple-element.58), channel_id=1, source_target_pairs={{16,0},{17,1},{18,2},{19,3},{20,4},{21,5},{22,6},{23,7},{24,8},{25... | collective-permute-start | bytes 786440 | tf_op jit(solution)/shard_map/ppermute | solution.py:41
  43.1 10.3 %collective-permute-start.20 = (bf16[4,64,512]{2,1,0:T(8,128)(2,1)S(1)}, bf16[4,64,512]{2,1,0:T(8,128)(2,1)S(1)}, u32[]{:S(2)}, u32[]{:S(2)}) collective-permute-start(bf16[4,64,512]{2,1,0:T(8,128)(2,1)S(1)} %constant_dynamic-update-slice_fusion.rest_0_), channel_id=1, source_target_pairs={{0,17},{1,16},{2,19},{3,18},{4,21},{5,20},{6,23},{7,22},{8,25},{9,... | collective-permute-start | bytes 786440 | tf_op jit(solution)/shard_map/ppermute | solution.py:41
  46.2 8.8 %collective-permute-start.18 = (bf16[4,64,512]{2,1,0:T(8,128)(2,1)S(1)}, bf16[4,64,512]{2,1,0:T(8,128)(2,1)S(1)}, u32[]{:S(2)}, u32[]{:S(2)}) collective-permute-start(bf16[4,64,512]{2,1,0:T(8,128)(2,1)S(1)} %constant_dynamic-update-slice_fusion.rest_0_), channel_id=1, source_target_pairs={{0,18},{1,19},{2,16},{3,17},{4,22},{5,23},{6,20},{7,21},{8,26},{9,... | collective-permute-start | bytes 786440 | tf_op jit(solution)/shard_map/ppermute | solution.py:41
  48.2 6.8 %collective-permute-start.19 = (bf16[4,64,512]{2,1,0:T(8,128)(2,1)S(1)}, bf16[4,64,512]{2,1,0:T(8,128)(2,1)S(1)}, u32[]{:S(2)}, u32[]{:S(2)}) collective-permute-start(bf16[4,64,512]{2,1,0:T(8,128)(2,1)S(1)} %constant_dynamic-update-slice_fusion.rest_0_), channel_id=1, source_target_pairs={{0,19},{1,18},{2,17},{3,16},{4,23},{5,22},{6,21},{7,20},{8,27},{9,... | collective-permute-start | bytes 786440 | tf_op jit(solution)/shard_map/ppermute | solution.py:41
  65.0 5.6 %collective-permute-start.33 = (bf16[32,256]{1,0:T(8,128)(2,1)S(1)}, bf16[32,256]{1,0:T(8,128)(2,1)S(1)}, u32[]{:S(2)}, u32[]{:S(2)}) collective-permute-start(bf16[32,256]{1,0:T(8,128)(2,1)S(1)} %add_convert_fusion.2.refs_3_), channel_id=1, source_target_pairs={{0,12},{1,13},{2,14},{3,15},{4,8},{5,9},{6,10},{7,11},{8,4},{9,5},... | collective-permute-start | bytes 49160 | tf_op jit(solution)/shard_map/ppermute | solution.py:41
  (19 other events, 138.7 us)

commit v3 on v2

--- a/solution.py
+++ b/solution.py
@@ -146,6 +146,36 @@
     )
 
 
+def mix_kernel(*rest, groups, layer):
+    parts, blocks, outs = rest[:groups], rest[groups:-groups], rest[-groups:]
+    inside = lax.axis_index("section") == layer
+
+    @pl.when(inside)
+    def _():
+        for part, out in zip(parts, outs):
+            out[...] = part[...]
+
+    @pl.when(jnp.logical_not(inside))
+    def _():
+        start = 0
+        for block in blocks:
+            for out in outs:
+                out[start : start + block.shape[0]] = block[...]
+            start += block.shape[0]
+
+
+def mix(parts, blocks, layer):
+    vmem = pl.BlockSpec(memory_space=pltpu.VMEM)
+    return pl.pallas_call(
+        functools.partial(mix_kernel, groups=len(parts), layer=layer),
+        out_shape=[jax.ShapeDtypeStruct(part.shape, part.dtype) for part in parts],
+        in_specs=[vmem] * (len(parts) + len(blocks)),
+        out_specs=[vmem] * len(parts),
+        compiler_params=pltpu.CompilerParams(vmem_limit_bytes=8 * 2**20),
+        name="mix",
+    )(*parts, *blocks)
+
+
 def meet_kernel(weight, *rest, first, blocks, layer, digits, names):
     inputs, before, (total, square) = rest[:blocks], rest[blocks:-2], rest[-2:]
     share, _, depth = inputs[0].shape
@@ -268,19 +298,26 @@
             final = number == rounds - 1
             if final:
                 at = layer if number % 2 == 0 else helper
-                sent = []
+                sent, shared = [], None
                 for step, one in zip(scatter_steps(radix, True), parts):
-                    if step > 0 or at != layer:
+                    if step == 1 and at != layer:
+                        (one,) = mix([one], [stack], layer)
+                        one = shared = send(one, routes=both, radix=radix, stride=stride, step=step)
+                    elif step > 0 or at != layer:
                         routes = both if step == 0 else [(layer, at)]
                         one = send(one, routes=routes, radix=radix, stride=stride, step=step)
                     sent.append(one)
                 if layer == 0 and rounds > 1:
                     stack, sent[:1] = lax.optimization_barrier((stack, sent[:1]))
             routes = [(helper, layer)] if final else both
-            gathered = [
-                stack if step == 0 else send(stack, routes=routes, radix=radix, stride=stride, step=step)
-                for step in gather_steps(radix, final)
-            ]
+            gathered = []
+            for step in gather_steps(radix, final):
+                if step == 0:
+                    gathered.append(stack)
+                elif final and step == 1 and shared is not None:
+                    gathered.append(shared)
+                else:
+                    gathered.append(send(stack, routes=routes, radix=radix, stride=stride, step=step))
             if not final:
                 gathered, parts[-1:] = lax.optimization_barrier((gathered, parts[-1:]))
                 stack = jnp.concatenate(gathered, axis=0)
@@ -293,10 +330,12 @@
             for i, step in enumerate(scatter_steps(radix, False)):
                 one = wide[i * part : (i + 1) * part].astype(jnp.bfloat16)
                 if step > 0 or to != at:
-                    routes = both if step == 0 else [(at, to)]
+                    routes = both if step <= 1 and to != at else [(at, to)]
                     one = send(one, routes=routes, radix=radix, stride=stride, step=step)
                 sent.append(one)
             at = to
+            if layer == 0:
+                sent = sent[-1:] + sent[:-1]
             wide = functools.reduce(jnp.add, [one.astype(jnp.float32) for one in sent])
 
         before = []

time: 72.9 us -> 77.7 us (1.066)
  waiting for transfers between devices: 16.3 us -> 20.1 us
  starting transfers between devices: 46.6 us -> 47.7 us
    ppermute x36 -> x34, waiting for transfers between devices: 16.3 us -> 20.1 us  [exchange(): return lax.ppermute(value, axes, pairs)]
    ppermute x36 -> x34, starting transfers between devices: 46.6 us -> 47.7 us  [exchange(): return lax.ppermute(value, axes, pairs)]
  transfers between devices with their start and end apart: 36 -> 34, of which waited for: 16 -> 16; matrix products, arithmetic and copies ran while one was open for 1% -> 1% of each run, Pallas kernels for 9% -> 8%
where the time goes in v3:
time: 77.7 us; the launch traced here: 77.3 us
  starting transfers between devices  47.7 us (61%)
  waiting for transfers between devices  20.1 us (26%)
  Pallas kernels  7.42 us (10%)
  between operations  1.1 us (1%)
  other arithmetic  0.94 us (1%)
    ppermute x34, starting transfers between devices, exchange(): return lax.ppermute(value, axes, pairs)  47.7 us
    ppermute x34, waiting for transfers between devices, exchange(): return lax.ppermute(value, axes, pairs)  20.1 us
    pallas_call x1, Pallas kernels, spread(): pl.pallas_call(functools.partial(first_spread_kernel, outputs=groups, lay...  4.68 us
    pallas_call x4, Pallas kernels, meet(): pl.pallas_call(functools.partial(meet_kernel, first=first, blocks=len(gro...  1.79 us
  transfers between devices with their start and end apart: 34, of which 16 were waited for; matrix products, arithmetic and copies ran while one was open for 1% of the time, Pallas kernels for 8%

profile of v3, /device:TPU:0, one launch (start us, length us, event | category | flops | bytes accessed | tf_op | source)
XLA Modules:
  0.0 77.3 jit_solution(8682878538022000748)
XLA Ops:
  0.6 4.6 %collective-permute-start = (bf16[1,64,512]{2,1,0:T(8,128)(2,1)}, bf16[1,64,512]{2,1,0:T(8,128)(2,1)S(1)}, u32[]{:S(2)}, u32[]{:S(2)}) collective-permute-start(bf16[1,64,512]{2,1,0:T(8,128)(2,1)} %bitcast.30), channel_id=1, source_target_pairs={{0,28},{1,29},{2,30},{3,31},{4,24},{5,25},{6,26},{7,27},{8,20},{9,... | collective-permute-start | bytes 196616 | tf_op jit(solution)/shard_map/ppermute | solution.py:41
  6.1 4.7 %first_spread.1 = (bf16[4,64,512]{2,1,0:T(8,128)(2,1)S(1)}, bf16[4,64,512]{2,1,0:T(8,128)(2,1)S(1)}, bf16[4,64,512]{2,1,0:T(8,128)(2,1)S(1)}, bf16[4,64,512]{2,1,0:T(8,128)(2,1)S(1)}) custom-call(bf16[64,512]{1,0:T(8,128)(2,1)} %bitcast.33, bf16[1,512,8192]{2,1,0:T(8,128)(2,1)} %weight.13), custom_call_target="tpu_custom_call" | custom-call | tf_op jit(solution)/shard_map/first_spread/pallas_call | solution.py:129
  10.8 1.3 %collective-permute-start.3 = (bf16[4,64,512]{2,1,0:T(8,128)(2,1)S(1)}, bf16[4,64,512]{2,1,0:T(8,128)(2,1)S(1)}, u32[]{:S(2)}, u32[]{:S(2)}) collective-permute-start(bf16[4,64,512]{2,1,0:T(8,128)(2,1)S(1)} %get-tuple-element.37), channel_id=1, source_target_pairs={{0,19},{1,18},{2,17},{3,16},{4,23},{5,22},{6,21},{7,20},{8,27},{9,... | collective-permute-start | bytes 786440 | tf_op jit(solution)/shard_map/ppermute | solution.py:41
  12.1 1.3 %collective-permute-start.7 = (bf16[4,64,512]{2,1,0:T(8,128)(2,1)S(1)}, bf16[4,64,512]{2,1,0:T(8,128)(2,1)S(1)}, u32[]{:S(2)}, u32[]{:S(2)}) collective-permute-start(bf16[4,64,512]{2,1,0:T(8,128)(2,1)S(1)} %get-tuple-element.44), channel_id=1, source_target_pairs={{0,18},{1,19},{2,16},{3,17},{4,22},{5,23},{6,20},{7,21},{8,26},{9,... | collective-permute-start | bytes 786440 | tf_op jit(solution)/shard_map/ppermute | solution.py:41
  13.7 1.6 %collective-permute-start.8 = (bf16[4,64,512]{2,1,0:T(8,128)(2,1)S(1)}, bf16[4,64,512]{2,1,0:T(8,128)(2,1)S(1)}, u32[]{:S(2)}, u32[]{:S(2)}) collective-permute-start(bf16[4,64,512]{2,1,0:T(8,128)(2,1)S(1)} %get-tuple-element.45), channel_id=1, source_target_pairs={{0,16},{1,17},{2,18},{3,19},{4,20},{5,21},{6,22},{7,23},{8,24},{9,... | collective-permute-start | bytes 786440 | tf_op jit(solution)/shard_map/ppermute | solution.py:41
  17.5 1.3 %collective-permute-start.5 = (bf16[4,64,512]{2,1,0:T(8,128)(2,1)S(1)}, bf16[4,64,512]{2,1,0:T(8,128)(2,1)S(1)}, u32[]{:S(2)}, u32[]{:S(2)}) collective-permute-start(bf16[4,64,512]{2,1,0:T(8,128)(2,1)S(1)} %constant_dynamic-update-slice_fusion.rest_1_.rest_0_), channel_id=1, source_target_pairs={{16,3},{17,2},{18,1},{19,0},{20,7},{21,6},{22,5},{23,4},{24,11},{2... | collective-permute-start | bytes 786440 | tf_op jit(solution)/shard_map/ppermute | solution.py:41
  19.7 2.6 %collective-permute-done.6.rest_1_ = bf16[4,64,512]{2,1,0:T(8,128)(2,1)S(1)} collective-permute-done((bf16[4,64,512]{2,1,0:T(8,128)(2,1)S(1)}, bf16[4,64,512]{2,1,0:T(8,128)(2,1)S(1)}, u32[]{:S(2)}, u32[]{:S(2)}) %collective-permute-start.6) | collective-permute-done | bytes 262176 | tf_op jit(solution)/shard_map/ppermute | solution.py:41
  22.5 1.3 %collective-permute-start.10 = (bf16[1,64,512]{2,1,0:T(8,128)(2,1)S(1)}, bf16[1,64,512]{2,1,0:T(8,128)(2,1)S(1)}, u32[]{:S(2)}, u32[]{:S(2)}) collective-permute-start(bf16[1,64,512]{2,1,0:T(8,128)(2,1)S(1)} %get-tuple-element.69), channel_id=1, source_target_pairs={{16,12},{17,13},{18,14},{19,15},{20,8},{21,9},{22,10},{23,11},{24,... | collective-permute-start | bytes 196616 | tf_op jit(solution)/shard_map/ppermute | solution.py:41
  23.8 1.3 %collective-permute-start.11 = (bf16[1,64,512]{2,1,0:T(8,128)(2,1)S(1)}, bf16[1,64,512]{2,1,0:T(8,128)(2,1)S(1)}, u32[]{:S(2)}, u32[]{:S(2)}) collective-permute-start(bf16[1,64,512]{2,1,0:T(8,128)(2,1)S(1)} %get-tuple-element.68), channel_id=1, source_target_pairs={{16,8},{17,9},{18,10},{19,11},{20,12},{21,13},{22,14},{23,15},{24,... | collective-permute-start | bytes 196616 | tf_op jit(solution)/shard_map/ppermute | solution.py:41
  25.1 4.2 %collective-permute-start.12 = (bf16[1,64,512]{2,1,0:T(8,128)(2,1)S(1)}, bf16[1,64,512]{2,1,0:T(8,128)(2,1)S(1)}, u32[]{:S(2)}, u32[]{:S(2)}) collective-permute-start(bf16[1,64,512]{2,1,0:T(8,128)(2,1)S(1)} %get-tuple-element.67), channel_id=1, source_target_pairs={{0,20},{1,21},{2,22},{3,23},{4,16},{5,17},{6,18},{7,19},{8,28},{9,... | collective-permute-start | bytes 196616 | tf_op jit(solution)/shard_map/ppermute | solution.py:41
  31.6 1.4 %collective-permute-start.13 = (bf16[64,512]{1,0:T(8,128)(2,1)S(1)}, bf16[64,512]{1,0:T(8,128)(2,1)S(1)}, u32[]{:S(2)}, u32[]{:S(2)}) collective-permute-start(bf16[64,512]{1,0:T(8,128)(2,1)S(1)} %fusion.7), channel_id=1, source_target_pairs={{16,0},{17,1},{18,2},{19,3},{20,4},{21,5},{22,6},{23,7},{24,8},{25... | collective-permute-start | bytes 196616 | tf_op jit(solution)/shard_map/ppermute | solution.py:41
  33.9 1.5 %collective-permute-start.14 = (bf16[1,64,512]{2,1,0:T(8,128)(2,1)S(1)}, bf16[1,64,512]{2,1,0:T(8,128)(2,1)S(1)}, u32[]{:S(2)}, u32[]{:S(2)}) collective-permute-start(bf16[1,64,512]{2,1,0:T(8,128)(2,1)S(1)} %bitcast.26), channel_id=1, source_target_pairs={{16,12},{17,13},{18,14},{19,15},{20,8},{21,9},{22,10},{23,11},{24,... | collective-permute-start | bytes 196616 | tf_op jit(solution)/shard_map/ppermute | solution.py:41
  36.4 1.6 %collective-permute-start.16 = (bf16[1,64,512]{2,1,0:T(8,128)(2,1)S(1)}, bf16[1,64,512]{2,1,0:T(8,128)(2,1)S(1)}, u32[]{:S(2)}, u32[]{:S(2)}) collective-permute-start(bf16[1,64,512]{2,1,0:T(8,128)(2,1)S(1)} %bitcast.28), channel_id=1, source_target_pairs={{16,4},{17,5},{18,6},{19,7},{20,0},{21,1},{22,2},{23,3},{24,12},{2... | collective-permute-start | bytes 196616 | tf_op jit(solution)/shard_map/ppermute | solution.py:41
  40.6 2.4 %collective-permute-done.15 = bf16[1,64,512]{2,1,0:T(8,128)(2,1)S(1)} collective-permute-done((bf16[1,64,512]{2,1,0:T(8,128)(2,1)S(1)}, bf16[1,64,512]{2,1,0:T(8,128)(2,1)S(1)}, u32[]{:S(2)}, u32[]{:S(2)}) %collective-permute-start.15) | collective-permute-done | bytes 65568 | tf_op jit(solution)/shard_map/ppermute | solution.py:41
  44.8 3.1 %collective-permute-start.17 = (bf16[4,64,512]{2,1,0:T(8,128)(2,1)S(1)}, bf16[4,64,512]{2,1,0:T(8,128)(2,1)S(1)}, u32[]{:S(2)}, u32[]{:S(2)}) collective-permute-start(bf16[4,64,512]{2,1,0:T(8,128)(2,1)S(1)} %constant_dynamic-update-slice_fusion.4.rest_1_.rest_0_), channel_id=1, source_target_pairs={{0,18},{1,19},{2,16},{3,17},{4,22},{5,23},{6,20},{7,21},{8,26},{9,... | collective-permute-start | bytes 786440 | tf_op jit(solution)/shard_map/ppermute | solution.py:41
  48.0 1.3 %collective-permute-start.18 = (bf16[4,64,512]{2,1,0:T(8,128)(2,1)S(1)}, bf16[4,64,512]{2,1,0:T(8,128)(2,1)S(1)}, u32[]{:S(2)}, u32[]{:S(2)}) collective-permute-start(bf16[4,64,512]{2,1,0:T(8,128)(2,1)S(1)} %constant_dynamic-update-slice_fusion.4.rest_1_.rest_0_), channel_id=1, source_target_pairs={{0,19},{1,18},{2,17},{3,16},{4,23},{5,22},{6,21},{7,20},{8,27},{9,... | collective-permute-start | bytes 786440 | tf_op jit(solution)/shard_map/ppermute | solution.py:41
  50.1 1.5 %collective-permute-done.19.rest_1_ = bf16[4,64,512]{2,1,0:T(8,128)(2,1)S(1)} collective-permute-done((bf16[4,64,512]{2,1,0:T(8,128)(2,1)S(1)}, bf16[4,64,512]{2,1,0:T(8,128)(2,1)S(1)}, u32[]{:S(2)}, u32[]{:S(2)}) %collective-permute-start.19) | collective-permute-done | bytes 262176 | tf_op jit(solution)/shard_map/ppermute | solution.py:41
  51.9 3.4 %collective-permute-start.23 = (bf16[1,64,512]{2,1,0:T(8,128)(2,1)S(1)}, bf16[1,64,512]{2,1,0:T(8,128)(2,1)S(1)}, u32[]{:S(2)}, u32[]{:S(2)}) collective-permute-start(bf16[1,64,512]{2,1,0:T(8,128)(2,1)S(1)} %get-tuple-element.62), channel_id=1, source_target_pairs={{0,28},{1,29},{2,30},{3,31},{4,24},{5,25},{6,26},{7,27},{8,20},{9,... | collective-permute-start | bytes 196616 | tf_op jit(solution)/shard_map/ppermute | solution.py:41
  55.3 1.3 %collective-permute-start.24 = (bf16[1,64,512]{2,1,0:T(8,128)(2,1)S(1)}, bf16[1,64,512]{2,1,0:T(8,128)(2,1)S(1)}, u32[]{:S(2)}, u32[]{:S(2)}) collective-permute-start(bf16[1,64,512]{2,1,0:T(8,128)(2,1)S(1)} %get-tuple-element.65), channel_id=1, source_target_pairs={{0,24},{1,25},{2,26},{3,27},{4,28},{5,29},{6,30},{7,31},{8,16},{9,... | collective-permute-start | bytes 196616 | tf_op jit(solution)/shard_map/ppermute | solution.py:41
  56.8 1.6 %collective-permute-start.26 = (bf16[1,64,512]{2,1,0:T(8,128)(2,1)S(1)}, bf16[1,64,512]{2,1,0:T(8,128)(2,1)S(1)}, u32[]{:S(2)}, u32[]{:S(2)}) collective-permute-start(bf16[1,64,512]{2,1,0:T(8,128)(2,1)S(1)} %get-tuple-element.63), channel_id=1, source_target_pairs={{16,0},{17,1},{18,2},{19,3},{20,4},{21,5},{22,6},{23,7},{24,8},{25... | collective-permute-start | bytes 196616 | tf_op jit(solution)/shard_map/ppermute | solution.py:41
  58.9 2.7 %collective-permute-done.25 = bf16[1,64,512]{2,1,0:T(8,128)(2,1)S(1)} collective-permute-done((bf16[1,64,512]{2,1,0:T(8,128)(2,1)S(1)}, bf16[1,64,512]{2,1,0:T(8,128)(2,1)S(1)}, u32[]{:S(2)}, u32[]{:S(2)}) %collective-permute-start.25) | collective-permute-done | bytes 65568 | tf_op jit(solution)/shard_map/ppermute | solution.py:41
  63.2 2.0 %collective-permute-start.28 = (bf16[32,256]{1,0:T(8,128)(2,1)S(1)}, bf16[32,256]{1,0:T(8,128)(2,1)S(1)}, u32[]{:S(2)}, u32[]{:S(2)}) collective-permute-start(bf16[32,256]{1,0:T(8,128)(2,1)S(1)} %add_convert_fusion.3), channel_id=1, source_target_pairs={{0,3},{1,2},{2,1},{3,0},{4,7},{5,6},{6,5},{7,4},{8,11},{9,10},{10,... | collective-permute-start | bytes 49160 | tf_op jit(solution)/shard_map/ppermute | solution.py:41
  70.1 1.9 %collective-permute-start.31 = (bf16[32,256]{1,0:T(8,128)(2,1)S(1)}, bf16[32,256]{1,0:T(8,128)(2,1)S(1)}, u32[]{:S(2)}, u32[]{:S(2)}) collective-permute-start(bf16[32,256]{1,0:T(8,128)(2,1)S(1)} %add_convert_fusion.2.refs_3_), channel_id=1, source_target_pairs={{0,12},{1,13},{2,14},{3,15},{4,8},{5,9},{6,10},{7,11},{8,4},{9,5},... | collective-permute-start | bytes 49160 | tf_op jit(solution)/shard_map/ppermute | solution.py:41
  72.0 2.6 %collective-permute-start.33 = (bf16[32,256]{1,0:T(8,128)(2,1)S(1)}, bf16[32,256]{1,0:T(8,128)(2,1)S(1)}, u32[]{:S(2)}, u32[]{:S(2)}) collective-permute-start(bf16[32,256]{1,0:T(8,128)(2,1)S(1)} %add_convert_fusion.2.refs_3_), channel_id=1, source_target_pairs={{0,4},{1,5},{2,6},{3,7},{4,0},{5,1},{6,2},{7,3},{8,12},{9,13},{10,... | collective-permute-start | bytes 49160 | tf_op jit(solution)/shard_map/ppermute | solution.py:41
  (91 shorter events, 23.8 us)
Async XLA Ops:
  0.6 12.8 %collective-permute-start = (bf16[1,64,512]{2,1,0:T(8,128)(2,1)}, bf16[1,64,512]{2,1,0:T(8,128)(2,1)S(1)}, u32[]{:S(2)}, u32[]{:S(2)}) collective-permute-start(bf16[1,64,512]{2,1,0:T(8,128)(2,1)} %bitcast.30), channel_id=1, source_target_pairs={{0,28},{1,29},{2,30},{3,31},{4,24},{5,25},{6,26},{7,27},{8,20},{9,... | collective-permute-start | bytes 196616 | tf_op jit(solution)/shard_map/ppermute | solution.py:41
  5.2 8.3 %collective-permute-start.1 = (bf16[1,64,512]{2,1,0:T(8,128)(2,1)}, bf16[1,64,512]{2,1,0:T(8,128)(2,1)S(1)}, u32[]{:S(2)}, u32[]{:S(2)}) collective-permute-start(bf16[1,64,512]{2,1,0:T(8,128)(2,1)} %bitcast.31), channel_id=1, source_target_pairs={{0,24},{1,25},{2,26},{3,27},{4,28},{5,29},{6,30},{7,31},{8,16},{9,... | collective-permute-start | bytes 196616 | tf_op jit(solution)/shard_map/ppermute | solution.py:41
  5.2 8.3 %collective-permute-start.2 = (bf16[1,64,512]{2,1,0:T(8,128)(2,1)}, bf16[1,64,512]{2,1,0:T(8,128)(2,1)S(1)}, u32[]{:S(2)}, u32[]{:S(2)}) collective-permute-start(bf16[1,64,512]{2,1,0:T(8,128)(2,1)} %bitcast.32), channel_id=1, source_target_pairs={{0,20},{1,21},{2,22},{3,23},{4,16},{5,17},{6,18},{7,19},{8,28},{9,... | collective-permute-start | bytes 196616 | tf_op jit(solution)/shard_map/ppermute | solution.py:41
  10.8 5.4 %collective-permute-start.3 = (bf16[4,64,512]{2,1,0:T(8,128)(2,1)S(1)}, bf16[4,64,512]{2,1,0:T(8,128)(2,1)S(1)}, u32[]{:S(2)}, u32[]{:S(2)}) collective-permute-start(bf16[4,64,512]{2,1,0:T(8,128)(2,1)S(1)} %get-tuple-element.37), channel_id=1, source_target_pairs={{0,19},{1,18},{2,17},{3,16},{4,23},{5,22},{6,21},{7,20},{8,27},{9,... | collective-permute-start | bytes 786440 | tf_op jit(solution)/shard_map/ppermute | solution.py:41
  12.1 7.6 %collective-permute-start.7 = (bf16[4,64,512]{2,1,0:T(8,128)(2,1)S(1)}, bf16[4,64,512]{2,1,0:T(8,128)(2,1)S(1)}, u32[]{:S(2)}, u32[]{:S(2)}) collective-permute-start(bf16[4,64,512]{2,1,0:T(8,128)(2,1)S(1)} %get-tuple-element.44), channel_id=1, source_target_pairs={{0,18},{1,19},{2,16},{3,17},{4,22},{5,23},{6,20},{7,21},{8,26},{9,... | collective-permute-start | bytes 786440 | tf_op jit(solution)/shard_map/ppermute | solution.py:41
  13.6 8.7 %collective-permute-start.6 = (bf16[4,64,512]{2,1,0:T(8,128)(2,1)S(1)}, bf16[4,64,512]{2,1,0:T(8,128)(2,1)S(1)}, u32[]{:S(2)}, u32[]{:S(2)}) collective-permute-start(bf16[4,64,512]{2,1,0:T(8,128)(2,1)S(1)} %mix.2), channel_id=1, source_target_pairs={{0,17},{1,16},{2,19},{3,18},{4,21},{5,20},{6,23},{7,22},{8,25},{9,... | collective-permute-start | bytes 786440 | tf_op jit(solution)/shard_map/ppermute | solution.py:41
  13.7 8.7 %collective-permute-start.8 = (bf16[4,64,512]{2,1,0:T(8,128)(2,1)S(1)}, bf16[4,64,512]{2,1,0:T(8,128)(2,1)S(1)}, u32[]{:S(2)}, u32[]{:S(2)}) collective-permute-start(bf16[4,64,512]{2,1,0:T(8,128)(2,1)S(1)} %get-tuple-element.45), channel_id=1, source_target_pairs={{0,16},{1,17},{2,18},{3,19},{4,20},{5,21},{6,22},{7,23},{8,24},{9,... | collective-permute-start | bytes 786440 | tf_op jit(solution)/shard_map/ppermute | solution.py:41
  16.3 13.9 %collective-permute-start.4 = (bf16[4,64,512]{2,1,0:T(8,128)(2,1)S(1)}, bf16[4,64,512]{2,1,0:T(8,128)(2,1)S(1)}, u32[]{:S(2)}, u32[]{:S(2)}) collective-permute-start(bf16[4,64,512]{2,1,0:T(8,128)(2,1)S(1)} %constant_dynamic-update-slice_fusion.rest_1_.rest_0_), channel_id=1, source_target_pairs={{16,2},{17,3},{18,0},{19,1},{20,6},{21,7},{22,4},{23,5},{24,10},{2... | collective-permute-start | bytes 786440 | tf_op jit(solution)/shard_map/ppermute | solution.py:41
  17.5 12.7 %collective-permute-start.5 = (bf16[4,64,512]{2,1,0:T(8,128)(2,1)S(1)}, bf16[4,64,512]{2,1,0:T(8,128)(2,1)S(1)}, u32[]{:S(2)}, u32[]{:S(2)}) collective-permute-start(bf16[4,64,512]{2,1,0:T(8,128)(2,1)S(1)} %constant_dynamic-update-slice_fusion.rest_1_.rest_0_), channel_id=1, source_target_pairs={{16,3},{17,2},{18,1},{19,0},{20,7},{21,6},{22,5},{23,4},{24,11},{2... | collective-permute-start | bytes 786440 | tf_op jit(solution)/shard_map/ppermute | solution.py:41
  22.5 8.9 %collective-permute-start.10 = (bf16[1,64,512]{2,1,0:T(8,128)(2,1)S(1)}, bf16[1,64,512]{2,1,0:T(8,128)(2,1)S(1)}, u32[]{:S(2)}, u32[]{:S(2)}) collective-permute-start(bf16[1,64,512]{2,1,0:T(8,128)(2,1)S(1)} %get-tuple-element.69), channel_id=1, source_target_pairs={{16,12},{17,13},{18,14},{19,15},{20,8},{21,9},{22,10},{23,11},{24,... | collective-permute-start | bytes 196616 | tf_op jit(solution)/shard_map/ppermute | solution.py:41
  23.8 7.6 %collective-permute-start.11 = (bf16[1,64,512]{2,1,0:T(8,128)(2,1)S(1)}, bf16[1,64,512]{2,1,0:T(8,128)(2,1)S(1)}, u32[]{:S(2)}, u32[]{:S(2)}) collective-permute-start(bf16[1,64,512]{2,1,0:T(8,128)(2,1)S(1)} %get-tuple-element.68), channel_id=1, source_target_pairs={{16,8},{17,9},{18,10},{19,11},{20,12},{21,13},{22,14},{23,15},{24,... | collective-permute-start | bytes 196616 | tf_op jit(solution)/shard_map/ppermute | solution.py:41
  25.1 6.4 %collective-permute-start.12 = (bf16[1,64,512]{2,1,0:T(8,128)(2,1)S(1)}, bf16[1,64,512]{2,1,0:T(8,128)(2,1)S(1)}, u32[]{:S(2)}, u32[]{:S(2)}) collective-permute-start(bf16[1,64,512]{2,1,0:T(8,128)(2,1)S(1)} %get-tuple-element.67), channel_id=1, source_target_pairs={{0,20},{1,21},{2,22},{3,23},{4,16},{5,17},{6,18},{7,19},{8,28},{9,... | collective-permute-start | bytes 196616 | tf_op jit(solution)/shard_map/ppermute | solution.py:41
  33.9 6.7 %collective-permute-start.14 = (bf16[1,64,512]{2,1,0:T(8,128)(2,1)S(1)}, bf16[1,64,512]{2,1,0:T(8,128)(2,1)S(1)}, u32[]{:S(2)}, u32[]{:S(2)}) collective-permute-start(bf16[1,64,512]{2,1,0:T(8,128)(2,1)S(1)} %bitcast.26), channel_id=1, source_target_pairs={{16,12},{17,13},{18,14},{19,15},{20,8},{21,9},{22,10},{23,11},{24,... | collective-permute-start | bytes 196616 | tf_op jit(solution)/shard_map/ppermute | solution.py:41
  35.4 7.7 %collective-permute-start.15 = (bf16[1,64,512]{2,1,0:T(8,128)(2,1)S(1)}, bf16[1,64,512]{2,1,0:T(8,128)(2,1)S(1)}, u32[]{:S(2)}, u32[]{:S(2)}) collective-permute-start(bf16[1,64,512]{2,1,0:T(8,128)(2,1)S(1)} %bitcast.27), channel_id=1, source_target_pairs={{16,8},{17,9},{18,10},{19,11},{20,12},{21,13},{22,14},{23,15},{24,... | collective-permute-start | bytes 196616 | tf_op jit(solution)/shard_map/ppermute | solution.py:41
  36.4 6.7 %collective-permute-start.16 = (bf16[1,64,512]{2,1,0:T(8,128)(2,1)S(1)}, bf16[1,64,512]{2,1,0:T(8,128)(2,1)S(1)}, u32[]{:S(2)}, u32[]{:S(2)}) collective-permute-start(bf16[1,64,512]{2,1,0:T(8,128)(2,1)S(1)} %bitcast.28), channel_id=1, source_target_pairs={{16,4},{17,5},{18,6},{19,7},{20,0},{21,1},{22,2},{23,3},{24,12},{2... | collective-permute-start | bytes 196616 | tf_op jit(solution)/shard_map/ppermute | solution.py:41
  38.0 10.0 %collective-permute-start.20 = (bf16[4,64,512]{2,1,0:T(8,128)(2,1)S(1)}, bf16[4,64,512]{2,1,0:T(8,128)(2,1)S(1)}, u32[]{:S(2)}, u32[]{:S(2)}) collective-permute-start(bf16[4,64,512]{2,1,0:T(8,128)(2,1)S(1)} %get-tuple-element.56), channel_id=1, source_target_pairs={{16,3},{17,2},{18,1},{19,0},{20,7},{21,6},{22,5},{23,4},{24,11},{2... | collective-permute-start | bytes 786440 | tf_op jit(solution)/shard_map/ppermute | solution.py:41
  39.3 10.8 %collective-permute-start.21 = (bf16[4,64,512]{2,1,0:T(8,128)(2,1)S(1)}, bf16[4,64,512]{2,1,0:T(8,128)(2,1)S(1)}, u32[]{:S(2)}, u32[]{:S(2)}) collective-permute-start(bf16[4,64,512]{2,1,0:T(8,128)(2,1)S(1)} %get-tuple-element.57), channel_id=1, source_target_pairs={{16,2},{17,3},{18,0},{19,1},{20,6},{21,7},{22,4},{23,5},{24,10},{2... | collective-permute-start | bytes 786440 | tf_op jit(solution)/shard_map/ppermute | solution.py:41
  43.2 8.5 %collective-permute-start.19 = (bf16[4,64,512]{2,1,0:T(8,128)(2,1)S(1)}, bf16[4,64,512]{2,1,0:T(8,128)(2,1)S(1)}, u32[]{:S(2)}, u32[]{:S(2)}) collective-permute-start(bf16[4,64,512]{2,1,0:T(8,128)(2,1)S(1)} %mix.3), channel_id=1, source_target_pairs={{16,1},{17,0},{18,3},{19,2},{20,5},{21,4},{22,7},{23,6},{24,9},{25... | collective-permute-start | bytes 786440 | tf_op jit(solution)/shard_map/ppermute | solution.py:41
  44.4 7.3 %collective-permute-start.22 = (bf16[4,64,512]{2,1,0:T(8,128)(2,1)S(1)}, bf16[4,64,512]{2,1,0:T(8,128)(2,1)S(1)}, u32[]{:S(2)}, u32[]{:S(2)}) collective-permute-start(bf16[4,64,512]{2,1,0:T(8,128)(2,1)S(1)} %get-tuple-element.58), channel_id=1, source_target_pairs={{16,0},{17,1},{18,2},{19,3},{20,4},{21,5},{22,6},{23,7},{24,8},{25... | collective-permute-start | bytes 786440 | tf_op jit(solution)/shard_map/ppermute | solution.py:41
  44.8 11.9 %collective-permute-start.17 = (bf16[4,64,512]{2,1,0:T(8,128)(2,1)S(1)}, bf16[4,64,512]{2,1,0:T(8,128)(2,1)S(1)}, u32[]{:S(2)}, u32[]{:S(2)}) collective-permute-start(bf16[4,64,512]{2,1,0:T(8,128)(2,1)S(1)} %constant_dynamic-update-slice_fusion.4.rest_1_.rest_0_), channel_id=1, source_target_pairs={{0,18},{1,19},{2,16},{3,17},{4,22},{5,23},{6,20},{7,21},{8,26},{9,... | collective-permute-start | bytes 786440 | tf_op jit(solution)/shard_map/ppermute | solution.py:41
  48.0 10.3 %collective-permute-start.18 = (bf16[4,64,512]{2,1,0:T(8,128)(2,1)S(1)}, bf16[4,64,512]{2,1,0:T(8,128)(2,1)S(1)}, u32[]{:S(2)}, u32[]{:S(2)}) collective-permute-start(bf16[4,64,512]{2,1,0:T(8,128)(2,1)S(1)} %constant_dynamic-update-slice_fusion.4.rest_1_.rest_0_), channel_id=1, source_target_pairs={{0,19},{1,18},{2,17},{3,16},{4,23},{5,22},{6,21},{7,20},{8,27},{9,... | collective-permute-start | bytes 786440 | tf_op jit(solution)/shard_map/ppermute | solution.py:41
  51.9 6.7 %collective-permute-start.23 = (bf16[1,64,512]{2,1,0:T(8,128)(2,1)S(1)}, bf16[1,64,512]{2,1,0:T(8,128)(2,1)S(1)}, u32[]{:S(2)}, u32[]{:S(2)}) collective-permute-start(bf16[1,64,512]{2,1,0:T(8,128)(2,1)S(1)} %get-tuple-element.62), channel_id=1, source_target_pairs={{0,28},{1,29},{2,30},{3,31},{4,24},{5,25},{6,26},{7,27},{8,20},{9,... | collective-permute-start | bytes 196616 | tf_op jit(solution)/shard_map/ppermute | solution.py:41
  56.6 5.0 %collective-permute-start.25 = (bf16[1,64,512]{2,1,0:T(8,128)(2,1)S(1)}, bf16[1,64,512]{2,1,0:T(8,128)(2,1)S(1)}, u32[]{:S(2)}, u32[]{:S(2)}) collective-permute-start(bf16[1,64,512]{2,1,0:T(8,128)(2,1)S(1)} %get-tuple-element.64), channel_id=1, source_target_pairs={{16,4},{17,5},{18,6},{19,7},{20,0},{21,1},{22,2},{23,3},{24,12},{2... | collective-permute-start | bytes 196616 | tf_op jit(solution)/shard_map/ppermute | solution.py:41
  70.1 5.6 %collective-permute-start.31 = (bf16[32,256]{1,0:T(8,128)(2,1)S(1)}, bf16[32,256]{1,0:T(8,128)(2,1)S(1)}, u32[]{:S(2)}, u32[]{:S(2)}) collective-permute-start(bf16[32,256]{1,0:T(8,128)(2,1)S(1)} %add_convert_fusion.2.refs_3_), channel_id=1, source_target_pairs={{0,12},{1,13},{2,14},{3,15},{4,8},{5,9},{6,10},{7,11},{8,4},{9,5},... | collective-permute-start | bytes 49160 | tf_op jit(solution)/shard_map/ppermute | solution.py:41
  (17 other events, 142.1 us)

commit v4 on v2

--- a/solution.py
+++ b/solution.py
@@ -38,6 +38,9 @@
             digit = t // stride % radix
             other = t + (peer(digit, step, radix) - digit) * stride
             pairs.append((start * tp + t, end * tp + other))
+    if len(routes) == 1 and routes[0][0] != routes[0][1]:
+        start, end = routes[0]
+        pairs += [(end * tp + t, start * tp + t) for t in range(tp)]
     return lax.ppermute(value, axes, pairs)
 
 

time: 72.9 us -> 66.6 us (0.914)
  starting transfers between devices: 46.6 us -> 37.1 us
  waiting for transfers between devices: 16.3 us -> 20 us
    ppermute x36, starting transfers between devices: 46.6 us -> 37.1 us  [exchange(): return lax.ppermute(value, axes, pairs)]
    ppermute x36, waiting for transfers between devices: 16.3 us -> 20 us  [exchange(): return lax.ppermute(value, axes, pairs)]
  transfers between devices with their start and end apart: 36 -> 36, of which waited for: 16 -> 18; matrix products, arithmetic and copies ran while one was open for 1% -> 1% of each run, Pallas kernels for 9% -> 10%
where the time goes in v4:
time: 66.6 us; the launch traced here: 66.4 us
  starting transfers between devices  37.1 us (56%)
  waiting for transfers between devices  20 us (30%)
  Pallas kernels  7.35 us (11%)
  other arithmetic  0.98 us (1%)
  between operations  0.89 us (1%)
    ppermute x36, starting transfers between devices, exchange(): return lax.ppermute(value, axes, pairs)  37.1 us
    ppermute x36, waiting for transfers between devices, exchange(): return lax.ppermute(value, axes, pairs)  20 us
    pallas_call x1, Pallas kernels, spread(): pl.pallas_call(functools.partial(first_spread_kernel, outputs=groups, lay...  4.68 us
    pallas_call x4, Pallas kernels, meet(): pl.pallas_call(functools.partial(meet_kernel, first=first, blocks=len(gro...  1.78 us
  transfers between devices with their start and end apart: 36, of which 18 were waited for; matrix products, arithmetic and copies ran while one was open for 1% of the time, Pallas kernels for 10%

profile of v4, /device:TPU:0, one launch (start us, length us, event | category | flops | bytes accessed | tf_op | source)
XLA Modules:
  0.0 66.4 jit_solution(12766734467966300284)
XLA Ops:
  0.6 4.6 %collective-permute-start = (bf16[1,64,512]{2,1,0:T(8,128)(2,1)}, bf16[1,64,512]{2,1,0:T(8,128)(2,1)S(1)}, u32[]{:S(2)}, u32[]{:S(2)}) collective-permute-start(bf16[1,64,512]{2,1,0:T(8,128)(2,1)} %bitcast.30), channel_id=1, source_target_pairs={{0,28},{1,29},{2,30},{3,31},{4,24},{5,25},{6,26},{7,27},{8,20},{9,... | collective-permute-start | bytes 196616 | tf_op jit(solution)/shard_map/ppermute | solution.py:44
  6.1 4.7 %first_spread.1 = (bf16[4,64,512]{2,1,0:T(8,128)(2,1)S(1)}, bf16[4,64,512]{2,1,0:T(8,128)(2,1)S(1)}, bf16[4,64,512]{2,1,0:T(8,128)(2,1)S(1)}, bf16[4,64,512]{2,1,0:T(8,128)(2,1)S(1)}) custom-call(bf16[64,512]{1,0:T(8,128)(2,1)} %bitcast.33, bf16[1,512,8192]{2,1,0:T(8,128)(2,1)} %weight.13), custom_call_target="tpu_custom_call" | custom-call | tf_op jit(solution)/shard_map/first_spread/pallas_call | solution.py:132
  10.9 1.6 %collective-permute-start.7 = (bf16[4,64,512]{2,1,0:T(8,128)(2,1)S(1)}, bf16[4,64,512]{2,1,0:T(8,128)(2,1)S(1)}, u32[]{:S(2)}, u32[]{:S(2)}) collective-permute-start(bf16[4,64,512]{2,1,0:T(8,128)(2,1)S(1)} %get-tuple-element.43), channel_id=1, source_target_pairs={{0,18},{1,19},{2,16},{3,17},{4,22},{5,23},{6,20},{7,21},{8,26},{9,... | collective-permute-start | bytes 786440 | tf_op jit(solution)/shard_map/ppermute | solution.py:44
  13.1 1.7 %collective-permute-done.3 = bf16[4,64,512]{2,1,0:T(8,128)(2,1)S(1)} collective-permute-done((bf16[4,64,512]{2,1,0:T(8,128)(2,1)S(1)}, bf16[4,64,512]{2,1,0:T(8,128)(2,1)S(1)}, u32[]{:S(2)}, u32[]{:S(2)}) %collective-permute-start.3) | collective-permute-done | bytes 262176 | tf_op jit(solution)/shard_map/ppermute | solution.py:44
  14.8 2.8 %collective-permute-start.6 = (bf16[4,64,512]{2,1,0:T(8,128)(2,1)S(1)}, bf16[4,64,512]{2,1,0:T(8,128)(2,1)S(1)}, u32[]{:S(2)}, u32[]{:S(2)}) collective-permute-start(bf16[4,64,512]{2,1,0:T(8,128)(2,1)S(1)} %pad_maximum_fusion.rest_0_), channel_id=1, source_target_pairs={{16,1},{17,0},{18,3},{19,2},{20,5},{21,4},{22,7},{23,6},{24,9},{25... | collective-permute-start | bytes 786440 | tf_op jit(solution)/shard_map/ppermute | solution.py:44
  18.5 1.8 %collective-permute-start.5 = (bf16[4,64,512]{2,1,0:T(8,128)(2,1)S(1)}, bf16[4,64,512]{2,1,0:T(8,128)(2,1)S(1)}, u32[]{:S(2)}, u32[]{:S(2)}) collective-permute-start(bf16[4,64,512]{2,1,0:T(8,128)(2,1)S(1)} %pad_maximum_fusion.rest_0_), channel_id=1, source_target_pairs={{16,3},{17,2},{18,1},{19,0},{20,7},{21,6},{22,5},{23,4},{24,11},{2... | collective-permute-start | bytes 786440 | tf_op jit(solution)/shard_map/ppermute | solution.py:44
  20.5 3.3 %collective-permute-start.11 = (bf16[1,64,512]{2,1,0:T(8,128)(2,1)S(1)}, bf16[1,64,512]{2,1,0:T(8,128)(2,1)S(1)}, u32[]{:S(2)}, u32[]{:S(2)}) collective-permute-start(bf16[1,64,512]{2,1,0:T(8,128)(2,1)S(1)} %get-tuple-element.69), channel_id=1, source_target_pairs={{16,8},{17,9},{18,10},{19,11},{20,12},{21,13},{22,14},{23,15},{24,... | collective-permute-start | bytes 196616 | tf_op jit(solution)/shard_map/ppermute | solution.py:44
  24.8 1.4 %collective-permute-done.5.rest_1_ = bf16[4,64,512]{2,1,0:T(8,128)(2,1)S(1)} collective-permute-done((bf16[4,64,512]{2,1,0:T(8,128)(2,1)S(1)}, bf16[4,64,512]{2,1,0:T(8,128)(2,1)S(1)}, u32[]{:S(2)}, u32[]{:S(2)}) %collective-permute-start.5) | collective-permute-done | bytes 262176 | tf_op jit(solution)/shard_map/ppermute | solution.py:44
  28.0 1.2 %collective-permute-done.14 = bf16[64,512]{1,0:T(8,128)(2,1)S(1)} collective-permute-done((bf16[64,512]{1,0:T(8,128)(2,1)S(1)}, bf16[64,512]{1,0:T(8,128)(2,1)S(1)}, u32[]{:S(2)}, u32[]{:S(2)}) %collective-permute-start.14) | collective-permute-done | bytes 65568 | tf_op jit(solution)/shard_map/ppermute | solution.py:44
  29.3 2.5 %collective-permute-start.15 = (bf16[1,64,512]{2,1,0:T(8,128)(2,1)S(1)}, bf16[1,64,512]{2,1,0:T(8,128)(2,1)S(1)}, u32[]{:S(2)}, u32[]{:S(2)}) collective-permute-start(bf16[1,64,512]{2,1,0:T(8,128)(2,1)S(1)} %bitcast.26), channel_id=1, source_target_pairs={{16,12},{17,13},{18,14},{19,15},{20,8},{21,9},{22,10},{23,11},{24,... | collective-permute-start | bytes 196616 | tf_op jit(solution)/shard_map/ppermute | solution.py:44
  31.8 1.4 %collective-permute-start.17 = (bf16[1,64,512]{2,1,0:T(8,128)(2,1)S(1)}, bf16[1,64,512]{2,1,0:T(8,128)(2,1)S(1)}, u32[]{:S(2)}, u32[]{:S(2)}) collective-permute-start(bf16[1,64,512]{2,1,0:T(8,128)(2,1)S(1)} %bitcast.28), channel_id=1, source_target_pairs={{16,4},{17,5},{18,6},{19,7},{20,0},{21,1},{22,2},{23,3},{24,12},{2... | collective-permute-start | bytes 196616 | tf_op jit(solution)/shard_map/ppermute | solution.py:44
  33.2 2.2 %collective-permute-start.21 = (bf16[4,64,512]{2,1,0:T(8,128)(2,1)S(1)}, bf16[4,64,512]{2,1,0:T(8,128)(2,1)S(1)}, u32[]{:S(2)}, u32[]{:S(2)}) collective-permute-start(bf16[4,64,512]{2,1,0:T(8,128)(2,1)S(1)} %get-tuple-element.55), channel_id=1, source_target_pairs={{16,3},{17,2},{18,1},{19,0},{20,7},{21,6},{22,5},{23,4},{24,11},{2... | collective-permute-start | bytes 786440 | tf_op jit(solution)/shard_map/ppermute | solution.py:44
  35.4 1.2 %collective-permute-start.23 = (bf16[4,64,512]{2,1,0:T(8,128)(2,1)S(1)}, bf16[4,64,512]{2,1,0:T(8,128)(2,1)S(1)}, u32[]{:S(2)}, u32[]{:S(2)}) collective-permute-start(bf16[4,64,512]{2,1,0:T(8,128)(2,1)S(1)} %get-tuple-element.57), channel_id=1, source_target_pairs={{16,1},{17,0},{18,3},{19,2},{20,5},{21,4},{22,7},{23,6},{24,9},{25... | collective-permute-start | bytes 786440 | tf_op jit(solution)/shard_map/ppermute | solution.py:44
  36.6 1.7 %collective-permute-done.16 = bf16[1,64,512]{2,1,0:T(8,128)(2,1)S(1)} collective-permute-done((bf16[1,64,512]{2,1,0:T(8,128)(2,1)S(1)}, bf16[1,64,512]{2,1,0:T(8,128)(2,1)S(1)}, u32[]{:S(2)}, u32[]{:S(2)}) %collective-permute-start.16) | collective-permute-done | bytes 65568 | tf_op jit(solution)/shard_map/ppermute | solution.py:44
  40.5 2.8 %collective-permute-done.22 = bf16[4,64,512]{2,1,0:T(8,128)(2,1)S(1)} collective-permute-done((bf16[4,64,512]{2,1,0:T(8,128)(2,1)S(1)}, bf16[4,64,512]{2,1,0:T(8,128)(2,1)S(1)}, u32[]{:S(2)}, u32[]{:S(2)}) %collective-permute-start.22) | collective-permute-done | bytes 262176 | tf_op jit(solution)/shard_map/ppermute | solution.py:44
  43.5 2.4 %collective-permute-start.25 = (bf16[1,64,512]{2,1,0:T(8,128)(2,1)S(1)}, bf16[1,64,512]{2,1,0:T(8,128)(2,1)S(1)}, u32[]{:S(2)}, u32[]{:S(2)}) collective-permute-start(bf16[1,64,512]{2,1,0:T(8,128)(2,1)S(1)} %get-tuple-element.62), channel_id=1, source_target_pairs={{0,28},{1,29},{2,30},{3,31},{4,24},{5,25},{6,26},{7,27},{8,20},{9,... | collective-permute-start | bytes 196616 | tf_op jit(solution)/shard_map/ppermute | solution.py:44
  46.0 1.4 %collective-permute-start.28 = (bf16[1,64,512]{2,1,0:T(8,128)(2,1)S(1)}, bf16[1,64,512]{2,1,0:T(8,128)(2,1)S(1)}, u32[]{:S(2)}, u32[]{:S(2)}) collective-permute-start(bf16[1,64,512]{2,1,0:T(8,128)(2,1)S(1)} %get-tuple-element.63), channel_id=1, source_target_pairs={{16,0},{17,1},{18,2},{19,3},{20,4},{21,5},{22,6},{23,7},{24,8},{25... | collective-permute-start | bytes 196616 | tf_op jit(solution)/shard_map/ppermute | solution.py:44
  49.3 1.2 %collective-permute-start.29 = (f32[32,256]{1,0:T(8,128)S(1)}, f32[32,256]{1,0:T(8,128)S(1)}, u32[]{:S(2)}, u32[]{:S(2)}) collective-permute-start(f32[32,256]{1,0:T(8,128)S(1)} %get-tuple-element.61), channel_id=1, source_target_pairs={{16,0},{17,1},{18,2},{19,3},{20,4},{21,5},{22,6},{23,7},{24,8},{25... | collective-permute-start | bytes 98312 | tf_op jit(solution)/shard_map/ppermute | solution.py:44
  51.4 2.5 %collective-permute-start.30 = (bf16[32,256]{1,0:T(8,128)(2,1)S(1)}, bf16[32,256]{1,0:T(8,128)(2,1)S(1)}, u32[]{:S(2)}, u32[]{:S(2)}) collective-permute-start(bf16[32,256]{1,0:T(8,128)(2,1)S(1)} %add_convert_fusion.3), channel_id=1, source_target_pairs={{0,3},{1,2},{2,1},{3,0},{4,7},{5,6},{6,5},{7,4},{8,11},{9,10},{10,... | collective-permute-start | bytes 49160 | tf_op jit(solution)/shard_map/ppermute | solution.py:44
  56.0 1.6 %collective-permute-done.31 = bf16[32,256]{1,0:T(8,128)(2,1)S(1)} collective-permute-done((bf16[32,256]{1,0:T(8,128)(2,1)S(1)}, bf16[32,256]{1,0:T(8,128)(2,1)S(1)}, u32[]{:S(2)}, u32[]{:S(2)}) %collective-permute-start.31) | collective-permute-done | bytes 16416 | tf_op jit(solution)/shard_map/ppermute | solution.py:44
  58.0 3.0 %collective-permute-start.33 = (bf16[32,256]{1,0:T(8,128)(2,1)S(1)}, bf16[32,256]{1,0:T(8,128)(2,1)S(1)}, u32[]{:S(2)}, u32[]{:S(2)}) collective-permute-start(bf16[32,256]{1,0:T(8,128)(2,1)S(1)} %add_convert_fusion.2.refs_3_), channel_id=1, source_target_pairs={{0,12},{1,13},{2,14},{3,15},{4,8},{5,9},{6,10},{7,11},{8,4},{9,5},... | collective-permute-start | bytes 49160 | tf_op jit(solution)/shard_map/ppermute | solution.py:44
  61.1 1.4 %collective-permute-start.35 = (bf16[32,256]{1,0:T(8,128)(2,1)S(1)}, bf16[32,256]{1,0:T(8,128)(2,1)S(1)}, u32[]{:S(2)}, u32[]{:S(2)}) collective-permute-start(bf16[32,256]{1,0:T(8,128)(2,1)S(1)} %add_convert_fusion.2.refs_3_), channel_id=1, source_target_pairs={{0,4},{1,5},{2,6},{3,7},{4,0},{5,1},{6,2},{7,3},{8,12},{9,13},{10,... | collective-permute-start | bytes 49160 | tf_op jit(solution)/shard_map/ppermute | solution.py:44
  62.5 1.1 %collective-permute-done.33.refs_0_ = bf16[32,256]{1,0:T(8,128)(2,1)S(1)} collective-permute-done((bf16[32,256]{1,0:T(8,128)(2,1)S(1)}, bf16[32,256]{1,0:T(8,128)(2,1)S(1)}, u32[]{:S(2)}, u32[]{:S(2)}) %collective-permute-start.33) | collective-permute-done | bytes 16416 | tf_op jit(solution)/shard_map/ppermute | solution.py:44
  63.6 2.1 %collective-permute-done.34.refs_1_ = bf16[32,256]{1,0:T(8,128)(2,1)S(1)} collective-permute-done((bf16[32,256]{1,0:T(8,128)(2,1)S(1)}, bf16[32,256]{1,0:T(8,128)(2,1)S(1)}, u32[]{:S(2)}, u32[]{:S(2)}) %collective-permute-start.34) | collective-permute-done | bytes 16416 | tf_op jit(solution)/shard_map/ppermute | solution.py:44
  (90 shorter events, 13.9 us)
Async XLA Ops:
  0.6 11.9 %collective-permute-start = (bf16[1,64,512]{2,1,0:T(8,128)(2,1)}, bf16[1,64,512]{2,1,0:T(8,128)(2,1)S(1)}, u32[]{:S(2)}, u32[]{:S(2)}) collective-permute-start(bf16[1,64,512]{2,1,0:T(8,128)(2,1)} %bitcast.30), channel_id=1, source_target_pairs={{0,28},{1,29},{2,30},{3,31},{4,24},{5,25},{6,26},{7,27},{8,20},{9,... | collective-permute-start | bytes 196616 | tf_op jit(solution)/shard_map/ppermute | solution.py:44
  5.2 7.3 %collective-permute-start.1 = (bf16[1,64,512]{2,1,0:T(8,128)(2,1)}, bf16[1,64,512]{2,1,0:T(8,128)(2,1)S(1)}, u32[]{:S(2)}, u32[]{:S(2)}) collective-permute-start(bf16[1,64,512]{2,1,0:T(8,128)(2,1)} %bitcast.31), channel_id=1, source_target_pairs={{0,24},{1,25},{2,26},{3,27},{4,28},{5,29},{6,30},{7,31},{8,16},{9,... | collective-permute-start | bytes 196616 | tf_op jit(solution)/shard_map/ppermute | solution.py:44
  5.2 7.3 %collective-permute-start.2 = (bf16[1,64,512]{2,1,0:T(8,128)(2,1)}, bf16[1,64,512]{2,1,0:T(8,128)(2,1)S(1)}, u32[]{:S(2)}, u32[]{:S(2)}) collective-permute-start(bf16[1,64,512]{2,1,0:T(8,128)(2,1)} %bitcast.32), channel_id=1, source_target_pairs={{0,20},{1,21},{2,22},{3,23},{4,16},{5,17},{6,18},{7,19},{8,28},{9,... | collective-permute-start | bytes 196616 | tf_op jit(solution)/shard_map/ppermute | solution.py:44
  10.9 7.6 %collective-permute-start.7 = (bf16[4,64,512]{2,1,0:T(8,128)(2,1)S(1)}, bf16[4,64,512]{2,1,0:T(8,128)(2,1)S(1)}, u32[]{:S(2)}, u32[]{:S(2)}) collective-permute-start(bf16[4,64,512]{2,1,0:T(8,128)(2,1)S(1)} %get-tuple-element.43), channel_id=1, source_target_pairs={{0,18},{1,19},{2,16},{3,17},{4,22},{5,23},{6,20},{7,21},{8,26},{9,... | collective-permute-start | bytes 786440 | tf_op jit(solution)/shard_map/ppermute | solution.py:44
  12.5 7.8 %collective-permute-start.8 = (bf16[4,64,512]{2,1,0:T(8,128)(2,1)S(1)}, bf16[4,64,512]{2,1,0:T(8,128)(2,1)S(1)}, u32[]{:S(2)}, u32[]{:S(2)}) collective-permute-start(bf16[4,64,512]{2,1,0:T(8,128)(2,1)S(1)} %get-tuple-element.44), channel_id=1, source_target_pairs={{0,17},{1,16},{2,19},{3,18},{4,21},{5,20},{6,23},{7,22},{8,25},{9,... | collective-permute-start | bytes 786440 | tf_op jit(solution)/shard_map/ppermute | solution.py:44
  12.6 7.7 %collective-permute-start.9 = (bf16[4,64,512]{2,1,0:T(8,128)(2,1)S(1)}, bf16[4,64,512]{2,1,0:T(8,128)(2,1)S(1)}, u32[]{:S(2)}, u32[]{:S(2)}) collective-permute-start(bf16[4,64,512]{2,1,0:T(8,128)(2,1)S(1)} %get-tuple-element.45), channel_id=1, source_target_pairs={{0,16},{1,17},{2,18},{3,19},{4,20},{5,21},{6,22},{7,23},{8,24},{9,... | collective-permute-start | bytes 786440 | tf_op jit(solution)/shard_map/ppermute | solution.py:44
  14.8 9.0 %collective-permute-start.6 = (bf16[4,64,512]{2,1,0:T(8,128)(2,1)S(1)}, bf16[4,64,512]{2,1,0:T(8,128)(2,1)S(1)}, u32[]{:S(2)}, u32[]{:S(2)}) collective-permute-start(bf16[4,64,512]{2,1,0:T(8,128)(2,1)S(1)} %pad_maximum_fusion.rest_0_), channel_id=1, source_target_pairs={{16,1},{17,0},{18,3},{19,2},{20,5},{21,4},{22,7},{23,6},{24,9},{25... | collective-permute-start | bytes 786440 | tf_op jit(solution)/shard_map/ppermute | solution.py:44
  17.6 7.1 %collective-permute-start.4 = (bf16[4,64,512]{2,1,0:T(8,128)(2,1)S(1)}, bf16[4,64,512]{2,1,0:T(8,128)(2,1)S(1)}, u32[]{:S(2)}, u32[]{:S(2)}) collective-permute-start(bf16[4,64,512]{2,1,0:T(8,128)(2,1)S(1)} %pad_maximum_fusion.rest_0_), channel_id=1, source_target_pairs={{16,2},{17,3},{18,0},{19,1},{20,6},{21,7},{22,4},{23,5},{24,10},{2... | collective-permute-start | bytes 786440 | tf_op jit(solution)/shard_map/ppermute | solution.py:44
  18.5 7.7 %collective-permute-start.5 = (bf16[4,64,512]{2,1,0:T(8,128)(2,1)S(1)}, bf16[4,64,512]{2,1,0:T(8,128)(2,1)S(1)}, u32[]{:S(2)}, u32[]{:S(2)}) collective-permute-start(bf16[4,64,512]{2,1,0:T(8,128)(2,1)S(1)} %pad_maximum_fusion.rest_0_), channel_id=1, source_target_pairs={{16,3},{17,2},{18,1},{19,0},{20,7},{21,6},{22,5},{23,4},{24,11},{2... | collective-permute-start | bytes 786440 | tf_op jit(solution)/shard_map/ppermute | solution.py:44
  20.5 6.9 %collective-permute-start.10 = (bf16[1,64,512]{2,1,0:T(8,128)(2,1)S(1)}, bf16[1,64,512]{2,1,0:T(8,128)(2,1)S(1)}, u32[]{:S(2)}, u32[]{:S(2)}) collective-permute-start(bf16[1,64,512]{2,1,0:T(8,128)(2,1)S(1)} %get-tuple-element.66), channel_id=1, source_target_pairs={{16,12},{17,13},{18,14},{19,15},{20,8},{21,9},{22,10},{23,11},{24,... | collective-permute-start | bytes 196616 | tf_op jit(solution)/shard_map/ppermute | solution.py:44
  20.5 6.8 %collective-permute-start.11 = (bf16[1,64,512]{2,1,0:T(8,128)(2,1)S(1)}, bf16[1,64,512]{2,1,0:T(8,128)(2,1)S(1)}, u32[]{:S(2)}, u32[]{:S(2)}) collective-permute-start(bf16[1,64,512]{2,1,0:T(8,128)(2,1)S(1)} %get-tuple-element.69), channel_id=1, source_target_pairs={{16,8},{17,9},{18,10},{19,11},{20,12},{21,13},{22,14},{23,15},{24,... | collective-permute-start | bytes 196616 | tf_op jit(solution)/shard_map/ppermute | solution.py:44
  29.3 6.2 %collective-permute-start.15 = (bf16[1,64,512]{2,1,0:T(8,128)(2,1)S(1)}, bf16[1,64,512]{2,1,0:T(8,128)(2,1)S(1)}, u32[]{:S(2)}, u32[]{:S(2)}) collective-permute-start(bf16[1,64,512]{2,1,0:T(8,128)(2,1)S(1)} %bitcast.26), channel_id=1, source_target_pairs={{16,12},{17,13},{18,14},{19,15},{20,8},{21,9},{22,10},{23,11},{24,... | collective-permute-start | bytes 196616 | tf_op jit(solution)/shard_map/ppermute | solution.py:44
  31.8 6.5 %collective-permute-start.16 = (bf16[1,64,512]{2,1,0:T(8,128)(2,1)S(1)}, bf16[1,64,512]{2,1,0:T(8,128)(2,1)S(1)}, u32[]{:S(2)}, u32[]{:S(2)}) collective-permute-start(bf16[1,64,512]{2,1,0:T(8,128)(2,1)S(1)} %bitcast.27), channel_id=1, source_target_pairs={{16,8},{17,9},{18,10},{19,11},{20,12},{21,13},{22,14},{23,15},{24,... | collective-permute-start | bytes 196616 | tf_op jit(solution)/shard_map/ppermute | solution.py:44
  31.8 6.5 %collective-permute-start.17 = (bf16[1,64,512]{2,1,0:T(8,128)(2,1)S(1)}, bf16[1,64,512]{2,1,0:T(8,128)(2,1)S(1)}, u32[]{:S(2)}, u32[]{:S(2)}) collective-permute-start(bf16[1,64,512]{2,1,0:T(8,128)(2,1)S(1)} %bitcast.28), channel_id=1, source_target_pairs={{16,4},{17,5},{18,6},{19,7},{20,0},{21,1},{22,2},{23,3},{24,12},{2... | collective-permute-start | bytes 196616 | tf_op jit(solution)/shard_map/ppermute | solution.py:44
  33.2 7.2 %collective-permute-start.21 = (bf16[4,64,512]{2,1,0:T(8,128)(2,1)S(1)}, bf16[4,64,512]{2,1,0:T(8,128)(2,1)S(1)}, u32[]{:S(2)}, u32[]{:S(2)}) collective-permute-start(bf16[4,64,512]{2,1,0:T(8,128)(2,1)S(1)} %get-tuple-element.55), channel_id=1, source_target_pairs={{16,3},{17,2},{18,1},{19,0},{20,7},{21,6},{22,5},{23,4},{24,11},{2... | collective-permute-start | bytes 786440 | tf_op jit(solution)/shard_map/ppermute | solution.py:44
  35.4 7.9 %collective-permute-start.22 = (bf16[4,64,512]{2,1,0:T(8,128)(2,1)S(1)}, bf16[4,64,512]{2,1,0:T(8,128)(2,1)S(1)}, u32[]{:S(2)}, u32[]{:S(2)}) collective-permute-start(bf16[4,64,512]{2,1,0:T(8,128)(2,1)S(1)} %get-tuple-element.56), channel_id=1, source_target_pairs={{16,2},{17,3},{18,0},{19,1},{20,6},{21,7},{22,4},{23,5},{24,10},{2... | collective-permute-start | bytes 786440 | tf_op jit(solution)/shard_map/ppermute | solution.py:44
  35.4 7.9 %collective-permute-start.23 = (bf16[4,64,512]{2,1,0:T(8,128)(2,1)S(1)}, bf16[4,64,512]{2,1,0:T(8,128)(2,1)S(1)}, u32[]{:S(2)}, u32[]{:S(2)}) collective-permute-start(bf16[4,64,512]{2,1,0:T(8,128)(2,1)S(1)} %get-tuple-element.57), channel_id=1, source_target_pairs={{16,1},{17,0},{18,3},{19,2},{20,5},{21,4},{22,7},{23,6},{24,9},{25... | collective-permute-start | bytes 786440 | tf_op jit(solution)/shard_map/ppermute | solution.py:44
  38.3 5.0 %collective-permute-start.24 = (bf16[4,64,512]{2,1,0:T(8,128)(2,1)S(1)}, bf16[4,64,512]{2,1,0:T(8,128)(2,1)S(1)}, u32[]{:S(2)}, u32[]{:S(2)}) collective-permute-start(bf16[4,64,512]{2,1,0:T(8,128)(2,1)S(1)} %get-tuple-element.58), channel_id=1, source_target_pairs={{16,0},{17,1},{18,2},{19,3},{20,4},{21,5},{22,6},{23,7},{24,8},{25... | collective-permute-start | bytes 786440 | tf_op jit(solution)/shard_map/ppermute | solution.py:44
  38.5 7.4 %collective-permute-start.20 = (bf16[4,64,512]{2,1,0:T(8,128)(2,1)S(1)}, bf16[4,64,512]{2,1,0:T(8,128)(2,1)S(1)}, u32[]{:S(2)}, u32[]{:S(2)}) collective-permute-start(bf16[4,64,512]{2,1,0:T(8,128)(2,1)S(1)} %constant_dynamic-update-slice_fusion.rest_0_), channel_id=1, source_target_pairs={{0,17},{1,16},{2,19},{3,18},{4,21},{5,20},{6,23},{7,22},{8,25},{9,... | collective-permute-start | bytes 786440 | tf_op jit(solution)/shard_map/ppermute | solution.py:44
  40.4 5.5 %collective-permute-start.18 = (bf16[4,64,512]{2,1,0:T(8,128)(2,1)S(1)}, bf16[4,64,512]{2,1,0:T(8,128)(2,1)S(1)}, u32[]{:S(2)}, u32[]{:S(2)}) collective-permute-start(bf16[4,64,512]{2,1,0:T(8,128)(2,1)S(1)} %constant_dynamic-update-slice_fusion.rest_0_), channel_id=1, source_target_pairs={{0,18},{1,19},{2,16},{3,17},{4,22},{5,23},{6,20},{7,21},{8,26},{9,... | collective-permute-start | bytes 786440 | tf_op jit(solution)/shard_map/ppermute | solution.py:44
  51.4 4.6 %collective-permute-start.30 = (bf16[32,256]{1,0:T(8,128)(2,1)S(1)}, bf16[32,256]{1,0:T(8,128)(2,1)S(1)}, u32[]{:S(2)}, u32[]{:S(2)}) collective-permute-start(bf16[32,256]{1,0:T(8,128)(2,1)S(1)} %add_convert_fusion.3), channel_id=1, source_target_pairs={{0,3},{1,2},{2,1},{3,0},{4,7},{5,6},{6,5},{7,4},{8,11},{9,10},{10,... | collective-permute-start | bytes 49160 | tf_op jit(solution)/shard_map/ppermute | solution.py:44
  58.0 5.6 %collective-permute-start.33 = (bf16[32,256]{1,0:T(8,128)(2,1)S(1)}, bf16[32,256]{1,0:T(8,128)(2,1)S(1)}, u32[]{:S(2)}, u32[]{:S(2)}) collective-permute-start(bf16[32,256]{1,0:T(8,128)(2,1)S(1)} %add_convert_fusion.2.refs_3_), channel_id=1, source_target_pairs={{0,12},{1,13},{2,14},{3,15},{4,8},{5,9},{6,10},{7,11},{8,4},{9,5},... | collective-permute-start | bytes 49160 | tf_op jit(solution)/shard_map/ppermute | solution.py:44
  61.1 4.6 %collective-permute-start.34 = (bf16[32,256]{1,0:T(8,128)(2,1)S(1)}, bf16[32,256]{1,0:T(8,128)(2,1)S(1)}, u32[]{:S(2)}, u32[]{:S(2)}) collective-permute-start(bf16[32,256]{1,0:T(8,128)(2,1)S(1)} %add_convert_fusion.2.refs_3_), channel_id=1, source_target_pairs={{0,8},{1,9},{2,10},{3,11},{4,12},{5,13},{6,14},{7,15},{8,0},{9,1},... | collective-permute-start | bytes 49160 | tf_op jit(solution)/shard_map/ppermute | solution.py:44
  61.1 4.6 %collective-permute-start.35 = (bf16[32,256]{1,0:T(8,128)(2,1)S(1)}, bf16[32,256]{1,0:T(8,128)(2,1)S(1)}, u32[]{:S(2)}, u32[]{:S(2)}) collective-permute-start(bf16[32,256]{1,0:T(8,128)(2,1)S(1)} %add_convert_fusion.2.refs_3_), channel_id=1, source_target_pairs={{0,4},{1,5},{2,6},{3,7},{4,0},{5,1},{6,2},{7,3},{8,12},{9,13},{10,... | collective-permute-start | bytes 49160 | tf_op jit(solution)/shard_map/ppermute | solution.py:44
  (19 other events, 134.0 us)

commit v5 on v4

--- a/solution.py
+++ b/solution.py
@@ -278,7 +278,7 @@
                         one = send(one, routes=routes, radix=radix, stride=stride, step=step)
                     sent.append(one)
                 if layer == 0 and rounds > 1:
-                    stack, sent[:1] = lax.optimization_barrier((stack, sent[:1]))
+                    stack, sent[-1:] = lax.optimization_barrier((stack, sent[-1:]))
             routes = [(helper, layer)] if final else both
             gathered = [
                 stack if step == 0 else send(stack, routes=routes, radix=radix, stride=stride, step=step)

time: 66.6 us -> 70.3 us (1.056)
  waiting for transfers between devices: 20 us -> 26 us
  starting transfers between devices: 37.1 us -> 34.8 us
    ppermute x36, waiting for transfers between devices: 20 us -> 26 us  [exchange(): return lax.ppermute(value, axes, pairs)]
    ppermute x36, starting transfers between devices: 37.1 us -> 34.8 us  [exchange(): return lax.ppermute(value, axes, pairs)]
  transfers between devices with their start and end apart: 36 -> 36, of which waited for: 18 -> 20; matrix products, arithmetic and copies ran while one was open for 1% -> 1% of each run, Pallas kernels for 10% -> 9%
where the time goes in v5:
time: 70.3 us; the launch traced here: 70.1 us
  starting transfers between devices  34.8 us (50%)
  waiting for transfers between devices  26 us (37%)
  Pallas kernels  7.37 us (10%)
  other arithmetic  0.98 us (1%)
  between operations  0.9 us (1%)
    ppermute x36, starting transfers between devices, exchange(): return lax.ppermute(value, axes, pairs)  34.8 us
    ppermute x36, waiting for transfers between devices, exchange(): return lax.ppermute(value, axes, pairs)  26 us
    pallas_call x1, Pallas kernels, spread(): pl.pallas_call(functools.partial(first_spread_kernel, outputs=groups, lay...  4.68 us
    pallas_call x4, Pallas kernels, meet(): pl.pallas_call(functools.partial(meet_kernel, first=first, blocks=len(gro...  1.8 us
  transfers between devices with their start and end apart: 36, of which 20 were waited for; matrix products, arithmetic and copies ran while one was open for 1% of the time, Pallas kernels for 9%

profile of v5, /device:TPU:0, one launch (start us, length us, event | category | flops | bytes accessed | tf_op | source)
XLA Modules:
  0.0 70.1 jit_solution(6300481199704880928)
XLA Ops:
  0.6 4.6 %collective-permute-start = (bf16[1,64,512]{2,1,0:T(8,128)(2,1)}, bf16[1,64,512]{2,1,0:T(8,128)(2,1)S(1)}, u32[]{:S(2)}, u32[]{:S(2)}) collective-permute-start(bf16[1,64,512]{2,1,0:T(8,128)(2,1)} %bitcast.30), channel_id=1, source_target_pairs={{0,28},{1,29},{2,30},{3,31},{4,24},{5,25},{6,26},{7,27},{8,20},{9,... | collective-permute-start | bytes 196616 | tf_op jit(solution)/shard_map/ppermute | solution.py:44
  6.1 4.7 %first_spread.1 = (bf16[4,64,512]{2,1,0:T(8,128)(2,1)S(1)}, bf16[4,64,512]{2,1,0:T(8,128)(2,1)S(1)}, bf16[4,64,512]{2,1,0:T(8,128)(2,1)S(1)}, bf16[4,64,512]{2,1,0:T(8,128)(2,1)S(1)}) custom-call(bf16[64,512]{1,0:T(8,128)(2,1)} %bitcast.33, bf16[1,512,8192]{2,1,0:T(8,128)(2,1)} %weight.13), custom_call_target="tpu_custom_call" | custom-call | tf_op jit(solution)/shard_map/first_spread/pallas_call | solution.py:132
  12.0 2.4 %collective-permute-start.7 = (bf16[4,64,512]{2,1,0:T(8,128)(2,1)S(1)}, bf16[4,64,512]{2,1,0:T(8,128)(2,1)S(1)}, u32[]{:S(2)}, u32[]{:S(2)}) collective-permute-start(bf16[4,64,512]{2,1,0:T(8,128)(2,1)S(1)} %get-tuple-element.42), channel_id=1, source_target_pairs={{0,19},{1,18},{2,17},{3,16},{4,23},{5,22},{6,21},{7,20},{8,27},{9,... | collective-permute-start | bytes 786440 | tf_op jit(solution)/shard_map/ppermute | solution.py:44
  15.2 1.6 %collective-permute-start.4 = (bf16[4,64,512]{2,1,0:T(8,128)(2,1)S(1)}, bf16[4,64,512]{2,1,0:T(8,128)(2,1)S(1)}, u32[]{:S(2)}, u32[]{:S(2)}) collective-permute-start(bf16[4,64,512]{2,1,0:T(8,128)(2,1)S(1)} %pad_maximum_fusion.rest_0_), channel_id=1, source_target_pairs={{16,2},{17,3},{18,0},{19,1},{20,6},{21,7},{22,4},{23,5},{24,10},{2... | collective-permute-start | bytes 786440 | tf_op jit(solution)/shard_map/ppermute | solution.py:44
  16.8 2.7 %collective-permute-done.7 = bf16[4,64,512]{2,1,0:T(8,128)(2,1)S(1)} collective-permute-done((bf16[4,64,512]{2,1,0:T(8,128)(2,1)S(1)}, bf16[4,64,512]{2,1,0:T(8,128)(2,1)S(1)}, u32[]{:S(2)}, u32[]{:S(2)}) %collective-permute-start.7) | collective-permute-done | bytes 262176 | tf_op jit(solution)/shard_map/ppermute | solution.py:44
  20.2 4.1 %collective-permute-done.8 = bf16[4,64,512]{2,1,0:T(8,128)(2,1)S(1)} collective-permute-done((bf16[4,64,512]{2,1,0:T(8,128)(2,1)S(1)}, bf16[4,64,512]{2,1,0:T(8,128)(2,1)S(1)}, u32[]{:S(2)}, u32[]{:S(2)}) %collective-permute-start.8) | collective-permute-done | bytes 262176 | tf_op jit(solution)/shard_map/ppermute | solution.py:44
  25.3 1.1 %collective-permute-start.10 = (bf16[1,64,512]{2,1,0:T(8,128)(2,1)S(1)}, bf16[1,64,512]{2,1,0:T(8,128)(2,1)S(1)}, u32[]{:S(2)}, u32[]{:S(2)}) collective-permute-start(bf16[1,64,512]{2,1,0:T(8,128)(2,1)S(1)} %get-tuple-element.66), channel_id=1, source_target_pairs={{16,12},{17,13},{18,14},{19,15},{20,8},{21,9},{22,10},{23,11},{24,... | collective-permute-start | bytes 196616 | tf_op jit(solution)/shard_map/ppermute | solution.py:44
  26.4 1.5 %collective-permute-start.11 = (bf16[1,64,512]{2,1,0:T(8,128)(2,1)S(1)}, bf16[1,64,512]{2,1,0:T(8,128)(2,1)S(1)}, u32[]{:S(2)}, u32[]{:S(2)}) collective-permute-start(bf16[1,64,512]{2,1,0:T(8,128)(2,1)S(1)} %get-tuple-element.69), channel_id=1, source_target_pairs={{16,8},{17,9},{18,10},{19,11},{20,12},{21,13},{22,14},{23,15},{24,... | collective-permute-start | bytes 196616 | tf_op jit(solution)/shard_map/ppermute | solution.py:44
  30.9 1.3 %collective-permute-done.11 = bf16[1,64,512]{2,1,0:T(8,128)(2,1)S(1)} collective-permute-done((bf16[1,64,512]{2,1,0:T(8,128)(2,1)S(1)}, bf16[1,64,512]{2,1,0:T(8,128)(2,1)S(1)}, u32[]{:S(2)}, u32[]{:S(2)}) %collective-permute-start.11) | collective-permute-done | bytes 65568 | tf_op jit(solution)/shard_map/ppermute | solution.py:44
  32.4 1.2 %collective-permute-done.14 = bf16[64,512]{1,0:T(8,128)(2,1)S(1)} collective-permute-done((bf16[64,512]{1,0:T(8,128)(2,1)S(1)}, bf16[64,512]{1,0:T(8,128)(2,1)S(1)}, u32[]{:S(2)}, u32[]{:S(2)}) %collective-permute-start.14) | collective-permute-done | bytes 65568 | tf_op jit(solution)/shard_map/ppermute | solution.py:44
  33.6 2.2 %collective-permute-start.15 = (bf16[1,64,512]{2,1,0:T(8,128)(2,1)S(1)}, bf16[1,64,512]{2,1,0:T(8,128)(2,1)S(1)}, u32[]{:S(2)}, u32[]{:S(2)}) collective-permute-start(bf16[1,64,512]{2,1,0:T(8,128)(2,1)S(1)} %bitcast.26), channel_id=1, source_target_pairs={{16,12},{17,13},{18,14},{19,15},{20,8},{21,9},{22,10},{23,11},{24,... | collective-permute-start | bytes 196616 | tf_op jit(solution)/shard_map/ppermute | solution.py:44
  35.9 1.7 %collective-permute-start.17 = (bf16[1,64,512]{2,1,0:T(8,128)(2,1)S(1)}, bf16[1,64,512]{2,1,0:T(8,128)(2,1)S(1)}, u32[]{:S(2)}, u32[]{:S(2)}) collective-permute-start(bf16[1,64,512]{2,1,0:T(8,128)(2,1)S(1)} %bitcast.28), channel_id=1, source_target_pairs={{16,4},{17,5},{18,6},{19,7},{20,0},{21,1},{22,2},{23,3},{24,12},{2... | collective-permute-start | bytes 196616 | tf_op jit(solution)/shard_map/ppermute | solution.py:44
  37.6 2.2 %collective-permute-start.21 = (bf16[4,64,512]{2,1,0:T(8,128)(2,1)S(1)}, bf16[4,64,512]{2,1,0:T(8,128)(2,1)S(1)}, u32[]{:S(2)}, u32[]{:S(2)}) collective-permute-start(bf16[4,64,512]{2,1,0:T(8,128)(2,1)S(1)} %get-tuple-element.55), channel_id=1, source_target_pairs={{16,3},{17,2},{18,1},{19,0},{20,7},{21,6},{22,5},{23,4},{24,11},{2... | collective-permute-start | bytes 786440 | tf_op jit(solution)/shard_map/ppermute | solution.py:44
  40.6 2.0 %collective-permute-done.16 = bf16[1,64,512]{2,1,0:T(8,128)(2,1)S(1)} collective-permute-done((bf16[1,64,512]{2,1,0:T(8,128)(2,1)S(1)}, bf16[1,64,512]{2,1,0:T(8,128)(2,1)S(1)}, u32[]{:S(2)}, u32[]{:S(2)}) %collective-permute-start.16) | collective-permute-done | bytes 65568 | tf_op jit(solution)/shard_map/ppermute | solution.py:44
  44.5 2.7 %collective-permute-done.22 = bf16[4,64,512]{2,1,0:T(8,128)(2,1)S(1)} collective-permute-done((bf16[4,64,512]{2,1,0:T(8,128)(2,1)S(1)}, bf16[4,64,512]{2,1,0:T(8,128)(2,1)S(1)}, u32[]{:S(2)}, u32[]{:S(2)}) %collective-permute-start.22) | collective-permute-done | bytes 262176 | tf_op jit(solution)/shard_map/ppermute | solution.py:44
  48.3 1.6 %collective-permute-start.25 = (bf16[1,64,512]{2,1,0:T(8,128)(2,1)S(1)}, bf16[1,64,512]{2,1,0:T(8,128)(2,1)S(1)}, u32[]{:S(2)}, u32[]{:S(2)}) collective-permute-start(bf16[1,64,512]{2,1,0:T(8,128)(2,1)S(1)} %get-tuple-element.62), channel_id=1, source_target_pairs={{0,28},{1,29},{2,30},{3,31},{4,24},{5,25},{6,26},{7,27},{8,20},{9,... | collective-permute-start | bytes 196616 | tf_op jit(solution)/shard_map/ppermute | solution.py:44
  50.1 1.4 %collective-permute-start.28 = (bf16[1,64,512]{2,1,0:T(8,128)(2,1)S(1)}, bf16[1,64,512]{2,1,0:T(8,128)(2,1)S(1)}, u32[]{:S(2)}, u32[]{:S(2)}) collective-permute-start(bf16[1,64,512]{2,1,0:T(8,128)(2,1)S(1)} %get-tuple-element.63), channel_id=1, source_target_pairs={{16,0},{17,1},{18,2},{19,3},{20,4},{21,5},{22,6},{23,7},{24,8},{25... | collective-permute-start | bytes 196616 | tf_op jit(solution)/shard_map/ppermute | solution.py:44
  53.4 1.8 %collective-permute-start.29 = (f32[32,256]{1,0:T(8,128)S(1)}, f32[32,256]{1,0:T(8,128)S(1)}, u32[]{:S(2)}, u32[]{:S(2)}) collective-permute-start(f32[32,256]{1,0:T(8,128)S(1)} %get-tuple-element.61), channel_id=1, source_target_pairs={{16,0},{17,1},{18,2},{19,3},{20,4},{21,5},{22,6},{23,7},{24,8},{25... | collective-permute-start | bytes 98312 | tf_op jit(solution)/shard_map/ppermute | solution.py:44
  56.1 1.8 %collective-permute-start.30 = (bf16[32,256]{1,0:T(8,128)(2,1)S(1)}, bf16[32,256]{1,0:T(8,128)(2,1)S(1)}, u32[]{:S(2)}, u32[]{:S(2)}) collective-permute-start(bf16[32,256]{1,0:T(8,128)(2,1)S(1)} %add_convert_fusion.3), channel_id=1, source_target_pairs={{0,3},{1,2},{2,1},{3,0},{4,7},{5,6},{6,5},{7,4},{8,11},{9,10},{10,... | collective-permute-start | bytes 49160 | tf_op jit(solution)/shard_map/ppermute | solution.py:44
  59.6 1.2 %collective-permute-done.30 = bf16[32,256]{1,0:T(8,128)(2,1)S(1)} collective-permute-done((bf16[32,256]{1,0:T(8,128)(2,1)S(1)}, bf16[32,256]{1,0:T(8,128)(2,1)S(1)}, u32[]{:S(2)}, u32[]{:S(2)}) %collective-permute-start.30) | collective-permute-done | bytes 16416 | tf_op jit(solution)/shard_map/ppermute | solution.py:44
  62.6 2.2 %collective-permute-start.33 = (bf16[32,256]{1,0:T(8,128)(2,1)S(1)}, bf16[32,256]{1,0:T(8,128)(2,1)S(1)}, u32[]{:S(2)}, u32[]{:S(2)}) collective-permute-start(bf16[32,256]{1,0:T(8,128)(2,1)S(1)} %add_convert_fusion.2.refs_3_), channel_id=1, source_target_pairs={{0,12},{1,13},{2,14},{3,15},{4,8},{5,9},{6,10},{7,11},{8,4},{9,5},... | collective-permute-start | bytes 49160 | tf_op jit(solution)/shard_map/ppermute | solution.py:44
  64.7 2.3 %collective-permute-start.35 = (bf16[32,256]{1,0:T(8,128)(2,1)S(1)}, bf16[32,256]{1,0:T(8,128)(2,1)S(1)}, u32[]{:S(2)}, u32[]{:S(2)}) collective-permute-start(bf16[32,256]{1,0:T(8,128)(2,1)S(1)} %add_convert_fusion.2.refs_3_), channel_id=1, source_target_pairs={{0,4},{1,5},{2,6},{3,7},{4,0},{5,1},{6,2},{7,3},{8,12},{9,13},{10,... | collective-permute-start | bytes 49160 | tf_op jit(solution)/shard_map/ppermute | solution.py:44
  67.0 1.2 %collective-permute-done.33.refs_0_ = bf16[32,256]{1,0:T(8,128)(2,1)S(1)} collective-permute-done((bf16[32,256]{1,0:T(8,128)(2,1)S(1)}, bf16[32,256]{1,0:T(8,128)(2,1)S(1)}, u32[]{:S(2)}, u32[]{:S(2)}) %collective-permute-start.33) | collective-permute-done | bytes 16416 | tf_op jit(solution)/shard_map/ppermute | solution.py:44
  68.2 1.2 %collective-permute-done.34.refs_1_ = bf16[32,256]{1,0:T(8,128)(2,1)S(1)} collective-permute-done((bf16[32,256]{1,0:T(8,128)(2,1)S(1)}, bf16[32,256]{1,0:T(8,128)(2,1)S(1)}, u32[]{:S(2)}, u32[]{:S(2)}) %collective-permute-start.34) | collective-permute-done | bytes 16416 | tf_op jit(solution)/shard_map/ppermute | solution.py:44
  (90 shorter events, 18.6 us)
Async XLA Ops:
  0.6 10.2 %collective-permute-start = (bf16[1,64,512]{2,1,0:T(8,128)(2,1)}, bf16[1,64,512]{2,1,0:T(8,128)(2,1)S(1)}, u32[]{:S(2)}, u32[]{:S(2)}) collective-permute-start(bf16[1,64,512]{2,1,0:T(8,128)(2,1)} %bitcast.30), channel_id=1, source_target_pairs={{0,28},{1,29},{2,30},{3,31},{4,24},{5,25},{6,26},{7,27},{8,20},{9,... | collective-permute-start | bytes 196616 | tf_op jit(solution)/shard_map/ppermute | solution.py:44
  5.2 6.7 %collective-permute-start.1 = (bf16[1,64,512]{2,1,0:T(8,128)(2,1)}, bf16[1,64,512]{2,1,0:T(8,128)(2,1)S(1)}, u32[]{:S(2)}, u32[]{:S(2)}) collective-permute-start(bf16[1,64,512]{2,1,0:T(8,128)(2,1)} %bitcast.31), channel_id=1, source_target_pairs={{0,24},{1,25},{2,26},{3,27},{4,28},{5,29},{6,30},{7,31},{8,16},{9,... | collective-permute-start | bytes 196616 | tf_op jit(solution)/shard_map/ppermute | solution.py:44
  5.2 6.7 %collective-permute-start.2 = (bf16[1,64,512]{2,1,0:T(8,128)(2,1)}, bf16[1,64,512]{2,1,0:T(8,128)(2,1)S(1)}, u32[]{:S(2)}, u32[]{:S(2)}) collective-permute-start(bf16[1,64,512]{2,1,0:T(8,128)(2,1)} %bitcast.32), channel_id=1, source_target_pairs={{0,20},{1,21},{2,22},{3,23},{4,16},{5,17},{6,18},{7,19},{8,28},{9,... | collective-permute-start | bytes 196616 | tf_op jit(solution)/shard_map/ppermute | solution.py:44
  12.0 7.5 %collective-permute-start.7 = (bf16[4,64,512]{2,1,0:T(8,128)(2,1)S(1)}, bf16[4,64,512]{2,1,0:T(8,128)(2,1)S(1)}, u32[]{:S(2)}, u32[]{:S(2)}) collective-permute-start(bf16[4,64,512]{2,1,0:T(8,128)(2,1)S(1)} %get-tuple-element.42), channel_id=1, source_target_pairs={{0,19},{1,18},{2,17},{3,16},{4,23},{5,22},{6,21},{7,20},{8,27},{9,... | collective-permute-start | bytes 786440 | tf_op jit(solution)/shard_map/ppermute | solution.py:44
  14.4 9.9 %collective-permute-start.8 = (bf16[4,64,512]{2,1,0:T(8,128)(2,1)S(1)}, bf16[4,64,512]{2,1,0:T(8,128)(2,1)S(1)}, u32[]{:S(2)}, u32[]{:S(2)}) collective-permute-start(bf16[4,64,512]{2,1,0:T(8,128)(2,1)S(1)} %get-tuple-element.43), channel_id=1, source_target_pairs={{0,18},{1,19},{2,16},{3,17},{4,22},{5,23},{6,20},{7,21},{8,26},{9,... | collective-permute-start | bytes 786440 | tf_op jit(solution)/shard_map/ppermute | solution.py:44
  14.4 10.7 %collective-permute-start.9 = (bf16[4,64,512]{2,1,0:T(8,128)(2,1)S(1)}, bf16[4,64,512]{2,1,0:T(8,128)(2,1)S(1)}, u32[]{:S(2)}, u32[]{:S(2)}) collective-permute-start(bf16[4,64,512]{2,1,0:T(8,128)(2,1)S(1)} %get-tuple-element.44), channel_id=1, source_target_pairs={{0,17},{1,16},{2,19},{3,18},{4,21},{5,20},{6,23},{7,22},{8,25},{9,... | collective-permute-start | bytes 786440 | tf_op jit(solution)/shard_map/ppermute | solution.py:44
  15.1 12.7 %collective-permute-start.6 = (bf16[4,64,512]{2,1,0:T(8,128)(2,1)S(1)}, bf16[4,64,512]{2,1,0:T(8,128)(2,1)S(1)}, u32[]{:S(2)}, u32[]{:S(2)}) collective-permute-start(bf16[4,64,512]{2,1,0:T(8,128)(2,1)S(1)} %pad_maximum_fusion.rest_0_), channel_id=1, source_target_pairs={{16,1},{17,0},{18,3},{19,2},{20,5},{21,4},{22,7},{23,6},{24,9},{25... | collective-permute-start | bytes 786440 | tf_op jit(solution)/shard_map/ppermute | solution.py:44
  15.2 13.6 %collective-permute-start.4 = (bf16[4,64,512]{2,1,0:T(8,128)(2,1)S(1)}, bf16[4,64,512]{2,1,0:T(8,128)(2,1)S(1)}, u32[]{:S(2)}, u32[]{:S(2)}) collective-permute-start(bf16[4,64,512]{2,1,0:T(8,128)(2,1)S(1)} %pad_maximum_fusion.rest_0_), channel_id=1, source_target_pairs={{16,2},{17,3},{18,0},{19,1},{20,6},{21,7},{22,4},{23,5},{24,10},{2... | collective-permute-start | bytes 786440 | tf_op jit(solution)/shard_map/ppermute | solution.py:44
  19.5 9.4 %collective-permute-start.5 = (bf16[4,64,512]{2,1,0:T(8,128)(2,1)S(1)}, bf16[4,64,512]{2,1,0:T(8,128)(2,1)S(1)}, u32[]{:S(2)}, u32[]{:S(2)}) collective-permute-start(bf16[4,64,512]{2,1,0:T(8,128)(2,1)S(1)} %pad_maximum_fusion.rest_0_), channel_id=1, source_target_pairs={{16,3},{17,2},{18,1},{19,0},{20,7},{21,6},{22,5},{23,4},{24,11},{2... | collective-permute-start | bytes 786440 | tf_op jit(solution)/shard_map/ppermute | solution.py:44
  25.3 5.6 %collective-permute-start.10 = (bf16[1,64,512]{2,1,0:T(8,128)(2,1)S(1)}, bf16[1,64,512]{2,1,0:T(8,128)(2,1)S(1)}, u32[]{:S(2)}, u32[]{:S(2)}) collective-permute-start(bf16[1,64,512]{2,1,0:T(8,128)(2,1)S(1)} %get-tuple-element.66), channel_id=1, source_target_pairs={{16,12},{17,13},{18,14},{19,15},{20,8},{21,9},{22,10},{23,11},{24,... | collective-permute-start | bytes 196616 | tf_op jit(solution)/shard_map/ppermute | solution.py:44
  26.4 5.8 %collective-permute-start.11 = (bf16[1,64,512]{2,1,0:T(8,128)(2,1)S(1)}, bf16[1,64,512]{2,1,0:T(8,128)(2,1)S(1)}, u32[]{:S(2)}, u32[]{:S(2)}) collective-permute-start(bf16[1,64,512]{2,1,0:T(8,128)(2,1)S(1)} %get-tuple-element.69), channel_id=1, source_target_pairs={{16,8},{17,9},{18,10},{19,11},{20,12},{21,13},{22,14},{23,15},{24,... | collective-permute-start | bytes 196616 | tf_op jit(solution)/shard_map/ppermute | solution.py:44
  33.6 6.2 %collective-permute-start.15 = (bf16[1,64,512]{2,1,0:T(8,128)(2,1)S(1)}, bf16[1,64,512]{2,1,0:T(8,128)(2,1)S(1)}, u32[]{:S(2)}, u32[]{:S(2)}) collective-permute-start(bf16[1,64,512]{2,1,0:T(8,128)(2,1)S(1)} %bitcast.26), channel_id=1, source_target_pairs={{16,12},{17,13},{18,14},{19,15},{20,8},{21,9},{22,10},{23,11},{24,... | collective-permute-start | bytes 196616 | tf_op jit(solution)/shard_map/ppermute | solution.py:44
  35.9 6.8 %collective-permute-start.16 = (bf16[1,64,512]{2,1,0:T(8,128)(2,1)S(1)}, bf16[1,64,512]{2,1,0:T(8,128)(2,1)S(1)}, u32[]{:S(2)}, u32[]{:S(2)}) collective-permute-start(bf16[1,64,512]{2,1,0:T(8,128)(2,1)S(1)} %bitcast.27), channel_id=1, source_target_pairs={{16,8},{17,9},{18,10},{19,11},{20,12},{21,13},{22,14},{23,15},{24,... | collective-permute-start | bytes 196616 | tf_op jit(solution)/shard_map/ppermute | solution.py:44
  35.9 6.8 %collective-permute-start.17 = (bf16[1,64,512]{2,1,0:T(8,128)(2,1)S(1)}, bf16[1,64,512]{2,1,0:T(8,128)(2,1)S(1)}, u32[]{:S(2)}, u32[]{:S(2)}) collective-permute-start(bf16[1,64,512]{2,1,0:T(8,128)(2,1)S(1)} %bitcast.28), channel_id=1, source_target_pairs={{16,4},{17,5},{18,6},{19,7},{20,0},{21,1},{22,2},{23,3},{24,12},{2... | collective-permute-start | bytes 196616 | tf_op jit(solution)/shard_map/ppermute | solution.py:44
  37.6 6.9 %collective-permute-start.21 = (bf16[4,64,512]{2,1,0:T(8,128)(2,1)S(1)}, bf16[4,64,512]{2,1,0:T(8,128)(2,1)S(1)}, u32[]{:S(2)}, u32[]{:S(2)}) collective-permute-start(bf16[4,64,512]{2,1,0:T(8,128)(2,1)S(1)} %get-tuple-element.55), channel_id=1, source_target_pairs={{16,3},{17,2},{18,1},{19,0},{20,7},{21,6},{22,5},{23,4},{24,11},{2... | collective-permute-start | bytes 786440 | tf_op jit(solution)/shard_map/ppermute | solution.py:44
  39.8 7.5 %collective-permute-start.22 = (bf16[4,64,512]{2,1,0:T(8,128)(2,1)S(1)}, bf16[4,64,512]{2,1,0:T(8,128)(2,1)S(1)}, u32[]{:S(2)}, u32[]{:S(2)}) collective-permute-start(bf16[4,64,512]{2,1,0:T(8,128)(2,1)S(1)} %get-tuple-element.56), channel_id=1, source_target_pairs={{16,2},{17,3},{18,0},{19,1},{20,6},{21,7},{22,4},{23,5},{24,10},{2... | collective-permute-start | bytes 786440 | tf_op jit(solution)/shard_map/ppermute | solution.py:44
  39.8 8.3 %collective-permute-start.23 = (bf16[4,64,512]{2,1,0:T(8,128)(2,1)S(1)}, bf16[4,64,512]{2,1,0:T(8,128)(2,1)S(1)}, u32[]{:S(2)}, u32[]{:S(2)}) collective-permute-start(bf16[4,64,512]{2,1,0:T(8,128)(2,1)S(1)} %get-tuple-element.57), channel_id=1, source_target_pairs={{16,1},{17,0},{18,3},{19,2},{20,5},{21,4},{22,7},{23,6},{24,9},{25... | collective-permute-start | bytes 786440 | tf_op jit(solution)/shard_map/ppermute | solution.py:44
  42.7 5.5 %collective-permute-start.24 = (bf16[4,64,512]{2,1,0:T(8,128)(2,1)S(1)}, bf16[4,64,512]{2,1,0:T(8,128)(2,1)S(1)}, u32[]{:S(2)}, u32[]{:S(2)}) collective-permute-start(bf16[4,64,512]{2,1,0:T(8,128)(2,1)S(1)} %get-tuple-element.58), channel_id=1, source_target_pairs={{16,0},{17,1},{18,2},{19,3},{20,4},{21,5},{22,6},{23,7},{24,8},{25... | collective-permute-start | bytes 786440 | tf_op jit(solution)/shard_map/ppermute | solution.py:44
  42.9 7.0 %collective-permute-start.20 = (bf16[4,64,512]{2,1,0:T(8,128)(2,1)S(1)}, bf16[4,64,512]{2,1,0:T(8,128)(2,1)S(1)}, u32[]{:S(2)}, u32[]{:S(2)}) collective-permute-start(bf16[4,64,512]{2,1,0:T(8,128)(2,1)S(1)} %constant_dynamic-update-slice_fusion.rest_0_), channel_id=1, source_target_pairs={{0,17},{1,16},{2,19},{3,18},{4,21},{5,20},{6,23},{7,22},{8,25},{9,... | collective-permute-start | bytes 786440 | tf_op jit(solution)/shard_map/ppermute | solution.py:44
  44.5 5.5 %collective-permute-start.18 = (bf16[4,64,512]{2,1,0:T(8,128)(2,1)S(1)}, bf16[4,64,512]{2,1,0:T(8,128)(2,1)S(1)}, u32[]{:S(2)}, u32[]{:S(2)}) collective-permute-start(bf16[4,64,512]{2,1,0:T(8,128)(2,1)S(1)} %constant_dynamic-update-slice_fusion.rest_0_), channel_id=1, source_target_pairs={{0,18},{1,19},{2,16},{3,17},{4,22},{5,23},{6,20},{7,21},{8,26},{9,... | collective-permute-start | bytes 786440 | tf_op jit(solution)/shard_map/ppermute | solution.py:44
  56.1 4.6 %collective-permute-start.30 = (bf16[32,256]{1,0:T(8,128)(2,1)S(1)}, bf16[32,256]{1,0:T(8,128)(2,1)S(1)}, u32[]{:S(2)}, u32[]{:S(2)}) collective-permute-start(bf16[32,256]{1,0:T(8,128)(2,1)S(1)} %add_convert_fusion.3), channel_id=1, source_target_pairs={{0,3},{1,2},{2,1},{3,0},{4,7},{5,6},{6,5},{7,4},{8,11},{9,10},{10,... | collective-permute-start | bytes 49160 | tf_op jit(solution)/shard_map/ppermute | solution.py:44
  62.6 5.6 %collective-permute-start.33 = (bf16[32,256]{1,0:T(8,128)(2,1)S(1)}, bf16[32,256]{1,0:T(8,128)(2,1)S(1)}, u32[]{:S(2)}, u32[]{:S(2)}) collective-permute-start(bf16[32,256]{1,0:T(8,128)(2,1)S(1)} %add_convert_fusion.2.refs_3_), channel_id=1, source_target_pairs={{0,12},{1,13},{2,14},{3,15},{4,8},{5,9},{6,10},{7,11},{8,4},{9,5},... | collective-permute-start | bytes 49160 | tf_op jit(solution)/shard_map/ppermute | solution.py:44
  64.7 4.6 %collective-permute-start.34 = (bf16[32,256]{1,0:T(8,128)(2,1)S(1)}, bf16[32,256]{1,0:T(8,128)(2,1)S(1)}, u32[]{:S(2)}, u32[]{:S(2)}) collective-permute-start(bf16[32,256]{1,0:T(8,128)(2,1)S(1)} %add_convert_fusion.2.refs_3_), channel_id=1, source_target_pairs={{0,8},{1,9},{2,10},{3,11},{4,12},{5,13},{6,14},{7,15},{8,0},{9,1},... | collective-permute-start | bytes 49160 | tf_op jit(solution)/shard_map/ppermute | solution.py:44
  64.7 4.6 %collective-permute-start.35 = (bf16[32,256]{1,0:T(8,128)(2,1)S(1)}, bf16[32,256]{1,0:T(8,128)(2,1)S(1)}, u32[]{:S(2)}, u32[]{:S(2)}) collective-permute-start(bf16[32,256]{1,0:T(8,128)(2,1)S(1)} %add_convert_fusion.2.refs_3_), channel_id=1, source_target_pairs={{0,4},{1,5},{2,6},{3,7},{4,0},{5,1},{6,2},{7,3},{8,12},{9,13},{10,... | collective-permute-start | bytes 49160 | tf_op jit(solution)/shard_map/ppermute | solution.py:44
  (19 other events, 141.4 us)
